TPU v7x, 512 devices: a whole 4x8x8 slice. The times are simulated.
512 devices in a mesh: seq: 512 (over x, z, y, core).
Axes of the slice: x: 4, y: 8, z: 8, core: 2. Of those that a mesh axis runs over, the one named last changes fastest.
Arguments:
- query: bfloat16 [65536, 384], P('seq'), may hold values from -6 to 6
- keys: bfloat16 [65536, 384], P('seq'), may hold values from -6 to 6
- values: bfloat16 [65536, 384], P('seq'), may hold values from -6 to 6
- grad_out: bfloat16 [65536, 384], P('seq'), may hold values from -6 to 6
Outputs:
- attended: bfloat16 [65536, 384], P('seq')
- grad_query: bfloat16 [65536, 384], P('seq')
- grad_keys: bfloat16 [65536, 384], P('seq')
- grad_values: bfloat16 [65536, 384], P('seq')
All inputs are finite; a program needn't handle non-finite values.
Results may differ from a plain program's by a relative error of at most 0.024.
Values may be sent and summed in bfloat16 or wider, within the bound.
No kernel may reach another device: no remote copies, remote signals or barrier semaphores. Data moves between devices by JAX's collectives and lax.ppermute only.
A program may use at most 64 MiB of HBM per device.

v0:
```python
from functools import reduce

import jax
import jax.numpy as jnp
from jax import lax
from jax.sharding import PartitionSpec as P

HD = 64
SEG = 512


NEGATIVE = -1e30
level_limit = 5


def from_partner(block, axis, distance):
    count = lax.axis_size(axis)
    route = []
    for low in range(count):
        high = low | 1 << distance
        if high != low and high < count:
            route += [(low, high), (high, low)]
    return lax.ppermute(block, axis, route)


def column_slots(slots):
    return jnp.repeat(slots, HD)


def select_rows(source, stride, slots):
    row_count = source.shape[-2]
    width = source.shape[-1]
    grouped = source.reshape(source.shape[:-2] + (row_count // stride, stride, width))
    chosen = jnp.arange(stride)[:, None] == column_slots(slots)[None, :]
    picked = jnp.where(chosen, grouped, jnp.zeros((), source.dtype))
    return jnp.sum(picked, axis=-2)


def place_rows(source, stride, slots, fill_value):
    row_count = source.shape[-2]
    width = source.shape[-1]
    chosen = jnp.arange(stride)[:, None] == column_slots(slots)[None, :]
    placed = jnp.where(chosen, source[..., :, None, :], jnp.full((), fill_value, source.dtype))
    return placed.reshape(source.shape[:-2] + (row_count * stride, width))


def select_stats(source, stride, slots):
    head_count, row_count = source.shape
    grouped = source.reshape(head_count, row_count // stride, stride)
    chosen = jnp.arange(stride)[None, :] == slots[:, None]
    return jnp.sum(jnp.where(chosen[:, None, :], grouped, 0.0), axis=2)


def place_stats(source, stride, slots, fill_value):
    head_count, row_count = source.shape
    chosen = jnp.arange(stride)[None, :] == slots[:, None]
    placed = jnp.where(
        chosen[:, None, :], source[:, :, None], jnp.full((), fill_value, jnp.float32)
    )
    return placed.reshape(head_count, row_count * stride)


def spread_heads(stats):
    return jnp.repeat(stats.T, HD, axis=1)


def to_flat(stacked):
    head_count, row_count, tail_dim = stacked.shape
    return stacked.transpose(1, 0, 2).reshape(row_count, head_count * tail_dim)


def lower_side(device, bit_index):
    return device // 2**bit_index % 2 == 0


def join_halves(current, partner, lower):
    first_half = jnp.where(lower, current, partner)
    second_half = jnp.where(lower, partner, current)
    return jnp.concatenate([first_half, second_half], 1)


def split_halves(current, lower):
    half_rows = current.shape[1] // 2
    first_half = current[:, :half_rows]
    second_half = current[:, half_rows:]
    return (jnp.where(lower, first_half, second_half), jnp.where(lower, second_half, first_half))


def double_level(current, group_bits, device):
    for bit_index in range(group_bits):
        partner = from_partner(current, "seq", bit_index)
        current = join_halves(current, partner, lower_side(device, bit_index))
    return current


def halve_level(current, group_bits, device):
    for bit_index in reversed(range(group_bits)):
        retained, outgoing = split_halves(current, lower_side(device, bit_index))
        partner = from_partner(outgoing.astype(jnp.bfloat16), "seq", bit_index).astype(
            outgoing.dtype
        )
        current = retained + partner
    return current


def level_forward(query_rows, key_pair, seg_count):
    head_count = query_rows.shape[1] // HD
    factor = HD ** (-0.5)

    def one_head(head_index):
        column_start = head_index * HD
        query_head = lax.dynamic_slice_in_dim(query_rows, column_start, HD, 1).reshape(
            seg_count, -1, HD
        )
        key_head = lax.dynamic_slice_in_dim(key_pair[0], column_start, HD, 1).reshape(
            seg_count, -1, HD
        )
        value_head = lax.dynamic_slice_in_dim(key_pair[1], column_start, HD, 1).reshape(
            seg_count, -1, HD
        )
        scores = (
            jnp.einsum("sad,sbd->sab", query_head, key_head, preferred_element_type=jnp.float32)
            * factor
        )
        row_max = jnp.max(scores, axis=2)
        weights = jnp.exp(scores - row_max[:, :, None])
        row_sum = jnp.sum(weights, axis=2)
        weighted = jnp.einsum(
            "sab,sbd->sad",
            weights.astype(jnp.bfloat16),
            value_head,
            preferred_element_type=jnp.float32,
        )
        return (row_max.reshape(-1), row_sum.reshape(-1), weighted.reshape(-1, HD))

    row_max, row_sum, weighted = lax.map(one_head, jnp.arange(head_count))
    return (row_max, row_sum, to_flat(weighted))


def level_backward(query_rows, key_pair, grad_rows, log_rows, delta_rows, seg_count):
    head_count = query_rows.shape[1] // HD
    factor = HD ** (-0.5)

    def one_head(head_index):
        column_start = head_index * HD
        query_head = lax.dynamic_slice_in_dim(query_rows, column_start, HD, 1).reshape(
            seg_count, -1, HD
        )
        key_head = lax.dynamic_slice_in_dim(key_pair[0], column_start, HD, 1).reshape(
            seg_count, -1, HD
        )
        value_head = lax.dynamic_slice_in_dim(key_pair[1], column_start, HD, 1).reshape(
            seg_count, -1, HD
        )
        grad_head = lax.dynamic_slice_in_dim(grad_rows, column_start, HD, 1).reshape(
            seg_count, -1, HD
        )
        log_head = lax.dynamic_index_in_dim(log_rows, head_index, 0, False).reshape(seg_count, -1)
        delta_head = lax.dynamic_index_in_dim(delta_rows, head_index, 0, False).reshape(
            seg_count, -1
        )
        scores = (
            jnp.einsum("sad,sbd->sab", query_head, key_head, preferred_element_type=jnp.float32)
            * factor
        )
        weights = jnp.exp(scores - log_head[:, :, None])
        grad_weights = jnp.einsum(
            "sad,sbd->sab", grad_head, value_head, preferred_element_type=jnp.float32
        )
        grad_scores = (weights * (grad_weights - delta_head[:, :, None])).astype(jnp.bfloat16)
        grad_query = (
            jnp.einsum("sab,sbd->sad", grad_scores, key_head, preferred_element_type=jnp.float32)
            * factor
        )
        grad_keys = (
            jnp.einsum("sab,sad->sbd", grad_scores, query_head, preferred_element_type=jnp.float32)
            * factor
        )
        grad_values = jnp.einsum(
            "sab,sad->sbd",
            weights.astype(jnp.bfloat16),
            grad_head,
            preferred_element_type=jnp.float32,
        )
        return (grad_query.reshape(-1, HD), grad_keys.reshape(-1, HD), grad_values.reshape(-1, HD))

    grad_query, grad_keys, grad_values = lax.map(one_head, jnp.arange(head_count))
    return (to_flat(grad_query), jnp.stack([to_flat(grad_keys), to_flat(grad_values)], 0))


def per_device(query, keys, values, grad_out):
    local_rows, feature_width = query.shape
    head_count = feature_width // HD
    device = lax.axis_index("seq")
    slide_rows = local_rows * lax.axis_size("seq")
    level_count = min(level_limit, (slide_rows // SEG).bit_length())
    pair_split = jnp.stack([keys, values], 0)
    strides = [2**level_index for level_index in range(level_count)]
    group_bits = [max(1, SEG * stride // local_rows).bit_length() - 1 for stride in strides]
    segments = [max(1, local_rows // (SEG * stride)) for stride in strides]
    offsets = [jnp.arange(head_count) % stride for stride in strides]
    remote_levels = [
        level_index for level_index in range(level_count) if group_bits[level_index] > 0
    ]
    first_remote = remote_levels[0]
    key_pairs = {}
    for level_index in remote_levels:
        start_rows = select_rows(pair_split, strides[level_index], offsets[level_index])
        key_pairs[level_index] = double_level(start_rows, group_bits[level_index], device)
    maxima, sums, accums = ([], [], [])
    for level_index in range(level_count):
        stride = strides[level_index]
        query_rows = select_rows(query, stride, offsets[level_index])
        row_max, row_sum, weighted = level_forward(
            query_rows, key_pairs[level_index], segments[level_index]
        )
        maxima.append(place_stats(row_max, stride, offsets[level_index], NEGATIVE))
        sums.append(place_stats(row_sum, stride, offsets[level_index], 0.0))
        accums.append(place_rows(weighted, stride, offsets[level_index], 0.0))
    overall = reduce(jnp.maximum, maxima)
    denominator = jnp.zeros((head_count, local_rows), jnp.float32)
    numerator = jnp.zeros((local_rows, feature_width), jnp.float32)
    for level_max, level_sum, level_acc in zip(maxima, sums, accums):
        factor_level = jnp.exp(level_max - overall)
        denominator = denominator + factor_level * level_sum
        numerator = numerator + spread_heads(factor_level) * level_acc
    attended = (numerator / spread_heads(denominator)).astype(jnp.bfloat16)
    log_total = overall + jnp.log(denominator)
    products = grad_out.astype(jnp.float32) * attended.astype(jnp.float32)
    row_delta = jnp.sum(products.reshape(local_rows, head_count, HD), axis=2).T
    grad_query = jnp.zeros((local_rows, feature_width), jnp.float32)
    grad_pairs = {}
    for level_index in range(level_count):
        stride = strides[level_index]
        query_rows = select_rows(query, stride, offsets[level_index])
        grad_rows = select_rows(grad_out, stride, offsets[level_index])
        log_rows = select_stats(log_total, stride, offsets[level_index])
        delta_rows = select_stats(row_delta, stride, offsets[level_index])
        level_query, level_pair = level_backward(
            query_rows,
            key_pairs[level_index],
            grad_rows,
            log_rows,
            delta_rows,
            segments[level_index],
        )
        grad_query = grad_query + place_rows(level_query, stride, offsets[level_index], 0.0)
        grad_pairs[level_index] = level_pair
    grad_pair = jnp.zeros((2, local_rows, feature_width), jnp.float32)
    for level_index in remote_levels:
        own_rows = halve_level(grad_pairs[level_index], group_bits[level_index], device)
        grad_pair = grad_pair + place_rows(
            own_rows, strides[level_index], offsets[level_index], 0.0
        )
    return (
        attended,
        grad_query.astype(jnp.bfloat16),
        grad_pair[0].astype(jnp.bfloat16),
        grad_pair[1].astype(jnp.bfloat16),
    )


def solution(mesh):
    return jax.shard_map(
        per_device,
        mesh=mesh,
        in_specs=(P("seq", None), P("seq", None), P("seq", None), P("seq", None)),
        out_specs=(P("seq", None), P("seq", None), P("seq", None), P("seq", None)),
        check_vma=False,
    )
```

profile of v0, /device:TPU:1, one launch (start us, length us, event | category | flops | bytes accessed | tf_op | source)
XLA Modules:
  0.0 599.8 jit_solution(3386952435505574774)
XLA Ops:
  3.4 8.8 %collective-permute-start.2 = (bf16[2,64,384]{2,1,0:T(8,128)(2,1)S(1)}, bf16[2,64,384]{2,1,0:T(8,128)(2,1)S(1)}, u32[]{:S(2)}, u32[]{:S(2)}) collective-permute-start(bf16[2,64,384]{2,1,0:T(8,128)(2,1)S(1)} %fusion.194), channel_id=1, source_target_pairs={{0,1},{1,0},{2,3},{3,2},{4,5},{5,4},{6,7},{7,6},{8,9},{9,8},{10,11... | collective-permute-start | bytes 294920 | tf_op jit(solution)/shard_map/ppermute | solution.py:23
  13.4 2.1 collective-permute-start
  16.0 2.4 collective-permute-start.5
  20.9 2.4 collective-permute-start.14
  37.0 3.4 collective-permute-start.10
  44.4 4.3 collective-permute-start.11
  48.7 2.5 collective-permute-start.17
  51.2 3.0 collective-permute-start.3
  54.3 2.4 collective-permute-start.7
  56.8 6.6 %collective-permute-start.12 = (bf16[2,128,384]{2,1,0:T(8,128)(2,1)S(1)}, bf16[2,128,384]{2,1,0:T(8,128)(2,1)S(1)}, u32[]{:S(2)}, u32[]{:S(2)}) collective-permute-start(bf16[2,128,384]{2,1,0:T(8,128)(2,1)S(1)} %pad_maximum_fusion.18), channel_id=1, source_target_pairs={{0,8},{8,0},{1,9},{9,1},{2,10},{10,2},{3,11},{11,3},{4,12},{12,4},... | collective-permute-start | bytes 589832 | tf_op jit(solution)/shard_map/ppermute | solution.py:23
  65.6 2.2 collective-permute-start.1
  68.7 4.0 collective-permute-start.4
  72.7 4.8 collective-permute-done.7
  78.4 3.7 collective-permute-start.8
  85.8 3.1 collective-permute-start.19
  89.5 21.6 %while.140 = (s32[]{:T(128)}, f32[6,128]{1,0:T(8,128)S(1)}, f32[6,128]{1,0:T(8,128)}, f32[6,128,64]{1,2,0:T(8,128)S(1)}, s32[6]{0:T(128)S(1)}, /*index=5*/bf16[1...) while((s32[]{:T(128)}, f32[6,128]{1,0:T(8,128)S(1)}, ...), condition=%wide.region_3.4_spmd, body=%wide.region_0.3_spmd.sunk | while | flops 17170180 | bytes 2692279 | solution.py:136
  121.8 13.4 %while.141 = (s32[]{:T(128)}, f32[6,64]{1,0:T(8,128)S(1)}, f32[6,64]{1,0:T(8,128)S(1)}, f32[6,64,64]{2,1,0:T(8,128)S(1)}, s32[6]{0:T(128)S(1)}, /*index=5*/bf16[...) while((s32[]{:T(128)}, f32[6,64]{1,0:T(8,128)S(1)}, ...), condition=%wide.region_9.10_spmd, body=%wide.region_6.9_spmd.sunk | while | flops 8585094 | bytes 2280887 | solution.py:136
  144.9 12.3 %while.142 = (s32[]{:T(128)}, f32[6,32]{1,0:T(8,128)S(1)}, f32[6,32]{1,0:T(8,128)S(1)}, f32[6,32,64]{2,1,0:T(8,128)S(1)}, s32[6]{0:T(128)S(1)}, /*index=5*/bf16[...) while((s32[]{:T(128)}, f32[6,32]{1,0:T(8,128)S(1)}, ...), condition=%wide.region_15.16_spmd, body=%wide.region_12.15_spmd.sunk | while | flops 4292550 | bytes 2058807 | solution.py:136
  166.5 13.1 %while.143 = (s32[]{:T(128)}, f32[6,16]{1,0:T(8,128)S(1)}, f32[6,16]{1,0:T(8,128)S(1)}, f32[6,16,64]{2,1,0:T(8,128)S(1)}, s32[6]{0:T(128)S(1)}, /*index=5*/bf16[...) while((s32[]{:T(128)}, f32[6,16]{1,0:T(8,128)S(1)}, ...), condition=%wide.region_21.22_spmd, body=%wide.region_18.21_spmd.sunk | while | flops 2146278 | bytes 1947767 | solution.py:136
  188.9 43.4 %while.144 = (s32[]{:T(128)}, f32[6,8]{1,0:T(8,128)}, f32[6,8]{1,0:T(8,128)}, f32[6,8,64]{2,1,0:T(8,128)}, s32[6]{0:T(128)}, /*index=5*/bf16[8,384]{1,0:T(8,128)...) while((s32[]{:T(128)}, f32[6,8]{1,0:T(8,128)}, ...), condition=%wide.region_27.28_spmd, body=%wide.region_24.27_spmd.sunk | while | flops 1073142 | bytes 1892755 | solution.py:136
  245.4 2.2 convert_multiply_fusion
  257.3 54.2 %while.145 = (s32[]{:T(128)}, f32[6,128,64]{1,2,0:T(8,128)}, f32[6,512,64]{1,2,0:T(8,128)}, f32[6,512,64]{1,2,0:T(8,128)}, s32[6]{0:T(128)}, /*index=5*/bf16[128...) while((s32[]{:T(128)}, f32[6,128,64]{1,2,0:T(8,128)}, ...), condition=%wide.region_30.31_spmd, body=%wide.region_29.30_spmd.sunk | while | flops 42377224 | bytes 3578617 | solution.py:187
  311.6 2.2 select_convert_fusion.4
  319.1 39.2 %while.146 = (s32[]{:T(128)}, f32[6,64,64]{2,1,0:T(8,128)}, f32[6,512,64]{1,2,0:T(8,128)}, f32[6,512,64]{1,2,0:T(8,128)}, s32[6]{0:T(128)S(1)}, /*index=5*/bf16[...) while((s32[]{:T(128)}, f32[6,64,64]{2,1,0:T(8,128)}, ...), condition=%wide.region_35.36_spmd, body=%wide.region_34.35_spmd.sunk | while | flops 21205000 | bytes 2922233 | solution.py:187
  359.8 2.3 copy.491
  362.1 2.0 select_convert_fusion.3
  364.1 5.2 collective-permute-start.22
  372.0 35.3 %while.147 = (s32[]{:T(128)}, f32[6,32,64]{2,1,0:T(8,128)S(1)}, f32[6,512,64]{1,2,0:T(8,128)}, f32[6,512,64]{1,2,0:T(8,128)}, s32[6]{0:T(128)S(1)}, /*index=5*/b...) while((s32[]{:T(128)}, f32[6,32,64]{2,1,0:T(8,128)S(1)}, ...), condition=%wide.region_40.41_spmd, body=%wide.region_39.40_spmd.sunk | while | flops 10618889 | bytes 2577149 | solution.py:187
  408.8 2.6 copy.496
  411.5 2.0 select_convert_fusion.2
  413.4 5.6 collective-permute-start.25
  421.5 35.1 %while.148 = (s32[]{:T(128)}, f32[6,16,64]{2,1,0:T(8,128)S(1)}, f32[6,512,64]{1,2,0:T(8,128)}, f32[6,512,64]{1,2,0:T(8,128)}, s32[6]{0:T(128)S(1)}, /*index=5*/b...) while((s32[]{:T(128)}, f32[6,16,64]{2,1,0:T(8,128)S(1)}, ...), condition=%wide.region_45.46_spmd, body=%wide.region_44.45_spmd.sunk | while | flops 5325833 | bytes 2404861 | solution.py:187
  464.7 35.1 %while.149 = (s32[]{:T(128)}, f32[6,8,64]{2,1,0:T(8,128)S(1)}, f32[6,512,64]{1,2,0:T(8,128)}, f32[6,512,64]{1,2,0:T(8,128)}, s32[6]{0:T(128)S(1)}, /*index=5*/bf...) while((s32[]{:T(128)}, f32[6,8,64]{2,1,0:T(8,128)S(1)}, ...), condition=%wide.region_50.51_spmd, body=%wide.region_49.50_spmd.sunk | while | flops 2679305 | bytes 2318717 | solution.py:187
  503.5 5.0 collective-permute-start.34
  522.4 2.1 fusion.201
  529.3 8.0 %collective-permute-start.21 = (bf16[2,128,384]{1,2,0:T(8,128)(2,1)}, bf16[2,128,384]{1,2,0:T(8,128)(2,1)}, u32[]{:S(2)}, u32[]{:S(2)}) collective-permute-start(bf16[2,128,384]{1,2,0:T(8,128)(2,1)} %select_convert_fusion.9), channel_id=1, source_target_pairs={{0,1},{1,0},{2,3},{3,2},{4,5},{5,4},{6,7},{7,6},{8,9},{9,8},{10,11... | collective-permute-start | bytes 589832 | tf_op jit(solution)/shard_map/ppermute | solution.py:23
  541.8 2.5 collective-permute-start.26
  545.5 4.6 collective-permute-start.30
  551.3 2.5 collective-permute-start.35
  553.9 3.0 collective-permute-start.24
  556.9 4.5 collective-permute-done.26
  563.5 4.5 collective-permute-start.31
  568.1 3.8 collective-permute-start.36
  572.5 3.7 collective-permute-start.28
  576.2 1.9 collective-permute-done.36
  580.2 4.0 collective-permute-start.32
  586.7 6.2 %collective-permute-start.33 = (bf16[2,16,384]{2,1,0:T(8,128)(2,1)S(1)}, bf16[2,16,384]{2,1,0:T(8,128)(2,1)S(1)}, u32[]{:S(2)}, u32[]{:S(2)}) collective-permute-start(bf16[2,16,384]{2,1,0:T(8,128)(2,1)S(1)} %select_convert_fusion.18), channel_id=1, source_target_pairs={{0,1},{1,0},{2,3},{3,2},{4,5},{5,4},{6,7},{7,6},{8,9},{9,8},{10,11... | collective-permute-start | bytes 73736 | tf_op jit(solution)/shard_map/ppermute | solution.py:23
  592.9 2.8 collective-permute-start.39
  (1021 shorter events, 359.5 us)
Async XLA Ops:
  0.6 14.8 %copy-start.12 = (bf16[128,384]{1,0:T(8,128)(2,1)S(1)}, bf16[128,384]{1,0:T(8,128)(2,1)}, u32[]{:S(2)}) copy-start(bf16[128,384]{1,0:T(8,128)(2,1)} %param.25) | copy-start | bytes 294916
  0.6 12.5 %copy-start.11 = (bf16[128,384]{1,0:T(8,128)(2,1)S(1)}, bf16[128,384]{1,0:T(8,128)(2,1)}, u32[]{:S(2)}) copy-start(bf16[128,384]{1,0:T(8,128)(2,1)} %param.26) | copy-start | bytes 294916
  3.4 47.8 %collective-permute-start.2 = (bf16[2,64,384]{2,1,0:T(8,128)(2,1)S(1)}, bf16[2,64,384]{2,1,0:T(8,128)(2,1)S(1)}, u32[]{:S(2)}, u32[]{:S(2)}) collective-permute-start(bf16[2,64,384]{2,1,0:T(8,128)(2,1)S(1)} %fusion.194), channel_id=1, source_target_pairs={{0,1},{1,0},{2,3},{3,2},{4,5},{5,4},{6,7},{7,6},{8,9},{9,8},{10,11... | collective-permute-start | bytes 294920 | tf_op jit(solution)/shard_map/ppermute | solution.py:23
  13.3 10.7 %copy-start.1 = (bf16[128,384]{1,0:T(8,128)(2,1)S(1)}, bf16[128,384]{1,0:T(8,128)(2,1)}, u32[]{:S(2)}) copy-start(bf16[128,384]{1,0:T(8,128)(2,1)} %param.24) | copy-start | bytes 294916
  13.3 10.7 %copy-start.8 = (bf16[128,384]{1,0:T(8,128)(2,1)S(1)}, bf16[128,384]{1,0:T(8,128)(2,1)}, u32[]{:S(2)}) copy-start(bf16[128,384]{1,0:T(8,128)(2,1)} %param.27) | copy-start | bytes 294916
  13.4 52.1 %collective-permute-start = (bf16[2,128,384]{1,2,0:T(8,128)(2,1)S(1)}, bf16[2,128,384]{1,2,0:T(8,128)(2,1)S(1)}, u32[]{:S(2)}, u32[]{:S(2)}) collective-permute-start(bf16[2,128,384]{1,2,0:T(8,128)(2,1)S(1)} %pad_maximum_fusion.15), channel_id=1, source_target_pairs={{0,1},{1,0},{2,3},{3,2},{4,5},{5,4},{6,7},{7,6},{8,9},{9,8},{10,11... | collective-permute-start | bytes 589832 | tf_op jit(solution)/shard_map/ppermute | solution.py:23
  16.0 26.4 %collective-permute-start.5 = (bf16[2,32,384]{2,1,0:T(8,128)(2,1)S(1)}, bf16[2,32,384]{2,1,0:T(8,128)(2,1)S(1)}, u32[]{:S(2)}, u32[]{:S(2)}) collective-permute-start(bf16[2,32,384]{2,1,0:T(8,128)(2,1)S(1)} %fusion.195), channel_id=1, source_target_pairs={{0,1},{1,0},{2,3},{3,2},{4,5},{5,4},{6,7},{7,6},{8,9},{9,8},{10,11... | collective-permute-start | bytes 147464 | tf_op jit(solution)/shard_map/ppermute | solution.py:23
  18.7 18.2 %collective-permute-start.9 = (bf16[2,16,384]{2,1,0:T(8,128)(2,1)S(1)}, bf16[2,16,384]{2,1,0:T(8,128)(2,1)S(1)}, u32[]{:S(2)}, u32[]{:S(2)}) collective-permute-start(bf16[2,16,384]{2,1,0:T(8,128)(2,1)S(1)} %fusion.196), channel_id=1, source_target_pairs={{0,1},{1,0},{2,3},{3,2},{4,5},{5,4},{6,7},{7,6},{8,9},{9,8},{10,11... | collective-permute-start | bytes 73736 | tf_op jit(solution)/shard_map/ppermute | solution.py:23
  20.9 14.1 %collective-permute-start.14 = (bf16[2,8,384]{2,1,0:T(8,128)(2,1)S(1)}, bf16[2,8,384]{2,1,0:T(8,128)(2,1)S(1)}, u32[]{:S(2)}, u32[]{:S(2)}) collective-permute-start(bf16[2,8,384]{2,1,0:T(8,128)(2,1)S(1)} %fusion.197), channel_id=1, source_target_pairs={{0,1},{1,0},{2,3},{3,2},{4,5},{5,4},{6,7},{7,6},{8,9},{9,8},{10,11... | collective-permute-start | bytes 36872 | tf_op jit(solution)/shard_map/ppermute | solution.py:23
  35.0 5.3 collective-permute-start.15
  37.0 7.3 %collective-permute-start.10 = (bf16[2,32,384]{2,1,0:T(8,128)(2,1)S(1)}, bf16[2,32,384]{2,1,0:T(8,128)(2,1)S(1)}, u32[]{:S(2)}, u32[]{:S(2)}) collective-permute-start(bf16[2,32,384]{2,1,0:T(8,128)(2,1)S(1)} %pad_maximum_fusion.23), channel_id=1, source_target_pairs={{0,2},{2,0},{1,3},{3,1},{4,6},{6,4},{5,7},{7,5},{8,10},{10,8},{9,1... | collective-permute-start | bytes 147464 | tf_op jit(solution)/shard_map/ppermute | solution.py:23
  40.4 8.2 %collective-permute-start.16 = (bf16[2,32,384]{2,1,0:T(8,128)(2,1)S(1)}, bf16[2,32,384]{2,1,0:T(8,128)(2,1)S(1)}, u32[]{:S(2)}, u32[]{:S(2)}) collective-permute-start(bf16[2,32,384]{2,1,0:T(8,128)(2,1)S(1)} %pad_maximum_fusion.24), channel_id=1, source_target_pairs={{0,4},{4,0},{1,5},{5,1},{2,6},{6,2},{3,7},{7,3},{8,12},{12,8},{9,1... | collective-permute-start | bytes 147464 | tf_op jit(solution)/shard_map/ppermute | solution.py:23
  42.4 11.9 %collective-permute-start.6 = (bf16[2,64,384]{2,1,0:T(8,128)(2,1)S(1)}, bf16[2,64,384]{2,1,0:T(8,128)(2,1)S(1)}, u32[]{:S(2)}, u32[]{:S(2)}) collective-permute-start(bf16[2,64,384]{2,1,0:T(8,128)(2,1)S(1)} %pad_maximum_fusion.20), channel_id=1, source_target_pairs={{0,2},{2,0},{1,3},{3,1},{4,6},{6,4},{5,7},{7,5},{8,10},{10,8},{9,1... | collective-permute-start | bytes 294920 | tf_op jit(solution)/shard_map/ppermute | solution.py:23
  44.4 12.4 %collective-permute-start.11 = (bf16[2,64,384]{2,1,0:T(8,128)(2,1)S(1)}, bf16[2,64,384]{2,1,0:T(8,128)(2,1)S(1)}, u32[]{:S(2)}, u32[]{:S(2)}) collective-permute-start(bf16[2,64,384]{2,1,0:T(8,128)(2,1)S(1)} %pad_maximum_fusion.21), channel_id=1, source_target_pairs={{0,4},{4,0},{1,5},{5,1},{2,6},{6,2},{3,7},{7,3},{8,12},{12,8},{9,1... | collective-permute-start | bytes 294920 | tf_op jit(solution)/shard_map/ppermute | solution.py:23
  48.7 14.8 %collective-permute-start.17 = (bf16[2,64,384]{2,1,0:T(8,128)(2,1)S(1)}, bf16[2,64,384]{2,1,0:T(8,128)(2,1)S(1)}, u32[]{:S(2)}, u32[]{:S(2)}) collective-permute-start(bf16[2,64,384]{2,1,0:T(8,128)(2,1)S(1)} %pad_maximum_fusion.22), channel_id=1, source_target_pairs={{0,8},{8,0},{1,9},{9,1},{2,10},{10,2},{3,11},{11,3},{4,12},{12,4},... | collective-permute-start | bytes 294920 | tf_op jit(solution)/shard_map/ppermute | solution.py:23
  51.2 16.5 %collective-permute-start.3 = (bf16[2,128,384]{2,1,0:T(8,128)(2,1)S(1)}, bf16[2,128,384]{2,1,0:T(8,128)(2,1)S(1)}, u32[]{:S(2)}, u32[]{:S(2)}) collective-permute-start(bf16[2,128,384]{2,1,0:T(8,128)(2,1)S(1)} %pad_maximum_fusion.16), channel_id=1, source_target_pairs={{0,2},{2,0},{1,3},{3,1},{4,6},{6,4},{5,7},{7,5},{8,10},{10,8},{9,1... | collective-permute-start | bytes 589832 | tf_op jit(solution)/shard_map/ppermute | solution.py:23
  54.3 23.2 %collective-permute-start.7 = (bf16[2,128,384]{2,1,0:T(8,128)(2,1)S(1)}, bf16[2,128,384]{2,1,0:T(8,128)(2,1)S(1)}, u32[]{:S(2)}, u32[]{:S(2)}) collective-permute-start(bf16[2,128,384]{2,1,0:T(8,128)(2,1)S(1)} %pad_maximum_fusion.17), channel_id=1, source_target_pairs={{0,4},{4,0},{1,5},{5,1},{2,6},{6,2},{3,7},{7,3},{8,12},{12,8},{9,1... | collective-permute-start | bytes 589832 | tf_op jit(solution)/shard_map/ppermute | solution.py:23
  56.8 25.3 %collective-permute-start.12 = (bf16[2,128,384]{2,1,0:T(8,128)(2,1)S(1)}, bf16[2,128,384]{2,1,0:T(8,128)(2,1)S(1)}, u32[]{:S(2)}, u32[]{:S(2)}) collective-permute-start(bf16[2,128,384]{2,1,0:T(8,128)(2,1)S(1)} %pad_maximum_fusion.18), channel_id=1, source_target_pairs={{0,8},{8,0},{1,9},{9,1},{2,10},{10,2},{3,11},{11,3},{4,12},{12,4},... | collective-permute-start | bytes 589832 | tf_op jit(solution)/shard_map/ppermute | solution.py:23
  63.5 21.4 %collective-permute-start.18 = (bf16[2,128,384]{2,1,0:T(8,128)(2,1)S(1)}, bf16[2,128,384]{2,1,0:T(8,128)(2,1)S(1)}, u32[]{:S(2)}, u32[]{:S(2)}) collective-permute-start(bf16[2,128,384]{2,1,0:T(8,128)(2,1)S(1)} %pad_maximum_fusion.19), channel_id=1, source_target_pairs={{0,16},{16,0},{1,17},{17,1},{2,18},{18,2},{3,19},{19,3},{4,20},{20... | collective-permute-start | bytes 589832 | tf_op jit(solution)/shard_map/ppermute | solution.py:23
  65.6 23.3 %collective-permute-start.1 = (bf16[2,256,384]{1,2,0:T(8,128)(2,1)S(1)}, bf16[2,256,384]{1,2,0:T(8,128)(2,1)S(1)}, u32[]{:S(2)}, u32[]{:S(2)}) collective-permute-start(bf16[2,256,384]{1,2,0:T(8,128)(2,1)S(1)} %pad_maximum_fusion.10), channel_id=1, source_target_pairs={{0,2},{2,0},{1,3},{3,1},{4,6},{6,4},{5,7},{7,5},{8,10},{10,8},{9,1... | collective-permute-start | bytes 1179656 | tf_op jit(solution)/shard_map/ppermute | solution.py:23
  68.7 51.3 %collective-permute-start.4 = (bf16[2,256,384]{2,1,0:T(8,128)(2,1)}, bf16[2,256,384]{2,1,0:T(8,128)(2,1)}, u32[]{:S(2)}, u32[]{:S(2)}) collective-permute-start(bf16[2,256,384]{2,1,0:T(8,128)(2,1)} %pad_maximum_fusion.11), channel_id=1, source_target_pairs={{0,4},{4,0},{1,5},{5,1},{2,6},{6,2},{3,7},{7,3},{8,12},{12,8},{9,1... | collective-permute-start | bytes 1179656 | tf_op jit(solution)/shard_map/ppermute | solution.py:23
  78.4 64.6 %collective-permute-start.8 = (bf16[2,256,384]{2,1,0:T(8,128)(2,1)}, bf16[2,256,384]{2,1,0:T(8,128)(2,1)}, u32[]{:S(2)}, u32[]{:S(2)}) collective-permute-start(bf16[2,256,384]{2,1,0:T(8,128)(2,1)} %pad_maximum_fusion.12), channel_id=1, source_target_pairs={{0,8},{8,0},{1,9},{9,1},{2,10},{10,2},{3,11},{11,3},{4,12},{12,4},... | collective-permute-start | bytes 1179656 | tf_op jit(solution)/shard_map/ppermute | solution.py:23
  83.0 81.6 %collective-permute-start.13 = (bf16[2,256,384]{2,1,0:T(8,128)(2,1)}, bf16[2,256,384]{2,1,0:T(8,128)(2,1)}, u32[]{:S(2)}, u32[]{:S(2)}) collective-permute-start(bf16[2,256,384]{2,1,0:T(8,128)(2,1)} %pad_maximum_fusion.13), channel_id=1, source_target_pairs={{0,16},{16,0},{1,17},{17,1},{2,18},{18,2},{3,19},{19,3},{4,20},{20... | collective-permute-start | bytes 1179656 | tf_op jit(solution)/shard_map/ppermute | solution.py:23
  85.8 100.7 %collective-permute-start.19 = (bf16[2,256,384]{2,1,0:T(8,128)(2,1)}, bf16[2,256,384]{2,1,0:T(8,128)(2,1)}, u32[]{:S(2)}, u32[]{:S(2)}) collective-permute-start(bf16[2,256,384]{2,1,0:T(8,128)(2,1)} %pad_maximum_fusion.14), channel_id=1, source_target_pairs={{0,32},{32,0},{1,33},{33,1},{2,34},{34,2},{3,35},{35,3},{4,36},{36... | collective-permute-start | bytes 1179656 | tf_op jit(solution)/shard_map/ppermute | solution.py:23
  121.8 13.4 %copy-start.93 = (pred[6,2]{1,0:T(8,128)(4,1)S(1)}, pred[6,2]{1,0:T(8,128)(4,1)}, u32[]{:S(2)}) copy-start(pred[6,2]{1,0:T(8,128)(4,1)} %iota_compare_fusion.6) | copy-start | bytes 40
  144.9 12.5 %copy-start.91 = (pred[6,4]{1,0:T(8,128)(4,1)S(1)}, pred[6,4]{1,0:T(8,128)(4,1)}, u32[]{:S(2)}) copy-start(pred[6,4]{1,0:T(8,128)(4,1)} %copy-done.90) | copy-start | bytes 76
  166.5 13.3 %copy-start.88 = (pred[6,8]{1,0:T(8,128)(4,1)S(1)}, pred[6,8]{1,0:T(8,128)(4,1)}, u32[]{:S(2)}) copy-start(pred[6,8]{1,0:T(8,128)(4,1)} %copy-done.87) | copy-start | bytes 148
  313.9 212.9 %collective-permute-start.20 = (bf16[2,256,384]{1,2,0:T(8,128)(2,1)}, bf16[2,256,384]{1,2,0:T(8,128)(2,1)}, u32[]{:S(2)}, u32[]{:S(2)}) collective-permute-start(bf16[2,256,384]{1,2,0:T(8,128)(2,1)} %select_convert_fusion.4), channel_id=1, source_target_pairs={{0,2},{2,0},{1,3},{3,1},{4,6},{6,4},{5,7},{7,5},{8,10},{10,8},{9,1... | collective-permute-start | bytes 1179656 | tf_op jit(solution)/shard_map/ppermute | solution.py:23
  364.1 173.2 %collective-permute-start.22 = (bf16[2,256,384]{2,1,0:T(8,128)(2,1)}, bf16[2,256,384]{2,1,0:T(8,128)(2,1)}, u32[]{:S(2)}, u32[]{:S(2)}) collective-permute-start(bf16[2,256,384]{2,1,0:T(8,128)(2,1)} %select_convert_fusion.3), channel_id=1, source_target_pairs={{0,4},{4,0},{1,5},{5,1},{2,6},{6,2},{3,7},{7,3},{8,12},{12,8},{9,1... | collective-permute-start | bytes 1179656 | tf_op jit(solution)/shard_map/ppermute | solution.py:23
  413.4 127.1 %collective-permute-start.25 = (bf16[2,256,384]{2,1,0:T(8,128)(2,1)}, bf16[2,256,384]{2,1,0:T(8,128)(2,1)}, u32[]{:S(2)}, u32[]{:S(2)}) collective-permute-start(bf16[2,256,384]{2,1,0:T(8,128)(2,1)} %select_convert_fusion.2), channel_id=1, source_target_pairs={{0,8},{8,0},{1,9},{9,1},{2,10},{10,2},{3,11},{11,3},{4,12},{12,4},... | collective-permute-start | bytes 1179656 | tf_op jit(solution)/shard_map/ppermute | solution.py:23
  460.5 83.8 %collective-permute-start.29 = (bf16[2,256,384]{2,1,0:T(8,128)(2,1)}, bf16[2,256,384]{2,1,0:T(8,128)(2,1)}, u32[]{:S(2)}, u32[]{:S(2)}) collective-permute-start(bf16[2,256,384]{2,1,0:T(8,128)(2,1)} %select_convert_fusion.1), channel_id=1, source_target_pairs={{0,16},{16,0},{1,17},{17,1},{2,18},{18,2},{3,19},{19,3},{4,20},{20... | collective-permute-start | bytes 1179656 | tf_op jit(solution)/shard_map/ppermute | solution.py:23
  503.5 46.7 %collective-permute-start.34 = (bf16[2,256,384]{2,1,0:T(8,128)(2,1)}, bf16[2,256,384]{2,1,0:T(8,128)(2,1)}, u32[]{:S(2)}, u32[]{:S(2)}) collective-permute-start(bf16[2,256,384]{2,1,0:T(8,128)(2,1)} %select_convert_fusion), channel_id=1, source_target_pairs={{0,32},{32,0},{1,33},{33,1},{2,34},{34,2},{3,35},{35,3},{4,36},{36... | collective-permute-start | bytes 1179656 | tf_op jit(solution)/shard_map/ppermute | solution.py:23
  526.8 10.5 %copy-start.2 = (f32[1,512,384]{2,1,0:T(8,128)S(1)}, f32[1,512,384]{2,1,0:T(8,128)}, u32[]{:S(2)}) copy-start(f32[1,512,384]{2,1,0:T(8,128)} %copy.491) | copy-start | bytes 2359300
  529.3 67.5 %collective-permute-start.21 = (bf16[2,128,384]{1,2,0:T(8,128)(2,1)}, bf16[2,128,384]{1,2,0:T(8,128)(2,1)}, u32[]{:S(2)}, u32[]{:S(2)}) collective-permute-start(bf16[2,128,384]{1,2,0:T(8,128)(2,1)} %select_convert_fusion.9), channel_id=1, source_target_pairs={{0,1},{1,0},{2,3},{3,2},{4,5},{5,4},{6,7},{7,6},{8,9},{9,8},{10,11... | collective-permute-start | bytes 589832 | tf_op jit(solution)/shard_map/ppermute | solution.py:23
  538.6 15.1 %collective-permute-start.23 = (bf16[2,128,384]{2,1,0:T(8,128)(2,1)S(1)}, bf16[2,128,384]{2,1,0:T(8,128)(2,1)S(1)}, u32[]{:S(2)}, u32[]{:S(2)}) collective-permute-start(bf16[2,128,384]{2,1,0:T(8,128)(2,1)S(1)} %select_convert_fusion.8), channel_id=1, source_target_pairs={{0,2},{2,0},{1,3},{3,1},{4,6},{6,4},{5,7},{7,5},{8,10},{10,8},{9,1... | collective-permute-start | bytes 589832 | tf_op jit(solution)/shard_map/ppermute | solution.py:23
  541.8 19.5 %collective-permute-start.26 = (bf16[2,128,384]{2,1,0:T(8,128)(2,1)S(1)}, bf16[2,128,384]{2,1,0:T(8,128)(2,1)S(1)}, u32[]{:S(2)}, u32[]{:S(2)}) collective-permute-start(bf16[2,128,384]{2,1,0:T(8,128)(2,1)S(1)} %select_convert_fusion.7), channel_id=1, source_target_pairs={{0,4},{4,0},{1,5},{5,1},{2,6},{6,2},{3,7},{7,3},{8,12},{12,8},{9,1... | collective-permute-start | bytes 589832 | tf_op jit(solution)/shard_map/ppermute | solution.py:23
  545.5 17.9 %collective-permute-start.30 = (bf16[2,128,384]{2,1,0:T(8,128)(2,1)S(1)}, bf16[2,128,384]{2,1,0:T(8,128)(2,1)S(1)}, u32[]{:S(2)}, u32[]{:S(2)}) collective-permute-start(bf16[2,128,384]{2,1,0:T(8,128)(2,1)S(1)} %select_convert_fusion.6), channel_id=1, source_target_pairs={{0,8},{8,0},{1,9},{9,1},{2,10},{10,2},{3,11},{11,3},{4,12},{12,4},... | collective-permute-start | bytes 589832 | tf_op jit(solution)/shard_map/ppermute | solution.py:23
  551.3 16.7 %collective-permute-start.35 = (bf16[2,128,384]{2,1,0:T(8,128)(2,1)S(1)}, bf16[2,128,384]{2,1,0:T(8,128)(2,1)S(1)}, u32[]{:S(2)}, u32[]{:S(2)}) collective-permute-start(bf16[2,128,384]{2,1,0:T(8,128)(2,1)S(1)} %select_convert_fusion.5), channel_id=1, source_target_pairs={{0,16},{16,0},{1,17},{17,1},{2,18},{18,2},{3,19},{19,3},{4,20},{20... | collective-permute-start | bytes 589832 | tf_op jit(solution)/shard_map/ppermute | solution.py:23
  553.9 18.1 %collective-permute-start.24 = (bf16[2,64,384]{2,1,0:T(8,128)(2,1)S(1)}, bf16[2,64,384]{2,1,0:T(8,128)(2,1)S(1)}, u32[]{:S(2)}, u32[]{:S(2)}) collective-permute-start(bf16[2,64,384]{2,1,0:T(8,128)(2,1)S(1)} %select_convert_fusion.13), channel_id=1, source_target_pairs={{0,1},{1,0},{2,3},{3,2},{4,5},{5,4},{6,7},{7,6},{8,9},{9,8},{10,11... | collective-permute-start | bytes 294920 | tf_op jit(solution)/shard_map/ppermute | solution.py:23
  561.5 10.5 %collective-permute-start.27 = (bf16[2,64,384]{2,1,0:T(8,128)(2,1)S(1)}, bf16[2,64,384]{2,1,0:T(8,128)(2,1)S(1)}, u32[]{:S(2)}, u32[]{:S(2)}) collective-permute-start(bf16[2,64,384]{2,1,0:T(8,128)(2,1)S(1)} %select_convert_fusion.12), channel_id=1, source_target_pairs={{0,2},{2,0},{1,3},{3,1},{4,6},{6,4},{5,7},{7,5},{8,10},{10,8},{9,1... | collective-permute-start | bytes 294920 | tf_op jit(solution)/shard_map/ppermute | solution.py:23
  563.5 16.6 %collective-permute-start.31 = (bf16[2,64,384]{2,1,0:T(8,128)(2,1)S(1)}, bf16[2,64,384]{2,1,0:T(8,128)(2,1)S(1)}, u32[]{:S(2)}, u32[]{:S(2)}) collective-permute-start(bf16[2,64,384]{2,1,0:T(8,128)(2,1)S(1)} %select_convert_fusion.11), channel_id=1, source_target_pairs={{0,4},{4,0},{1,5},{5,1},{2,6},{6,2},{3,7},{7,3},{8,12},{12,8},{9,1... | collective-permute-start | bytes 294920 | tf_op jit(solution)/shard_map/ppermute | solution.py:23
  568.1 10.1 %collective-permute-start.36 = (bf16[2,64,384]{2,1,0:T(8,128)(2,1)S(1)}, bf16[2,64,384]{2,1,0:T(8,128)(2,1)S(1)}, u32[]{:S(2)}, u32[]{:S(2)}) collective-permute-start(bf16[2,64,384]{2,1,0:T(8,128)(2,1)S(1)} %select_convert_fusion.10), channel_id=1, source_target_pairs={{0,8},{8,0},{1,9},{9,1},{2,10},{10,2},{3,11},{11,3},{4,12},{12,4},... | collective-permute-start | bytes 294920 | tf_op jit(solution)/shard_map/ppermute | solution.py:23
  572.5 13.7 %collective-permute-start.28 = (bf16[2,32,384]{2,1,0:T(8,128)(2,1)S(1)}, bf16[2,32,384]{2,1,0:T(8,128)(2,1)S(1)}, u32[]{:S(2)}, u32[]{:S(2)}) collective-permute-start(bf16[2,32,384]{2,1,0:T(8,128)(2,1)S(1)} %select_convert_fusion.16), channel_id=1, source_target_pairs={{0,1},{1,0},{2,3},{3,2},{4,5},{5,4},{6,7},{7,6},{8,9},{9,8},{10,11... | collective-permute-start | bytes 147464 | tf_op jit(solution)/shard_map/ppermute | solution.py:23
  578.2 6.0 %collective-permute-start.37 = (bf16[2,32,384]{2,1,0:T(8,128)(2,1)S(1)}, bf16[2,32,384]{2,1,0:T(8,128)(2,1)S(1)}, u32[]{:S(2)}, u32[]{:S(2)}) collective-permute-start(bf16[2,32,384]{2,1,0:T(8,128)(2,1)S(1)} %select_convert_fusion.14), channel_id=1, source_target_pairs={{0,4},{4,0},{1,5},{5,1},{2,6},{6,2},{3,7},{7,3},{8,12},{12,8},{9,1... | collective-permute-start | bytes 147464 | tf_op jit(solution)/shard_map/ppermute | solution.py:23
  580.2 6.0 %collective-permute-start.32 = (bf16[2,32,384]{2,1,0:T(8,128)(2,1)S(1)}, bf16[2,32,384]{2,1,0:T(8,128)(2,1)S(1)}, u32[]{:S(2)}, u32[]{:S(2)}) collective-permute-start(bf16[2,32,384]{2,1,0:T(8,128)(2,1)S(1)} %select_convert_fusion.15), channel_id=1, source_target_pairs={{0,2},{2,0},{1,3},{3,1},{4,6},{6,4},{5,7},{7,5},{8,10},{10,8},{9,1... | collective-permute-start | bytes 147464 | tf_op jit(solution)/shard_map/ppermute | solution.py:23
  584.3 8.6 %collective-permute-start.38 = (bf16[2,16,384]{2,1,0:T(8,128)(2,1)S(1)}, bf16[2,16,384]{2,1,0:T(8,128)(2,1)S(1)}, u32[]{:S(2)}, u32[]{:S(2)}) collective-permute-start(bf16[2,16,384]{2,1,0:T(8,128)(2,1)S(1)} %select_convert_fusion.17), channel_id=1, source_target_pairs={{0,2},{2,0},{1,3},{3,1},{4,6},{6,4},{5,7},{7,5},{8,10},{10,8},{9,1... | collective-permute-start | bytes 73736 | tf_op jit(solution)/shard_map/ppermute | solution.py:23
  586.7 9.1 %collective-permute-start.33 = (bf16[2,16,384]{2,1,0:T(8,128)(2,1)S(1)}, bf16[2,16,384]{2,1,0:T(8,128)(2,1)S(1)}, u32[]{:S(2)}, u32[]{:S(2)}) collective-permute-start(bf16[2,16,384]{2,1,0:T(8,128)(2,1)S(1)} %select_convert_fusion.18), channel_id=1, source_target_pairs={{0,1},{1,0},{2,3},{3,2},{4,5},{5,4},{6,7},{7,6},{8,9},{9,8},{10,11... | collective-permute-start | bytes 73736 | tf_op jit(solution)/shard_map/ppermute | solution.py:23
  592.9 3.6 collective-permute-start.39
  (87 other events, 432.8 us)
where the time goes:
time: 605 us; the launch traced here: 600 us
  local copies, waits for them, and re-layouts  190 us (31%)
  starting transfers between devices  135 us (22%)
  matrix products  111 us (18%)
  loops' own time  98.2 us (16%)
  other arithmetic  50.5 us (8%)
  waiting for transfers between devices  11.9 us (2%)
    ppermute x40, starting transfers between devices, from_partner(): return lax.ppermute(block, axis, route)  135 us
    another operation x5, loops' own time, level_backward(): lax.map(one_head, jnp.arange(head_count))  78.3 us
    dynamic_slice x60, local copies, waits for them, and re-layouts, level_forward(): row_max, row_sum, weighted = lax.map(one_head, jnp.arange(head_count))  43.9 us
    dot_general x30, matrix products, one_head(): jnp.einsum('sab,sad->sbd', grad_scores, query_head, preferred_element_typ...  28.2 us
    dot_general x30, matrix products, one_head(): jnp.einsum('sab,sad->sbd', weights.astype(jnp.bfloat16), grad_head, prefe...  27.9 us
    dynamic_update_slice x60, local copies, waits for them, and re-layouts, level_forward(): row_max, row_sum, weighted = lax.map(one_head, jnp.arange(head_count))  24.4 us
    dot_general x60, matrix products, one_head(): jnp.einsum('sad,sbd->sab', query_head, key_head, preferred_element_type=j...  21.8 us
    broadcast_in_dim x36, local copies, waits for them, and re-layouts, place_rows(): jnp.where(chosen, source[..., :, None, :], jnp.full((), fill_value, sourc...  20.5 us
  transfers between devices with their start and end apart: 40, of which 4 were waited for; matrix products, arithmetic and copies ran while one was open for 39% of the time, Pallas kernels for 0%

commit v1 on v0

v1 whole, which is shorter than its diff:
```python
import jax
import jax.numpy as jnp
from jax import lax
from jax.experimental import pallas as pl
from jax.experimental.pallas import tpu as pltpu
from jax.sharding import PartitionSpec as P

HD = 64
NEG = -1e30
F32 = jnp.float32
BF16 = jnp.bfloat16

CORE, Y_ONE, Y_TWO, Y_SIX, Z_ONE, Z_TWO = 1, 2, 4, 12, 16, 32


def swap_with(block, flip):
    count = lax.axis_size("seq")
    return lax.ppermute(block, "seq", [(i, i ^ flip) for i in range(count)])


def dot(a, b):
    return jnp.dot(a, b, preferred_element_type=F32)


def left_half(shape):
    return lax.broadcasted_iota(jnp.int32, shape, len(shape) - 1) < HD


def pair_up(first, second, odd):
    low = left_half(first.shape)
    if odd:
        return jnp.where(low, pltpu.roll(first, HD, 1), second)
    return jnp.where(low, first, pltpu.roll(second, HD, 1))


def split_heads(where_ref, q_ref, k_ref, v_ref, g_ref, send_ref, keep_ref):
    core = where_ref[0]

    def head(h):
        tile = slice((h // 2) * 128, (h // 2) * 128 + 128)
        q, k, v, g = (r[:, tile].astype(F32) for r in (q_ref, k_ref, v_ref, g_ref))
        return pair_up(q, g, h % 2), pair_up(k, v, h % 2)

    for s in range(3):
        low, high = head(s), head(s + 3)
        for part in range(2):
            cols = slice(s * 256 + part * 128, s * 256 + part * 128 + 128)
            keep_ref[:, cols] = jnp.where(core == 0, low[part], high[part]).astype(BF16)
            send_ref[:, cols] = jnp.where(core == 0, high[part], low[part]).astype(BF16)


def source_rows(shape, axis, head):
    i = lax.broadcasted_iota(jnp.int32, shape, axis)
    row = jnp.where(i < 64, 4 + 8 * (i - 32), jnp.where(i < 128, 2 + 4 * (i - 64), 1 + 2 * (i - 128)))
    row = jnp.where(i < 16, 16 * i, jnp.where(i < 32, 8 + 16 * (i - 16), row))
    return (row + head) & 255


def sort_rows(where_ref, keep_ref, recv_ref, send_ref, own_ref):
    core, odd = where_ref[0], where_ref[1]
    keep, recv = keep_ref[...], recv_ref[...]
    rows = jnp.concatenate(
        [jnp.where(core == 0, keep, recv), jnp.where(core == 0, recv, keep)], 0
    )
    lane = lax.broadcasted_iota(jnp.int32, (256, 256), 1)
    slots = []
    for s in range(3):
        order = (lane == source_rows((256, 256), 0, 3 * core + s)).astype(BF16)
        slots.append(dot(order, rows[:, s * 256 : s * 256 + 256]))
    send_ref[:, :256] = jnp.where(odd == 0, slots[2], slots[0]).astype(BF16)
    send_ref[:, 256:] = slots[1][:, 128:].astype(BF16)
    own_ref[:, :256] = jnp.where(odd == 0, slots[0], slots[2]).astype(BF16)
    own_ref[:, 256:] = slots[1].astype(BF16)


def unsort_rows(where_ref, own_ref, recv_ref, send_ref, keep_ref):
    core, odd = where_ref[0], where_ref[1]
    first = jnp.where(odd == 0, own_ref[:, :256], recv_ref[:, :256].astype(F32)).astype(BF16)
    third = jnp.where(odd == 0, recv_ref[:, :256].astype(F32), own_ref[:, :256]).astype(BF16)
    middle = jnp.concatenate(
        [own_ref[:, 256:384], own_ref[:, 384:] + recv_ref[:, 256:].astype(F32)], 1
    ).astype(BF16)
    sub = lax.broadcasted_iota(jnp.int32, (256, 256), 0)
    for s, slot in enumerate((first, middle, third)):
        order = (sub == source_rows((256, 256), 1, 3 * core + s)).astype(BF16)
        rows = dot(order, slot)
        cols = slice(s * 256, s * 256 + 256)
        keep_ref[:, cols] = jnp.where(core == 0, rows[:128], rows[128:]).astype(BF16)
        send_ref[:, cols] = jnp.where(core == 0, rows[128:], rows[:128]).astype(BF16)


def join_heads(where_ref, keep_ref, recv_ref, att_ref, dq_ref, dk_ref, dv_ref):
    core = where_ref[0]
    keep, recv = keep_ref[...].astype(F32), recv_ref[...].astype(F32)
    low = jnp.where(core == 0, keep, recv)
    high = jnp.where(core == 0, recv, keep)

    def part(h, p):
        half = low if h < 3 else high
        start = (h % 3) * 256 + p * 128
        return half[:, start : start + 128]

    mask = left_half((128, 128))
    for p, (left_ref, right_ref) in enumerate(((dq_ref, att_ref), (dk_ref, dv_ref))):
        for j in range(3):
            even, odd = part(2 * j, p), part(2 * j + 1, p)
            tile = slice(j * 128, j * 128 + 128)
            left_ref[:, tile] = jnp.where(mask, even, pltpu.roll(odd, HD, 1)).astype(BF16)
            right_ref[:, tile] = jnp.where(mask, pltpu.roll(even, HD, 1), odd).astype(BF16)


def rank(shape, axis, step):
    i = lax.broadcasted_iota(jnp.int32, shape, axis)
    rank_of = jnp.zeros(shape, F32)
    for level in range(4):
        rank_of = rank_of + (i < (step << level)).astype(F32)
    return rank_of


def key_rank(part, shape):
    i = lax.broadcasted_iota(jnp.int32, shape, 0)
    if part == 2:
        i = i & 127
    elif part == 3:
        i = i & 63
    elif part == 4:
        i = i & 31
    rank_of = jnp.zeros(shape, F32)
    for level in range(4):
        rank_of = rank_of + (i < (32 << level)).astype(F32)
    return rank_of


def attend(qga_ref, qgb_ref, kv0_ref, r1_ref, r2_ref, r3_ref, r4_ref,
           outa_ref, outb_ref, d0_ref, d1_ref, d2_ref, d3_ref, d4_ref, e_ref):
    kv_refs = (kv0_ref, r1_ref, r2_ref, r3_ref, r4_ref)
    d_refs = (d0_ref, d1_ref, d2_ref, d3_ref, d4_ref)
    sub = lax.broadcasted_iota(jnp.int32, (128, 1), 0) < HD
    for which, (qg_ref, out_ref) in enumerate(((qga_ref, outa_ref), (qgb_ref, outb_ref))):
        cols = slice(which * 128, which * 128 + 128)
        total = qg_ref.shape[0]
        step = total // 16
        qg = qg_ref[...].astype(F32)
        scaled = jnp.where(left_half(qg.shape), qg * HD**-0.5, qg)
        qg_b = scaled.astype(BF16)
        turned = scaled.T
        q_t = jnp.where(sub, turned, 0.0).astype(BF16)
        g_t = jnp.where(sub, 0.0, turned)
        g_tb = g_t.astype(BF16)
        half = total // 2
        pieces = [(0, 0, 256, 0, half, True), (0, 0, 256, half, half, False), (0, 256, 256, 0, total, False)]
        for part in range(1, 5):
            pieces.append((part, 0, 256, 0, max(128, total >> part), True))
        maxima = [jnp.full((1, 128), NEG, F32) for _ in range(total // 128)]
        place = 0
        places, counts = [], []
        for part, row, rows, first, width, weighted in pieces:
            keys = kv_refs[part][row : row + rows, cols]
            scores = dot(keys, q_t[:, first : first + width])
            count = None
            if weighted:
                count = jnp.minimum(key_rank(part, (rows, width)), rank((rows, width), 1, step)) + (1.0 - part)
                if part > 0 and (total >> part) < width:
                    scores = jnp.where(count > 0.0, scores, NEG)
                count = jnp.maximum(count, 0.0)
            e_ref[place : place + rows, :width] = scores
            top = jnp.max(scores, axis=0, keepdims=True)
            for t in range(width // 128):
                at = first // 128 + t
                maxima[at] = jnp.maximum(maxima[at], top[:, t * 128 : t * 128 + 128])
            places.append(place)
            counts.append(count)
            place += rows
        peak = jnp.concatenate(maxima, 1)
        sums = [jnp.zeros((1, 128), F32) for _ in range(total // 128)]
        accs = [jnp.zeros((128, 128), F32) for _ in range(total // 128)]
        for (part, row, rows, first, width, weighted), place, count in zip(pieces, places, counts):
            weights = jnp.exp(e_ref[place : place + rows, :width] - peak[:, first : first + width])
            if weighted:
                weights = weights * count
            e_ref[place : place + rows, :width] = weights
            turned_keys = kv_refs[part][row : row + rows, cols].T
            acc = dot(turned_keys, weights.astype(BF16))
            total_w = jnp.sum(weights, axis=0, keepdims=True)
            for t in range(width // 128):
                at = first // 128 + t
                sums[at] = sums[at] + total_w[:, t * 128 : t * 128 + 128]
                accs[at] = accs[at] + acc[:, t * 128 : t * 128 + 128]
        inverse = 1.0 / jnp.concatenate(sums, 1)
        attended = (jnp.concatenate(accs, 1) * inverse).astype(BF16).astype(F32)
        delta = jnp.sum(g_t * attended, axis=0, keepdims=True)
        queries = [jnp.zeros((128, 128), F32) for _ in range(total // 128)]
        partial = {}
        for (part, row, rows, first, width, weighted), place in zip(pieces, places):
            span = slice(first, first + width)
            keys = kv_refs[part][row : row + rows, cols]
            probs = e_ref[place : place + rows, :width] * inverse[:, span]
            grads = probs * (dot(keys, g_tb[:, span]) - delta[:, span])
            grads_b = grads.astype(BF16)
            d_keys = dot(grads_b, qg_b[span])
            d_vals = dot(probs.astype(BF16), qg_b[span])
            both = jnp.where(left_half(d_keys.shape), d_keys, d_vals)
            if (part, row) in partial:
                both = both + partial[part, row]
            partial[part, row] = both
            d_query = dot(keys.T, grads_b)
            for t in range(width // 128):
                at = first // 128 + t
                queries[at] = queries[at] + d_query[:, t * 128 : t * 128 + 128]
        for (part, row), both in partial.items():
            ref = d_refs[part]
            ref[row : row + 256, cols] = both.astype(ref.dtype)
        out = jnp.where(sub, jnp.concatenate(queries, 1) * HD**-0.5, attended)
        out_ref[...] = out.T


def call(body, outs, *args, scalar=True, scratch=(), flops=0):
    vmem = pl.BlockSpec(memory_space=pltpu.VMEM)
    specs = [vmem] * len(args)
    if scalar:
        specs[0] = pl.BlockSpec(memory_space=pltpu.SMEM)
    moved = sum(a.size * a.dtype.itemsize for a in args)
    return pl.pallas_call(
        body,
        out_shape=[jax.ShapeDtypeStruct(s, d) for s, d in outs],
        in_specs=specs,
        out_specs=[vmem] * len(outs),
        scratch_shapes=list(scratch),
        compiler_params=pltpu.CompilerParams(vmem_limit_bytes=48 * 1024 * 1024),
        cost_estimate=pl.CostEstimate(flops=flops, bytes_accessed=moved, transcendentals=0),
    )(*args)


CLASSES = (0, 16, 32, 64, 128, 256)


def interleave(own, partner):
    parts = []
    for a, b in zip(CLASSES, CLASSES[1:]):
        parts += [own[a:b], partner[a:b]]
    return jnp.concatenate(parts, 0)


def separate(rows):
    own, partner = [], []
    for a, b in zip(CLASSES, CLASSES[1:]):
        own.append(rows[2 * a : a + b])
        partner.append(rows[a + b : 2 * b])
    return jnp.concatenate(own, 0), jnp.concatenate(partner, 0)


def head_rows(blocks, rows):
    return jnp.concatenate([array[at : at + rows] for array, at in blocks], 0)


def add_rows(arrays, blocks, rows, extra):
    extra = extra.astype(F32)
    for n, (name, at) in enumerate(blocks):
        piece = extra[n * rows : n * rows + rows]
        arrays[name] = lax.dynamic_update_slice_in_dim(
            arrays[name], arrays[name][at : at + rows] + piece, at, 0
        )


def per_device(query, keys, values, grad_out):
    device = lax.axis_index("seq")
    place = jnp.stack([device & 1, (device >> 1) & 1]).astype(jnp.int32)
    send, keep = call(split_heads, [((128, 768), BF16)] * 2, place, query, keys, values, grad_out)
    send, own = call(sort_rows, [((256, 384), BF16), ((256, 512), BF16)], place, keep, swap_with(send, CORE))
    other = swap_with(send, Y_ONE)
    qg_a = interleave(own[:, :128], other[:, :128])
    qg_b = own[:, 256:384]
    kv0 = interleave(
        jnp.concatenate([own[:, 128:256], own[:, 384:]], 1), other[:, 128:]
    )
    b1 = [(0, 0)]
    b2 = b1 + [(1, 0)]
    b3 = b2 + [(2, 0), (2, 128)]
    b4 = b3 + [(3, 0), (3, 64), (3, 128), (3, 192)]
    steps = ((b1, 256, Y_TWO), (b2, 128, Y_SIX), (b3, 64, Z_ONE), (b4, 32, Z_TWO))
    kv = [kv0]
    for blocks, rows, flip in steps:
        kv.append(swap_with(head_rows([(kv[n], at) for n, at in blocks], rows), flip))
    out_a, out_b, *grads = call(
        attend,
        [((512, 128), F32), ((256, 128), F32), ((512, 256), F32)]
        + [((256, 256), F32)] * 3 + [((256, 256), BF16)],
        qg_a, qg_b, *kv,
        scalar=False,
        scratch=[pltpu.VMEM((7 * 256, 512), F32)],
        flops=int(6e8),
    )
    for part, (blocks, rows, flip) in reversed(list(enumerate(steps, 1))):
        add_rows(grads, blocks, rows, swap_with(grads[part].astype(BF16), flip))
    own_a, other_a = separate(out_a)
    own_kv, other_kv = separate(grads[0])
    send = jnp.concatenate([other_a, other_kv], 1).astype(BF16)
    own = jnp.concatenate([own_a, own_kv[:, :128], out_b, own_kv[:, 128:]], 1)
    send, keep = call(unsort_rows, [((128, 768), BF16)] * 2, place, own, swap_with(send, Y_ONE))
    return tuple(
        call(join_heads, [((128, 384), BF16)] * 4, place, keep, swap_with(send, CORE))
    )


def solution(mesh):
    spec = P("seq", None)
    return jax.shard_map(
        per_device, mesh=mesh, in_specs=(spec,) * 4, out_specs=(spec,) * 4, check_vma=False
    )
```

time: 605 us -> 114 us (0.19)
  local copies, waits for them, and re-layouts: 190 us -> 3.94 us
  matrix products: 111 us -> 0 us
  loops' own time: 98.2 us -> 0 us
  starting transfers between devices: 135 us -> 48.4 us
  other arithmetic: 50.5 us -> 0.52 us
  waiting for transfers between devices: 11.9 us -> 51.9 us
  Pallas kernels: 0 us -> 7.73 us
    dot_general x210 -> x0, matrix products: 111 us -> none  [the longest x30 28.2 us: one_head(): jnp.einsum('sab,sad->sbd', grad_scores, query_head, preferred_element_typ...]
    another operation x10 -> x0, loops' own time: 98.2 us -> none  [the longest x5 78.3 us: level_backward(): lax.map(one_head, jnp.arange(head_count))]
    ppermute x40 -> x12, starting transfers between devices: 135 us -> 48.4 us  [swap_with(): return lax.ppermute(block, 'seq', [(i, i ^ flip) for i in range(count)])]
    dynamic_slice x60 -> x0, local copies, waits for them, and re-layouts: 43.9 us -> none  [level_forward(): row_max, row_sum, weighted = lax.map(one_head, jnp.arange(head_count))]
    ppermute x40 -> x12, waiting for transfers between devices: 11.9 us -> 51.9 us  [swap_with(): return lax.ppermute(block, 'seq', [(i, i ^ flip) for i in range(count)])]
    broadcast_in_dim x88 -> x0, local copies, waits for them, and re-layouts: 33.1 us -> none  [the longest x36 20.5 us: place_rows(): jnp.where(chosen, source[..., :, None, :], jnp.full((), fill_value, sourc...]
    another operation x32 -> x0, local copies, waits for them, and re-layouts: 27.1 us -> none  [the longest x8 13.3 us: level_backward(): jnp.stack([to_flat(grad_keys), to_flat(grad_values)], 0)]
    dynamic_update_slice x60 -> x0, local copies, waits for them, and re-layouts: 24.4 us -> none  [level_forward(): row_max, row_sum, weighted = lax.map(one_head, jnp.arange(head_count))]
  transfers between devices with their start and end apart: 40 -> 12, of which waited for: 4 -> 12; matrix products, arithmetic and copies ran while one was open for 39% -> 0% of each run, Pallas kernels for 0% -> 0%
where the time goes in v1:
time: 114 us
  waiting for transfers between devices  51.9 us (46%)
  starting transfers between devices  48.4 us (42%)
  Pallas kernels  7.73 us (7%)
  local copies, waits for them, and re-layouts  3.94 us (3%)
  between operations  1.24 us (1%)
    ppermute x12, waiting for transfers between devices, swap_with(): return lax.ppermute(block, 'seq', [(i, i ^ flip) for i in range(count)])  51.9 us
    ppermute x12, starting transfers between devices, swap_with(): return lax.ppermute(block, 'seq', [(i, i ^ flip) for i in range(count)])  48.4 us
    pallas_call x5, Pallas kernels, call(): pl.pallas_call(body, out_shape=[jax.ShapeDtypeStruct(s, d) for s, d in ou...  7.73 us
    unnamed x51, local copies, waits for them, and re-layouts  3.8 us
  transfers between devices with their start and end apart: 12, of which 12 were waited for; matrix products, arithmetic and copies ran while one was open for 0% of the time, Pallas kernels for 0%

profile of v1, /device:TPU:1, one launch (start us, length us, event | category | flops | bytes accessed | tf_op | source)
XLA Modules:
  0.0 113.7 jit_solution(9019095623797610451)
XLA Ops:
  0.6 0.1 pad_add_fusion.where_ref
  0.7 0.0 copy-start
  0.7 0.9 copy-done
  1.6 0.0 copy-start.1
  1.6 0.9 copy-done.1
  2.5 0.0 copy-start.2
  2.5 0.9 copy-done.2
  3.4 0.0 copy-start.3
  3.4 0.9 copy-done.3
  4.3 0.7 shard_map.75
  5.0 8.8 %collective-permute-start = (bf16[128,768]{1,0:T(8,128)(2,1)S(1)}, bf16[128,768]{1,0:T(8,128)(2,1)S(1)}, u32[]{:S(2)}, u32[]{:S(2)}) collective-permute-start(bf16[128,768]{1,0:T(8,128)(2,1)S(1)} %get-tuple-element.18), channel_id=1, source_target_pairs={{0,1},{1,0},{2,3},{3,2},{4,5},{5,4},{6,7},{7,6},{8,9},{9,8},{10,11... | collective-permute-start | bytes 589832 | tf_op jit(solution)/shard_map/ppermute | solution.py:18
  13.8 1.0 collective-permute-done.recv_ref
  14.9 0.8 shard_map.76
  15.8 1.9 %collective-permute-start.1 = (bf16[256,384]{1,0:T(8,128)(2,1)S(1)}, bf16[256,384]{1,0:T(8,128)(2,1)S(1)}, u32[]{:S(2)}, u32[]{:S(2)}) collective-permute-start(bf16[256,384]{1,0:T(8,128)(2,1)S(1)} %get-tuple-element.20), channel_id=1, source_target_pairs={{0,2},{1,3},{2,0},{3,1},{4,6},{5,7},{6,4},{7,5},{8,10},{9,11},{10,... | collective-permute-start | bytes 589832 | tf_op jit(solution)/shard_map/ppermute | solution.py:18
  17.7 6.0 %collective-permute-done.1 = bf16[256,384]{1,0:T(8,128)(2,1)S(1)} collective-permute-done((bf16[256,384]{1,0:T(8,128)(2,1)S(1)}, bf16[256,384]{1,0:T(8,128)(2,1)S(1)}, u32[]{:S(2)}, u32[]{:S(2)}) %collective-permute-start.1) | collective-permute-done | bytes 196640 | tf_op jit(solution)/shard_map/ppermute | solution.py:18
  24.0 1.9 %collective-permute-start.2 = (bf16[256,256]{1,0:T(8,128)(2,1)S(1)}, bf16[256,256]{1,0:T(8,128)(2,1)S(1)}, u32[]{:S(2)}, u32[]{:S(2)}) collective-permute-start(bf16[256,256]{1,0:T(8,128)(2,1)S(1)} %get-tuple-element.56), channel_id=1, source_target_pairs={{0,4},{1,5},{2,6},{3,7},{4,0},{5,1},{6,2},{7,3},{8,12},{9,13},{10,... | collective-permute-start | bytes 393224 | tf_op jit(solution)/shard_map/ppermute | solution.py:18
  26.0 9.0 %collective-permute-done.2.r1_ref = bf16[256,256]{1,0:T(8,128)(2,1)S(1)} collective-permute-done((bf16[256,256]{1,0:T(8,128)(2,1)S(1)}, bf16[256,256]{1,0:T(8,128)(2,1)S(1)}, u32[]{:S(2)}, u32[]{:S(2)}) %collective-permute-start.2) | collective-permute-done | bytes 131104 | tf_op jit(solution)/shard_map/ppermute | solution.py:18
  35.0 1.9 %collective-permute-start.3 = (bf16[256,256]{1,0:T(8,128)(2,1)S(1)}, bf16[256,256]{1,0:T(8,128)(2,1)S(1)}, u32[]{:S(2)}, u32[]{:S(2)}) collective-permute-start(bf16[256,256]{1,0:T(8,128)(2,1)S(1)} %constant_dynamic-update-slice_fusion.28), channel_id=1, source_target_pairs={{0,12},{1,13},{2,14},{3,15},{4,8},{5,9},{6,10},{7,11},{8,4},{9,5},... | collective-permute-start | bytes 393224 | tf_op jit(solution)/shard_map/ppermute | solution.py:18
  36.9 6.6 %collective-permute-done.3.r2_ref = bf16[256,256]{1,0:T(8,128)(2,1)S(1)} collective-permute-done((bf16[256,256]{1,0:T(8,128)(2,1)S(1)}, bf16[256,256]{1,0:T(8,128)(2,1)S(1)}, u32[]{:S(2)}, u32[]{:S(2)}) %collective-permute-start.3) | collective-permute-done | bytes 131104 | tf_op jit(solution)/shard_map/ppermute | solution.py:18
  43.5 1.9 %collective-permute-start.4 = (bf16[256,256]{1,0:T(8,128)(2,1)S(1)}, bf16[256,256]{1,0:T(8,128)(2,1)S(1)}, u32[]{:S(2)}, u32[]{:S(2)}) collective-permute-start(bf16[256,256]{1,0:T(8,128)(2,1)S(1)} %constant_dynamic-update-slice_fusion.35), channel_id=1, source_target_pairs={{0,16},{1,17},{2,18},{3,19},{4,20},{5,21},{6,22},{7,23},{8,24},{9,... | collective-permute-start | bytes 393224 | tf_op jit(solution)/shard_map/ppermute | solution.py:18
  45.5 3.8 %collective-permute-done.4.r3_ref = bf16[256,256]{1,0:T(8,128)(2,1)S(1)} collective-permute-done((bf16[256,256]{1,0:T(8,128)(2,1)S(1)}, bf16[256,256]{1,0:T(8,128)(2,1)S(1)}, u32[]{:S(2)}, u32[]{:S(2)}) %collective-permute-start.4) | collective-permute-done | bytes 131104 | tf_op jit(solution)/shard_map/ppermute | solution.py:18
  49.3 2.3 %collective-permute-start.5 = (bf16[256,256]{1,0:T(8,128)(2,1)S(1)}, bf16[256,256]{1,0:T(8,128)(2,1)S(1)}, u32[]{:S(2)}, u32[]{:S(2)}) collective-permute-start(bf16[256,256]{1,0:T(8,128)(2,1)S(1)} %constant_dynamic-update-slice_fusion.42), channel_id=1, source_target_pairs={{0,32},{1,33},{2,34},{3,35},{4,36},{5,37},{6,38},{7,39},{8,40},{9,... | collective-permute-start | bytes 393224 | tf_op jit(solution)/shard_map/ppermute | solution.py:18
  51.6 5.5 %collective-permute-done.5.r4_ref = bf16[256,256]{1,0:T(8,128)(2,1)S(1)} collective-permute-done((bf16[256,256]{1,0:T(8,128)(2,1)S(1)}, bf16[256,256]{1,0:T(8,128)(2,1)S(1)}, u32[]{:S(2)}, u32[]{:S(2)}) %collective-permute-start.5) | collective-permute-done | bytes 131104 | tf_op jit(solution)/shard_map/ppermute | solution.py:18
  57.0 3.9 %shard_map.77 = (f32[512,128]{1,0:T(8,128)S(1)}, f32[256,128]{1,0:T(8,128)S(1)}, f32[512,256]{1,0:T(8,128)S(1)}, f32[256,256]{1,0:T(8,128)S(1)}, f32[256,256]{1,...) custom-call(bf16[512,128]{1,0:T(8,128)(2,1)S(1)} %constant_dynamic-update-slice_fusion.qga_ref, ...), custom_call_target="tpu_custom_call" | custom-call | flops 600000000 | bytes 983040 | tf_op jit(solution)/shard_map/pallas_call | solution.py:223
  61.0 1.9 %collective-permute-start.6 = (bf16[256,256]{1,0:T(8,128)(2,1)S(1)}, bf16[256,256]{1,0:T(8,128)(2,1)S(1)}, u32[]{:S(2)}, u32[]{:S(2)}) collective-permute-start(bf16[256,256]{1,0:T(8,128)(2,1)S(1)} %get-tuple-element.23), channel_id=1, source_target_pairs={{0,32},{1,33},{2,34},{3,35},{4,36},{5,37},{6,38},{7,39},{8,40},{9,... | collective-permute-start | bytes 393224 | tf_op jit(solution)/shard_map/ppermute | solution.py:18
  62.9 6.1 %collective-permute-done.6 = bf16[256,256]{1,0:T(8,128)(2,1)S(1)} collective-permute-done((bf16[256,256]{1,0:T(8,128)(2,1)S(1)}, bf16[256,256]{1,0:T(8,128)(2,1)S(1)}, u32[]{:S(2)}, u32[]{:S(2)}) %collective-permute-start.6) | collective-permute-done | bytes 131104 | tf_op jit(solution)/shard_map/ppermute | solution.py:18
  69.1 1.9 %collective-permute-start.7 = (bf16[256,256]{1,0:T(8,128)(2,1)S(1)}, bf16[256,256]{1,0:T(8,128)(2,1)S(1)}, u32[]{:S(2)}, u32[]{:S(2)}) collective-permute-start(bf16[256,256]{1,0:T(8,128)(2,1)S(1)} %convert_element_type.23), channel_id=1, source_target_pairs={{0,16},{1,17},{2,18},{3,19},{4,20},{5,21},{6,22},{7,23},{8,24},{9,... | collective-permute-start | bytes 393224 | tf_op jit(solution)/shard_map/ppermute | solution.py:18
  71.1 3.8 %collective-permute-done.7 = bf16[256,256]{1,0:T(8,128)(2,1)S(1)} collective-permute-done((bf16[256,256]{1,0:T(8,128)(2,1)S(1)}, bf16[256,256]{1,0:T(8,128)(2,1)S(1)}, u32[]{:S(2)}, u32[]{:S(2)}) %collective-permute-start.7) | collective-permute-done | bytes 131104 | tf_op jit(solution)/shard_map/ppermute | solution.py:18
  75.0 7.1 %collective-permute-start.8 = (bf16[256,256]{1,0:T(8,128)(2,1)S(1)}, bf16[256,256]{1,0:T(8,128)(2,1)S(1)}, u32[]{:S(2)}, u32[]{:S(2)}) collective-permute-start(bf16[256,256]{1,0:T(8,128)(2,1)S(1)} %convert_element_type.25), channel_id=1, source_target_pairs={{0,12},{1,13},{2,14},{3,15},{4,8},{5,9},{6,10},{7,11},{8,4},{9,5},... | collective-permute-start | bytes 393224 | tf_op jit(solution)/shard_map/ppermute | solution.py:18
  82.1 2.3 %collective-permute-done.8 = bf16[256,256]{1,0:T(8,128)(2,1)S(1)} collective-permute-done((bf16[256,256]{1,0:T(8,128)(2,1)S(1)}, bf16[256,256]{1,0:T(8,128)(2,1)S(1)}, u32[]{:S(2)}, u32[]{:S(2)}) %collective-permute-start.8) | collective-permute-done | bytes 131104 | tf_op jit(solution)/shard_map/ppermute | solution.py:18
  84.4 0.1 fusion.1
  84.5 8.9 %collective-permute-start.9 = (bf16[256,256]{1,0:T(8,128)(2,1)S(1)}, bf16[256,256]{1,0:T(8,128)(2,1)S(1)}, u32[]{:S(2)}, u32[]{:S(2)}) collective-permute-start(bf16[256,256]{1,0:T(8,128)(2,1)S(1)} %convert_element_type.27), channel_id=1, source_target_pairs={{0,4},{1,5},{2,6},{3,7},{4,0},{5,1},{6,2},{7,3},{8,12},{9,13},{10,... | collective-permute-start | bytes 393224 | tf_op jit(solution)/shard_map/ppermute | solution.py:18
  93.4 2.5 %collective-permute-done.9 = bf16[256,256]{1,0:T(8,128)(2,1)S(1)} collective-permute-done((bf16[256,256]{1,0:T(8,128)(2,1)S(1)}, bf16[256,256]{1,0:T(8,128)(2,1)S(1)}, u32[]{:S(2)}, u32[]{:S(2)}) %collective-permute-start.9) | collective-permute-done | bytes 131104 | tf_op jit(solution)/shard_map/ppermute | solution.py:18
  96.0 1.9 %collective-permute-start.10 = (bf16[256,384]{1,0:T(8,128)(2,1)S(1)}, bf16[256,384]{1,0:T(8,128)(2,1)S(1)}, u32[]{:S(2)}, u32[]{:S(2)}) collective-permute-start(bf16[256,384]{1,0:T(8,128)(2,1)S(1)} %pad_maximum_fusion.1), channel_id=1, source_target_pairs={{0,2},{1,3},{2,0},{3,1},{4,6},{5,7},{6,4},{7,5},{8,10},{9,11},{10,... | collective-permute-start | bytes 589832 | tf_op jit(solution)/shard_map/ppermute | solution.py:18
  98.1 4.3 %collective-permute-done.10.recv_ref = bf16[256,384]{1,0:T(8,128)(2,1)S(1)} collective-permute-done((bf16[256,384]{1,0:T(8,128)(2,1)S(1)}, bf16[256,384]{1,0:T(8,128)(2,1)S(1)}, u32[]{:S(2)}, u32[]{:S(2)}) %collective-permute-start.10) | collective-permute-done | bytes 196640 | tf_op jit(solution)/shard_map/ppermute | solution.py:18
  102.4 0.9 shard_map.78
  103.3 8.0 %collective-permute-start.11 = (bf16[128,768]{1,0:T(8,128)(2,1)S(1)}, bf16[128,768]{1,0:T(8,128)(2,1)S(1)}, u32[]{:S(2)}, u32[]{:S(2)}) collective-permute-start(bf16[128,768]{1,0:T(8,128)(2,1)S(1)} %get-tuple-element.29), channel_id=1, source_target_pairs={{0,1},{1,0},{2,3},{3,2},{4,5},{5,4},{6,7},{7,6},{8,9},{9,8},{10,11... | collective-permute-start | bytes 589832 | tf_op jit(solution)/shard_map/ppermute | solution.py:18
  111.3 1.0 collective-permute-done.11.recv_ref
  112.3 1.4 %shard_map.79 = (bf16[128,384]{1,0:T(8,128)(2,1)}, bf16[128,384]{1,0:T(8,128)(2,1)}, bf16[128,384]{1,0:T(8,128)(2,1)}, bf16[128,384]{1,0:T(8,128)(2,1)}) custom-call(s32[2]{0:T(128)S(1)} %pad_add_fusion.where_ref, bf16[128,768]{1,0:T(8,128)(2,1)S(1)} %get-tuple-element.28.keep_ref, bf16[128,768]{1,0:T(8,128)(2,1)S(1)} %collective-permute-done.11.recv_ref), custom_call_target="tpu_custom_call" | custom-call | bytes 393224 | tf_op jit(solution)/shard_map/pallas_call | solution.py:223
  (76 shorter events, 0.8 us)
Async XLA Ops:
  0.7 0.9 copy-start
  1.6 0.9 copy-start.1
  2.5 0.9 copy-start.2
  3.4 0.9 copy-start.3
  5.0 9.8 %collective-permute-start = (bf16[128,768]{1,0:T(8,128)(2,1)S(1)}, bf16[128,768]{1,0:T(8,128)(2,1)S(1)}, u32[]{:S(2)}, u32[]{:S(2)}) collective-permute-start(bf16[128,768]{1,0:T(8,128)(2,1)S(1)} %get-tuple-element.18), channel_id=1, source_target_pairs={{0,1},{1,0},{2,3},{3,2},{4,5},{5,4},{6,7},{7,6},{8,9},{9,8},{10,11... | collective-permute-start | bytes 589832 | tf_op jit(solution)/shard_map/ppermute | solution.py:18
  15.8 8.0 %collective-permute-start.1 = (bf16[256,384]{1,0:T(8,128)(2,1)S(1)}, bf16[256,384]{1,0:T(8,128)(2,1)S(1)}, u32[]{:S(2)}, u32[]{:S(2)}) collective-permute-start(bf16[256,384]{1,0:T(8,128)(2,1)S(1)} %get-tuple-element.20), channel_id=1, source_target_pairs={{0,2},{1,3},{2,0},{3,1},{4,6},{5,7},{6,4},{7,5},{8,10},{9,11},{10,... | collective-permute-start | bytes 589832 | tf_op jit(solution)/shard_map/ppermute | solution.py:18
  24.0 11.0 %collective-permute-start.2 = (bf16[256,256]{1,0:T(8,128)(2,1)S(1)}, bf16[256,256]{1,0:T(8,128)(2,1)S(1)}, u32[]{:S(2)}, u32[]{:S(2)}) collective-permute-start(bf16[256,256]{1,0:T(8,128)(2,1)S(1)} %get-tuple-element.56), channel_id=1, source_target_pairs={{0,4},{1,5},{2,6},{3,7},{4,0},{5,1},{6,2},{7,3},{8,12},{9,13},{10,... | collective-permute-start | bytes 393224 | tf_op jit(solution)/shard_map/ppermute | solution.py:18
  35.0 8.5 %collective-permute-start.3 = (bf16[256,256]{1,0:T(8,128)(2,1)S(1)}, bf16[256,256]{1,0:T(8,128)(2,1)S(1)}, u32[]{:S(2)}, u32[]{:S(2)}) collective-permute-start(bf16[256,256]{1,0:T(8,128)(2,1)S(1)} %constant_dynamic-update-slice_fusion.28), channel_id=1, source_target_pairs={{0,12},{1,13},{2,14},{3,15},{4,8},{5,9},{6,10},{7,11},{8,4},{9,5},... | collective-permute-start | bytes 393224 | tf_op jit(solution)/shard_map/ppermute | solution.py:18
  43.5 5.7 %collective-permute-start.4 = (bf16[256,256]{1,0:T(8,128)(2,1)S(1)}, bf16[256,256]{1,0:T(8,128)(2,1)S(1)}, u32[]{:S(2)}, u32[]{:S(2)}) collective-permute-start(bf16[256,256]{1,0:T(8,128)(2,1)S(1)} %constant_dynamic-update-slice_fusion.35), channel_id=1, source_target_pairs={{0,16},{1,17},{2,18},{3,19},{4,20},{5,21},{6,22},{7,23},{8,24},{9,... | collective-permute-start | bytes 393224 | tf_op jit(solution)/shard_map/ppermute | solution.py:18
  49.3 7.8 %collective-permute-start.5 = (bf16[256,256]{1,0:T(8,128)(2,1)S(1)}, bf16[256,256]{1,0:T(8,128)(2,1)S(1)}, u32[]{:S(2)}, u32[]{:S(2)}) collective-permute-start(bf16[256,256]{1,0:T(8,128)(2,1)S(1)} %constant_dynamic-update-slice_fusion.42), channel_id=1, source_target_pairs={{0,32},{1,33},{2,34},{3,35},{4,36},{5,37},{6,38},{7,39},{8,40},{9,... | collective-permute-start | bytes 393224 | tf_op jit(solution)/shard_map/ppermute | solution.py:18
  61.0 8.0 %collective-permute-start.6 = (bf16[256,256]{1,0:T(8,128)(2,1)S(1)}, bf16[256,256]{1,0:T(8,128)(2,1)S(1)}, u32[]{:S(2)}, u32[]{:S(2)}) collective-permute-start(bf16[256,256]{1,0:T(8,128)(2,1)S(1)} %get-tuple-element.23), channel_id=1, source_target_pairs={{0,32},{1,33},{2,34},{3,35},{4,36},{5,37},{6,38},{7,39},{8,40},{9,... | collective-permute-start | bytes 393224 | tf_op jit(solution)/shard_map/ppermute | solution.py:18
  69.1 5.7 %collective-permute-start.7 = (bf16[256,256]{1,0:T(8,128)(2,1)S(1)}, bf16[256,256]{1,0:T(8,128)(2,1)S(1)}, u32[]{:S(2)}, u32[]{:S(2)}) collective-permute-start(bf16[256,256]{1,0:T(8,128)(2,1)S(1)} %convert_element_type.23), channel_id=1, source_target_pairs={{0,16},{1,17},{2,18},{3,19},{4,20},{5,21},{6,22},{7,23},{8,24},{9,... | collective-permute-start | bytes 393224 | tf_op jit(solution)/shard_map/ppermute | solution.py:18
  75.0 9.4 %collective-permute-start.8 = (bf16[256,256]{1,0:T(8,128)(2,1)S(1)}, bf16[256,256]{1,0:T(8,128)(2,1)S(1)}, u32[]{:S(2)}, u32[]{:S(2)}) collective-permute-start(bf16[256,256]{1,0:T(8,128)(2,1)S(1)} %convert_element_type.25), channel_id=1, source_target_pairs={{0,12},{1,13},{2,14},{3,15},{4,8},{5,9},{6,10},{7,11},{8,4},{9,5},... | collective-permute-start | bytes 393224 | tf_op jit(solution)/shard_map/ppermute | solution.py:18
  84.5 11.4 %collective-permute-start.9 = (bf16[256,256]{1,0:T(8,128)(2,1)S(1)}, bf16[256,256]{1,0:T(8,128)(2,1)S(1)}, u32[]{:S(2)}, u32[]{:S(2)}) collective-permute-start(bf16[256,256]{1,0:T(8,128)(2,1)S(1)} %convert_element_type.27), channel_id=1, source_target_pairs={{0,4},{1,5},{2,6},{3,7},{4,0},{5,1},{6,2},{7,3},{8,12},{9,13},{10,... | collective-permute-start | bytes 393224 | tf_op jit(solution)/shard_map/ppermute | solution.py:18
  96.0 6.4 %collective-permute-start.10 = (bf16[256,384]{1,0:T(8,128)(2,1)S(1)}, bf16[256,384]{1,0:T(8,128)(2,1)S(1)}, u32[]{:S(2)}, u32[]{:S(2)}) collective-permute-start(bf16[256,384]{1,0:T(8,128)(2,1)S(1)} %pad_maximum_fusion.1), channel_id=1, source_target_pairs={{0,2},{1,3},{2,0},{3,1},{4,6},{5,7},{6,4},{7,5},{8,10},{9,11},{10,... | collective-permute-start | bytes 589832 | tf_op jit(solution)/shard_map/ppermute | solution.py:18
  103.3 9.0 %collective-permute-start.11 = (bf16[128,768]{1,0:T(8,128)(2,1)S(1)}, bf16[128,768]{1,0:T(8,128)(2,1)S(1)}, u32[]{:S(2)}, u32[]{:S(2)}) collective-permute-start(bf16[128,768]{1,0:T(8,128)(2,1)S(1)} %get-tuple-element.29), channel_id=1, source_target_pairs={{0,1},{1,0},{2,3},{3,2},{4,5},{5,4},{6,7},{7,6},{8,9},{9,8},{10,11... | collective-permute-start | bytes 589832 | tf_op jit(solution)/shard_map/ppermute | solution.py:18

commit v2 on v1

--- a/solution.py
+++ b/solution.py
@@ -13,9 +13,17 @@
 CORE, Y_ONE, Y_TWO, Y_SIX, Z_ONE, Z_TWO = 1, 2, 4, 12, 16, 32
 
 
+def gather_pair(block, flip):
+    count = lax.axis_size("seq")
+    pairs = [[i, i ^ flip] for i in range(count) if i < i ^ flip]
+    return lax.all_gather(block, "seq", axis_index_groups=pairs, axis=0, tiled=False)
+
+
 def swap_with(block, flip):
-    count = lax.axis_size("seq")
-    return lax.ppermute(block, "seq", [(i, i ^ flip) for i in range(count)])
+    both = gather_pair(block, flip)
+    high = 1 << (flip.bit_length() - 1)
+    first = (lax.axis_index("seq") & high) == 0
+    return jnp.where(first, both[1], both[0])
 
 
 def dot(a, b):
@@ -33,22 +41,6 @@
     return jnp.where(low, first, pltpu.roll(second, HD, 1))
 
 
-def split_heads(where_ref, q_ref, k_ref, v_ref, g_ref, send_ref, keep_ref):
-    core = where_ref[0]
-
-    def head(h):
-        tile = slice((h // 2) * 128, (h // 2) * 128 + 128)
-        q, k, v, g = (r[:, tile].astype(F32) for r in (q_ref, k_ref, v_ref, g_ref))
-        return pair_up(q, g, h % 2), pair_up(k, v, h % 2)
-
-    for s in range(3):
-        low, high = head(s), head(s + 3)
-        for part in range(2):
-            cols = slice(s * 256 + part * 128, s * 256 + part * 128 + 128)
-            keep_ref[:, cols] = jnp.where(core == 0, low[part], high[part]).astype(BF16)
-            send_ref[:, cols] = jnp.where(core == 0, high[part], low[part]).astype(BF16)
-
-
 def source_rows(shape, axis, head):
     i = lax.broadcasted_iota(jnp.int32, shape, axis)
     row = jnp.where(i < 64, 4 + 8 * (i - 32), jnp.where(i < 128, 2 + 4 * (i - 64), 1 + 2 * (i - 128)))
@@ -56,17 +48,23 @@
     return (row + head) & 255
 
 
-def sort_rows(where_ref, keep_ref, recv_ref, send_ref, own_ref):
+def sort_rows(where_ref, x_ref, send_ref, own_ref):
     core, odd = where_ref[0], where_ref[1]
-    keep, recv = keep_ref[...], recv_ref[...]
-    rows = jnp.concatenate(
-        [jnp.where(core == 0, keep, recv), jnp.where(core == 0, recv, keep)], 0
-    )
+
+    def tile(array, h):
+        cols = slice((h // 2) * 128, (h // 2) * 128 + 128)
+        return jnp.concatenate([x_ref[0, array, :, cols], x_ref[1, array, :, cols]], 0).astype(F32)
+
+    def head(h):
+        q, k, v, g = (tile(array, h) for array in range(4))
+        return jnp.concatenate([pair_up(q, g, h % 2), pair_up(k, v, h % 2)], 1)
+
     lane = lax.broadcasted_iota(jnp.int32, (256, 256), 1)
     slots = []
     for s in range(3):
+        rows = jnp.where(core == 0, head(s), head(s + 3)).astype(BF16)
         order = (lane == source_rows((256, 256), 0, 3 * core + s)).astype(BF16)
-        slots.append(dot(order, rows[:, s * 256 : s * 256 + 256]))
+        slots.append(dot(order, rows))
     send_ref[:, :256] = jnp.where(odd == 0, slots[2], slots[0]).astype(BF16)
     send_ref[:, 256:] = slots[1][:, 128:].astype(BF16)
     own_ref[:, :256] = jnp.where(odd == 0, slots[0], slots[2]).astype(BF16)
@@ -91,7 +89,7 @@
 
 def join_heads(where_ref, keep_ref, recv_ref, att_ref, dq_ref, dk_ref, dv_ref):
     core = where_ref[0]
-    keep, recv = keep_ref[...].astype(F32), recv_ref[...].astype(F32)
+    keep, recv = keep_ref[...].astype(F32), recv_ref[1 - core].astype(F32)
     low = jnp.where(core == 0, keep, recv)
     high = jnp.where(core == 0, recv, keep)
 
@@ -117,18 +115,13 @@
     return rank_of
 
 
-def key_rank(part, shape):
+def levels_shared(level, shape, step):
     i = lax.broadcasted_iota(jnp.int32, shape, 0)
-    if part == 2:
-        i = i & 127
-    elif part == 3:
-        i = i & 63
-    elif part == 4:
-        i = i & 31
-    rank_of = jnp.zeros(shape, F32)
-    for level in range(4):
-        rank_of = rank_of + (i < (32 << level)).astype(F32)
-    return rank_of
+    i = i & (511 >> level)
+    key = jnp.zeros(shape, F32)
+    for k in range(4):
+        key = key + (i < (32 << k)).astype(F32)
+    return jnp.maximum(jnp.minimum(key, rank(shape, 1, step)) + (1.0 - level), 0.0)
 
 
 def attend(qga_ref, qgb_ref, kv0_ref, r1_ref, r2_ref, r3_ref, r4_ref,
@@ -148,21 +141,20 @@
         g_t = jnp.where(sub, 0.0, turned)
         g_tb = g_t.astype(BF16)
         half = total // 2
-        pieces = [(0, 0, 256, 0, half, True), (0, 0, 256, half, half, False), (0, 256, 256, 0, total, False)]
-        for part in range(1, 5):
-            pieces.append((part, 0, 256, 0, max(128, total >> part), True))
+        pieces = [(0, 0, 256, 0, half, 0), (0, 0, 256, half, half, None), (0, 256, 256, 0, total, None)]
+        for part, row, rows, level in ((1, 0, 256, 1), (2, 0, 256, 2), (3, 0, 256, 3), (3, 256, 128, 4), (4, 0, 128, 4)):
+            pieces.append((part, row, rows, 0, max(128, total >> level), level))
         maxima = [jnp.full((1, 128), NEG, F32) for _ in range(total // 128)]
         place = 0
         places, counts = [], []
-        for part, row, rows, first, width, weighted in pieces:
+        for part, row, rows, first, width, level in pieces:
             keys = kv_refs[part][row : row + rows, cols]
             scores = dot(keys, q_t[:, first : first + width])
             count = None
-            if weighted:
-                count = jnp.minimum(key_rank(part, (rows, width)), rank((rows, width), 1, step)) + (1.0 - part)
-                if part > 0 and (total >> part) < width:
+            if level is not None:
+                count = levels_shared(level, (rows, width), step)
+                if total >> level < width:
                     scores = jnp.where(count > 0.0, scores, NEG)
-                count = jnp.maximum(count, 0.0)
             e_ref[place : place + rows, :width] = scores
             top = jnp.max(scores, axis=0, keepdims=True)
             for t in range(width // 128):
@@ -174,9 +166,9 @@
         peak = jnp.concatenate(maxima, 1)
         sums = [jnp.zeros((1, 128), F32) for _ in range(total // 128)]
         accs = [jnp.zeros((128, 128), F32) for _ in range(total // 128)]
-        for (part, row, rows, first, width, weighted), place, count in zip(pieces, places, counts):
+        for (part, row, rows, first, width, level), place, count in zip(pieces, places, counts):
             weights = jnp.exp(e_ref[place : place + rows, :width] - peak[:, first : first + width])
-            if weighted:
+            if level is not None:
                 weights = weights * count
             e_ref[place : place + rows, :width] = weights
             turned_keys = kv_refs[part][row : row + rows, cols].T
@@ -191,7 +183,7 @@
         delta = jnp.sum(g_t * attended, axis=0, keepdims=True)
         queries = [jnp.zeros((128, 128), F32) for _ in range(total // 128)]
         partial = {}
-        for (part, row, rows, first, width, weighted), place in zip(pieces, places):
+        for (part, row, rows, first, width, level), place in zip(pieces, places):
             span = slice(first, first + width)
             keys = kv_refs[part][row : row + rows, cols]
             probs = e_ref[place : place + rows, :width] * inverse[:, span]
@@ -209,7 +201,7 @@
                 queries[at] = queries[at] + d_query[:, t * 128 : t * 128 + 128]
         for (part, row), both in partial.items():
             ref = d_refs[part]
-            ref[row : row + 256, cols] = both.astype(ref.dtype)
+            ref[row : row + both.shape[0], cols] = both.astype(ref.dtype)
         out = jnp.where(sub, jnp.concatenate(queries, 1) * HD**-0.5, attended)
         out_ref[...] = out.T
 
@@ -249,56 +241,53 @@
     return jnp.concatenate(own, 0), jnp.concatenate(partner, 0)
 
 
-def head_rows(blocks, rows):
-    return jnp.concatenate([array[at : at + rows] for array, at in blocks], 0)
-
-
-def add_rows(arrays, blocks, rows, extra):
-    extra = extra.astype(F32)
-    for n, (name, at) in enumerate(blocks):
-        piece = extra[n * rows : n * rows + rows]
-        arrays[name] = lax.dynamic_update_slice_in_dim(
-            arrays[name], arrays[name][at : at + rows] + piece, at, 0
-        )
+def add_rows(arrays, blocks, extra):
+    extra, start = extra.astype(F32), 0
+    for n, at, size in blocks:
+        piece = arrays[n][at : at + size] + extra[start : start + size]
+        arrays[n] = lax.dynamic_update_slice_in_dim(arrays[n], piece, at, 0)
+        start += size
 
 
 def per_device(query, keys, values, grad_out):
     device = lax.axis_index("seq")
     place = jnp.stack([device & 1, (device >> 1) & 1]).astype(jnp.int32)
-    send, keep = call(split_heads, [((128, 768), BF16)] * 2, place, query, keys, values, grad_out)
-    send, own = call(sort_rows, [((256, 384), BF16), ((256, 512), BF16)], place, keep, swap_with(send, CORE))
+    chip_rows = gather_pair(jnp.stack([query, keys, values, grad_out]), CORE)
+    send, own = call(sort_rows, [((256, 384), BF16), ((256, 512), BF16)], place, chip_rows)
     other = swap_with(send, Y_ONE)
     qg_a = interleave(own[:, :128], other[:, :128])
     qg_b = own[:, 256:384]
     kv0 = interleave(
         jnp.concatenate([own[:, 128:256], own[:, 384:]], 1), other[:, 128:]
     )
-    b1 = [(0, 0)]
-    b2 = b1 + [(1, 0)]
-    b3 = b2 + [(2, 0), (2, 128)]
-    b4 = b3 + [(3, 0), (3, 64), (3, 128), (3, 192)]
-    steps = ((b1, 256, Y_TWO), (b2, 128, Y_SIX), (b3, 64, Z_ONE), (b4, 32, Z_TWO))
-    kv = [kv0]
-    for blocks, rows, flip in steps:
-        kv.append(swap_with(head_rows([(kv[n], at) for n, at in blocks], rows), flip))
+    b1 = [(0, 0, 256)]
+    b2 = [(0, 0, 128), (1, 0, 128)]
+    ring = [(0, 0), (1, 0), (2, 0), (2, 128)]
+    b4 = [(n, at, 32) for n, at in ring]
+    b3 = [(n, at, 64) for n, at in ring] + [(4, 0, 128)]
+    steps = ((1, b1, Y_TWO), (2, b2, Y_SIX), (4, b4, Z_TWO), (3, b3, Z_ONE))
+    kv = {0: kv0}
+    for part, blocks, flip in steps:
+        rows = jnp.concatenate([kv[n][at : at + size] for n, at, size in blocks], 0)
+        kv[part] = swap_with(rows, flip)
     out_a, out_b, *grads = call(
         attend,
         [((512, 128), F32), ((256, 128), F32), ((512, 256), F32)]
-        + [((256, 256), F32)] * 3 + [((256, 256), BF16)],
-        qg_a, qg_b, *kv,
+        + [((n, 256), F32) for n in (256, 256, 384, 128)],
+        qg_a, qg_b, *(kv[n] for n in range(5)),
         scalar=False,
         scratch=[pltpu.VMEM((7 * 256, 512), F32)],
         flops=int(6e8),
     )
-    for part, (blocks, rows, flip) in reversed(list(enumerate(steps, 1))):
-        add_rows(grads, blocks, rows, swap_with(grads[part].astype(BF16), flip))
+    for part, blocks, flip in reversed(steps):
+        add_rows(grads, blocks, swap_with(grads[part].astype(BF16), flip))
     own_a, other_a = separate(out_a)
     own_kv, other_kv = separate(grads[0])
     send = jnp.concatenate([other_a, other_kv], 1).astype(BF16)
     own = jnp.concatenate([own_a, own_kv[:, :128], out_b, own_kv[:, 128:]], 1)
     send, keep = call(unsort_rows, [((128, 768), BF16)] * 2, place, own, swap_with(send, Y_ONE))
     return tuple(
-        call(join_heads, [((128, 384), BF16)] * 4, place, keep, swap_with(send, CORE))
+        call(join_heads, [((128, 384), BF16)] * 4, place, keep, gather_pair(send, CORE))
     )
 
 

time: 114 us -> 95.6 us (0.84)
  blocking collectives: 0 us -> 84.6 us
  waiting for transfers between devices: 51.9 us -> 0 us
  starting transfers between devices: 48.4 us -> 0 us
  local copies, waits for them, and re-layouts: 3.94 us -> 0.37 us
  other arithmetic: 0.52 us -> 1.78 us
    all_gather x0 -> x12, blocking collectives: none -> 84.6 us  [gather_pair(): lax.all_gather(block, 'seq', axis_index_groups=pairs, axis=0, tiled=False)]
    ppermute x12 -> x0, waiting for transfers between devices: 51.9 us -> none  [swap_with(): return lax.ppermute(block, 'seq', [(i, i ^ flip) for i in range(count)])]
    ppermute x12 -> x0, starting transfers between devices: 48.4 us -> none  [swap_with(): return lax.ppermute(block, 'seq', [(i, i ^ flip) for i in range(count)])]
    unnamed x51 -> x38, local copies, waits for them, and re-layouts: 3.8 us -> 0.23 us
    pallas_call x5 -> x4, Pallas kernels: 7.73 us -> 7.44 us  [call(): pl.pallas_call(body, out_shape=[jax.ShapeDtypeStruct(s, d) for s, d in ou...]
  transfers between devices with their start and end apart: 12 -> 0, of which waited for: 12 -> 0; matrix products, arithmetic and copies ran while one was open for 0% -> 0% of each run, Pallas kernels for 0% -> 0%
where the time goes in v2:
time: 95.6 us; the launch traced here: 95.3 us
  blocking collectives  84.6 us (88%)
  Pallas kernels  7.44 us (8%)
  other arithmetic  1.78 us (2%)
  between operations  1.2 us (1%)
    all_gather x12, blocking collectives, gather_pair(): lax.all_gather(block, 'seq', axis_index_groups=pairs, axis=0, tiled=False)  84.6 us
    pallas_call x4, Pallas kernels, call(): pl.pallas_call(body, out_shape=[jax.ShapeDtypeStruct(s, d) for s, d in ou...  7.44 us

profile of v2, /device:TPU:1, one launch (start us, length us, event | category | flops | bytes accessed | tf_op | source)
XLA Modules:
  0.0 95.3 jit_solution(6420710418324673279)
XLA Ops:
  0.6 0.1 pad_add_fusion.where_ref
  0.7 1.1 %pad_maximum_fusion.1 = bf16[4,128,384]{2,1,0:T(8,128)(2,1)S(1)} fusion(bf16[1,128,384]{2,1,0:T(8,128)(2,1)} %bitcast.124, bf16[1,128,384]{2,1,0:T(8,128)(2,1)} %bitcast.125, bf16[1,128,384]{2,1,0:T(8,128)(2,1)} %bitcast.126, bf16[1,128,384]{2,1,0:T(8,128)(2,1)} %bitcast.127), kind=kLoop, calls=%fused_computation.1 | loop fusion | flops 589824 | bytes 786432 | tf_op jit(solution)/shard_map/stack | solution.py:255
  1.8 8.9 %all-gather = bf16[8,128,384]{2,1,0:T(8,128)(2,1)S(1)} all-gather(bf16[4,128,384]{2,1,0:T(8,128)(2,1)S(1)} %pad_maximum_fusion.1), channel_id=2, replica_groups={{0,1},{2,3},{4,5},{6,7},{8,9},{10,11},{12,13},{14,15},{16,17},{18,19},{..., dimensions={0}, use_global_device_ids=true | all-gather | bytes 1179648 | tf_op jit(solution)/shard_map/all_gather | solution.py:19
  10.7 1.1 %shard_map.75 = (bf16[256,384]{1,0:T(8,128)(2,1)S(1)}, bf16[256,512]{1,0:T(8,128)(2,1)S(1)}) custom-call(s32[2]{0:T(128)S(1)} %pad_add_fusion.where_ref, bf16[2,4,128,384]{3,2,1,0:T(8,128)(2,1)S(1)} %bitcast.121), custom_call_target="tpu_custom_call" | custom-call | bytes 786440 | tf_op jit(solution)/shard_map/pallas_call | solution.py:215
  11.8 6.8 %all-gather.1 = bf16[512,384]{1,0:T(8,128)(2,1)S(1)} all-gather(bf16[256,384]{1,0:T(8,128)(2,1)S(1)} %get-tuple-element.16), channel_id=3, replica_groups={{0,2},{1,3},{4,6},{5,7},{8,10},{9,11},{12,14},{13,15},{16,18},{17,19},{..., dimensions={0}, use_global_device_ids=true | all-gather | bytes 589824 | tf_op jit(solution)/shard_map/all_gather | solution.py:19
  19.0 9.8 %all-gather.2 = bf16[512,256]{1,0:T(8,128)(2,1)S(1)} all-gather(bf16[256,256]{1,0:T(8,128)(2,1)S(1)} %get-tuple-element.55), channel_id=4, replica_groups={{0,4},{1,5},{2,6},{3,7},{8,12},{9,13},{10,14},{11,15},{16,20},{17,21},{..., dimensions={0}, use_global_device_ids=true | all-gather | bytes 393216 | tf_op jit(solution)/shard_map/all_gather | solution.py:19
  28.8 7.3 %all-gather.3 = bf16[512,256]{1,0:T(8,128)(2,1)S(1)} all-gather(bf16[256,256]{1,0:T(8,128)(2,1)S(1)} %constant_dynamic-update-slice_fusion.28), channel_id=5, replica_groups={{0,12},{1,13},{2,14},{3,15},{4,8},{5,9},{6,10},{7,11},{16,28},{17,29},{..., dimensions={0}, use_global_device_ids=true | all-gather | bytes 393216 | tf_op jit(solution)/shard_map/all_gather | solution.py:19
  36.2 5.4 %all-gather.4 = bf16[256,256]{1,0:T(8,128)(2,1)S(1)} all-gather(bf16[128,256]{1,0:T(8,128)(2,1)S(1)} %constant_dynamic-update-slice_fusion.35), channel_id=6, replica_groups={{0,32},{1,33},{2,34},{3,35},{4,36},{5,37},{6,38},{7,39},{8,40},{9,41},{..., dimensions={0}, use_global_device_ids=true | all-gather | bytes 196608 | tf_op jit(solution)/shard_map/all_gather | solution.py:19
  41.7 5.2 %all-gather.5 = bf16[768,256]{1,0:T(8,128)(2,1)S(1)} all-gather(bf16[384,256]{1,0:T(8,128)(2,1)S(1)} %get-tuple-element.28), channel_id=7, replica_groups={{0,16},{1,17},{2,18},{3,19},{4,20},{5,21},{6,22},{7,23},{8,24},{9,25},{..., dimensions={0}, use_global_device_ids=true | all-gather | bytes 589824 | tf_op jit(solution)/shard_map/all_gather | solution.py:19
  46.9 4.1 %shard_map.76 = (f32[512,128]{1,0:T(8,128)S(1)}, f32[256,128]{1,0:T(8,128)S(1)}, f32[512,256]{1,0:T(8,128)S(1)}, f32[256,256]{1,0:T(8,128)S(1)}, f32[256,256]{1,...) custom-call(bf16[512,128]{1,0:T(8,128)(2,1)S(1)} %constant_dynamic-update-slice_fusion.qga_ref, ...), custom_call_target="tpu_custom_call" | custom-call | flops 600000000 | bytes 983040 | tf_op jit(solution)/shard_map/pallas_call | solution.py:215
  51.2 5.2 %all-gather.6 = bf16[768,256]{1,0:T(8,128)(2,1)S(1)} all-gather(bf16[384,256]{1,0:T(8,128)(2,1)S(1)} %convert_element_type.38), channel_id=8, replica_groups={{0,16},{1,17},{2,18},{3,19},{4,20},{5,21},{6,22},{7,23},{8,24},{9,25},{..., dimensions={0}, use_global_device_ids=true | all-gather | bytes 589824 | tf_op jit(solution)/shard_map/all_gather | solution.py:19
  56.5 5.4 %all-gather.7 = bf16[256,256]{1,0:T(8,128)(2,1)S(1)} all-gather(bf16[128,256]{1,0:T(8,128)(2,1)S(1)} %fusion.10), channel_id=9, replica_groups={{0,32},{1,33},{2,34},{3,35},{4,36},{5,37},{6,38},{7,39},{8,40},{9,41},{..., dimensions={0}, use_global_device_ids=true | all-gather | bytes 196608 | tf_op jit(solution)/shard_map/all_gather | solution.py:19
  62.0 6.6 %all-gather.8 = bf16[512,256]{1,0:T(8,128)(2,1)S(1)} all-gather(bf16[256,256]{1,0:T(8,128)(2,1)S(1)} %convert_element_type.42), channel_id=10, replica_groups={{0,12},{1,13},{2,14},{3,15},{4,8},{5,9},{6,10},{7,11},{16,28},{17,29},{..., dimensions={0}, use_global_device_ids=true | all-gather | bytes 393216 | tf_op jit(solution)/shard_map/all_gather | solution.py:19
  68.7 0.1 fusion.6
  68.7 9.5 %all-gather.9 = bf16[512,256]{1,0:T(8,128)(2,1)S(1)} all-gather(bf16[256,256]{1,0:T(8,128)(2,1)S(1)} %convert_element_type.44), channel_id=11, replica_groups={{0,4},{1,5},{2,6},{3,7},{8,12},{9,13},{10,14},{11,15},{16,20},{17,21},{..., dimensions={0}, use_global_device_ids=true | all-gather | bytes 393216 | tf_op jit(solution)/shard_map/all_gather | solution.py:19
  78.4 6.2 %all_gather.90 = bf16[2,256,384]{2,1,0:T(8,128)(2,1)S(1)} all-gather(bf16[1,256,384]{2,1,0:T(8,128)(2,1)S(1)} %pad_maximum_fusion.2), channel_id=1, replica_groups={{0,2},{1,3},{4,6},{5,7},{8,10},{9,11},{12,14},{13,15},{16,18},{17,19},{..., dimensions={0}, use_global_device_ids=true | all-gather | bytes 589824 | tf_op jit(solution)/shard_map/all_gather | solution.py:19
  84.8 0.9 shard_map.77
  85.6 8.3 %all-gather.10 = bf16[256,768]{1,0:T(8,128)(2,1)S(1)} all-gather(bf16[128,768]{1,0:T(8,128)(2,1)S(1)} %get-tuple-element.25), channel_id=12, replica_groups={{0,1},{2,3},{4,5},{6,7},{8,9},{10,11},{12,13},{14,15},{16,17},{18,19},{..., dimensions={0}, use_global_device_ids=true | all-gather | bytes 589824 | tf_op jit(solution)/shard_map/all_gather | solution.py:19
  93.9 1.4 %shard_map.78 = (bf16[128,384]{1,0:T(8,128)(2,1)}, bf16[128,384]{1,0:T(8,128)(2,1)}, bf16[128,384]{1,0:T(8,128)(2,1)}, bf16[128,384]{1,0:T(8,128)(2,1)}) custom-call(s32[2]{0:T(128)S(1)} %pad_add_fusion.where_ref, bf16[128,768]{1,0:T(8,128)(2,1)S(1)} %get-tuple-element.24.keep_ref, bf16[2,128,768]{2,1,0:T(8,128)(2,1)S(1)} %bitcast.122), custom_call_target="tpu_custom_call" | custom-call | bytes 589832 | tf_op jit(solution)/shard_map/pallas_call | solution.py:215
  (78 shorter events, 0.9 us)

commit v3 on v2

--- a/solution.py
+++ b/solution.py
@@ -10,7 +10,7 @@
 F32 = jnp.float32
 BF16 = jnp.bfloat16
 
-CORE, Y_ONE, Y_TWO, Y_SIX, Z_ONE, Z_TWO = 1, 2, 4, 12, 16, 32
+CORE, Y_ONE, Y_THREE, Y_SIX, Z_ONE, Z_TWO = 1, 2, 6, 12, 16, 32
 
 
 def gather_pair(block, flip):
@@ -107,103 +107,119 @@
             right_ref[:, tile] = jnp.where(mask, pltpu.roll(even, HD, 1), odd).astype(BF16)
 
 
+PIECES = ((0, 0, 256, 0), (0, 256, 256, None), (1, 0, 256, 1), (2, 0, 256, 2), (3, 0, 256, 3), (3, 256, 128, 4), (4, 0, 128, 4))
+STARTS = (0, 512, 768, 1024, 1408)
+
+
 def rank(shape, axis, step):
     i = lax.broadcasted_iota(jnp.int32, shape, axis)
-    rank_of = jnp.zeros(shape, F32)
-    for level in range(4):
-        rank_of = rank_of + (i < (step << level)).astype(F32)
-    return rank_of
-
-
-def levels_shared(level, shape, step):
-    i = lax.broadcasted_iota(jnp.int32, shape, 0)
-    i = i & (511 >> level)
-    key = jnp.zeros(shape, F32)
-    for k in range(4):
-        key = key + (i < (32 << k)).astype(F32)
-    return jnp.maximum(jnp.minimum(key, rank(shape, 1, step)) + (1.0 - level), 0.0)
+    return sum((i < (step << level)).astype(F32) for level in range(4))
+
+
+def key_ranks(level):
+    i = lax.broadcasted_iota(jnp.int32, (256, 128), 0) & (511 >> max(level, 1))
+    return sum((i < (32 << k)).astype(F32) for k in range(4))
 
 
 def attend(qga_ref, qgb_ref, kv0_ref, r1_ref, r2_ref, r3_ref, r4_ref,
-           outa_ref, outb_ref, d0_ref, d1_ref, d2_ref, d3_ref, d4_ref, e_ref):
+           outa_ref, outb_ref, d0_ref, d1_ref, d2_ref, d3_ref, d4_ref,
+           ea_ref, eb_ref, pa_ref, pb_ref, ta_ref, tb_ref):
     kv_refs = (kv0_ref, r1_ref, r2_ref, r3_ref, r4_ref)
     d_refs = (d0_ref, d1_ref, d2_ref, d3_ref, d4_ref)
     sub = lax.broadcasted_iota(jnp.int32, (128, 1), 0) < HD
-    for which, (qg_ref, out_ref) in enumerate(((qga_ref, outa_ref), (qgb_ref, outb_ref))):
-        cols = slice(which * 128, which * 128 + 128)
+    ranks = [key_ranks(level) for level in (1, 2, 3)]
+    heads = []
+    for which, (qg_ref, out_ref, e_ref, p_ref, t_ref) in enumerate(
+        ((qga_ref, outa_ref, ea_ref, pa_ref, ta_ref), (qgb_ref, outb_ref, eb_ref, pb_ref, tb_ref))
+    ):
         total = qg_ref.shape[0]
-        step = total // 16
         qg = qg_ref[...].astype(F32)
-        scaled = jnp.where(left_half(qg.shape), qg * HD**-0.5, qg)
-        qg_b = scaled.astype(BF16)
-        turned = scaled.T
-        q_t = jnp.where(sub, turned, 0.0).astype(BF16)
+        low = left_half(qg.shape)
+        turned = qg.T
         g_t = jnp.where(sub, 0.0, turned)
-        g_tb = g_t.astype(BF16)
-        half = total // 2
-        pieces = [(0, 0, 256, 0, half, 0), (0, 0, 256, half, half, None), (0, 256, 256, 0, total, None)]
-        for part, row, rows, level in ((1, 0, 256, 1), (2, 0, 256, 2), (3, 0, 256, 3), (3, 256, 128, 4), (4, 0, 128, 4)):
-            pieces.append((part, row, rows, 0, max(128, total >> level), level))
-        maxima = [jnp.full((1, 128), NEG, F32) for _ in range(total // 128)]
+        query_rank = rank((1, 128), 1, total // 16)
+        shared = [jnp.minimum(r, query_rank) for r in ranks]
+        head = dict(
+            total=total, out=out_ref, e=e_ref, p=p_ref, t=t_ref, g_t=g_t, g_tb=g_t.astype(BF16),
+            q_t=jnp.where(sub, turned * HD**-0.5, 0.0).astype(BF16),
+            q_b=jnp.where(low, qg * HD**-0.5, 0.0).astype(BF16),
+            g_b=jnp.where(low, 0.0, qg).astype(BF16),
+            cols=slice(which * 128, which * 128 + 128), pieces=[],
+        )
         place = 0
-        places, counts = [], []
-        for part, row, rows, first, width, level in pieces:
-            keys = kv_refs[part][row : row + rows, cols]
-            scores = dot(keys, q_t[:, first : first + width])
-            count = None
-            if level is not None:
-                count = levels_shared(level, (rows, width), step)
-                if total >> level < width:
-                    scores = jnp.where(count > 0.0, scores, NEG)
-            e_ref[place : place + rows, :width] = scores
+        for part, row, rows, level in PIECES:
+            width = max(128, total >> (level or 0))
+            counts = [None] * (width // 128)
+            if level is not None and level < 4:
+                counts[0] = shared[max(level, 1) - 1] + (1.0 - level)
+            if level == 0 and total == 512:
+                counts[1] = 2.0
+            valid = None
+            if level is not None and total >> level < 128:
+                valid = query_rank >= level
+            head["pieces"].append((part, row, rows, width, place, counts, valid))
+            place += rows
+        heads.append(head)
+
+    for head in heads:
+        head["top"] = [jnp.full((1, 128), NEG, F32) for _ in range(head["total"] // 128)]
+    for n in range(len(PIECES)):
+        for head in heads:
+            part, row, rows, width, place, counts, valid = head["pieces"][n]
+            keys = kv_refs[part][row : row + rows, head["cols"]]
+            start = STARTS[part] + row
+            head["t"][:, start : start + rows] = keys.T
+            scores = dot(keys, head["q_t"][:, :width])
+            head["p"][place : place + rows, :width] = dot(keys, head["g_tb"][:, :width])
+            if valid is not None:
+                scores = jnp.where(valid, scores, NEG)
+            head["e"][place : place + rows, :width] = scores
             top = jnp.max(scores, axis=0, keepdims=True)
             for t in range(width // 128):
-                at = first // 128 + t
-                maxima[at] = jnp.maximum(maxima[at], top[:, t * 128 : t * 128 + 128])
-            places.append(place)
-            counts.append(count)
-            place += rows
-        peak = jnp.concatenate(maxima, 1)
-        sums = [jnp.zeros((1, 128), F32) for _ in range(total // 128)]
-        accs = [jnp.zeros((128, 128), F32) for _ in range(total // 128)]
-        for (part, row, rows, first, width, level), place, count in zip(pieces, places, counts):
-            weights = jnp.exp(e_ref[place : place + rows, :width] - peak[:, first : first + width])
-            if level is not None:
-                weights = weights * count
-            e_ref[place : place + rows, :width] = weights
-            turned_keys = kv_refs[part][row : row + rows, cols].T
-            acc = dot(turned_keys, weights.astype(BF16))
-            total_w = jnp.sum(weights, axis=0, keepdims=True)
+                head["top"][t] = jnp.maximum(head["top"][t], top[:, t * 128 : t * 128 + 128])
+
+    for head in heads:
+        tiles = head["total"] // 128
+        head["peak"] = jnp.concatenate(head["top"], 1)
+        head["sums"] = [jnp.zeros((1, 128), F32) for _ in range(tiles)]
+        head["accs"] = [jnp.zeros((128, 128), F32) for _ in range(tiles)]
+    for n in range(len(PIECES)):
+        for head in heads:
+            part, row, rows, width, place, counts, valid = head["pieces"][n]
+            weights = jnp.exp(head["e"][place : place + rows, :width] - head["peak"][:, :width])
+            if any(count is not None for count in counts):
+                cut = [weights[:, t * 128 : t * 128 + 128] for t in range(width // 128)]
+                cut = [w if c is None else w * c for w, c in zip(cut, counts)]
+                weights = jnp.concatenate(cut, 1)
+            head["e"][place : place + rows, :width] = weights
+            start = STARTS[part] + row
+            acc = dot(head["t"][:, start : start + rows], weights.astype(BF16))
+            added = jnp.sum(weights, axis=0, keepdims=True)
             for t in range(width // 128):
-                at = first // 128 + t
-                sums[at] = sums[at] + total_w[:, t * 128 : t * 128 + 128]
-                accs[at] = accs[at] + acc[:, t * 128 : t * 128 + 128]
-        inverse = 1.0 / jnp.concatenate(sums, 1)
-        attended = (jnp.concatenate(accs, 1) * inverse).astype(BF16).astype(F32)
-        delta = jnp.sum(g_t * attended, axis=0, keepdims=True)
-        queries = [jnp.zeros((128, 128), F32) for _ in range(total // 128)]
-        partial = {}
-        for (part, row, rows, first, width, level), place in zip(pieces, places):
-            span = slice(first, first + width)
-            keys = kv_refs[part][row : row + rows, cols]
-            probs = e_ref[place : place + rows, :width] * inverse[:, span]
-            grads = probs * (dot(keys, g_tb[:, span]) - delta[:, span])
-            grads_b = grads.astype(BF16)
-            d_keys = dot(grads_b, qg_b[span])
-            d_vals = dot(probs.astype(BF16), qg_b[span])
-            both = jnp.where(left_half(d_keys.shape), d_keys, d_vals)
-            if (part, row) in partial:
-                both = both + partial[part, row]
-            partial[part, row] = both
-            d_query = dot(keys.T, grads_b)
+                tile = slice(t * 128, t * 128 + 128)
+                head["sums"][t] = head["sums"][t] + added[:, tile]
+                head["accs"][t] = head["accs"][t] + acc[:, tile]
+
+    for head in heads:
+        head["inverse"] = 1.0 / jnp.concatenate(head["sums"], 1)
+        head["att"] = (jnp.concatenate(head["accs"], 1) * head["inverse"]).astype(BF16).astype(F32)
+        head["delta"] = jnp.sum(head["g_t"] * head["att"], axis=0, keepdims=True)
+        head["grads"] = [jnp.zeros((128, 128), F32) for _ in range(head["total"] // 128)]
+    for n in range(len(PIECES)):
+        for head in heads:
+            part, row, rows, width, place, counts, valid = head["pieces"][n]
+            probs = head["e"][place : place + rows, :width] * head["inverse"][:, :width]
+            grads = probs * (head["p"][place : place + rows, :width] - head["delta"][:, :width])
+            grads = grads.astype(BF16)
+            both = dot(grads, head["q_b"][:width]) + dot(probs.astype(BF16), head["g_b"][:width])
+            d_refs[part][row : row + rows, head["cols"]] = both
+            start = STARTS[part] + row
+            d_query = dot(head["t"][:, start : start + rows], grads)
             for t in range(width // 128):
-                at = first // 128 + t
-                queries[at] = queries[at] + d_query[:, t * 128 : t * 128 + 128]
-        for (part, row), both in partial.items():
-            ref = d_refs[part]
-            ref[row : row + both.shape[0], cols] = both.astype(ref.dtype)
-        out = jnp.where(sub, jnp.concatenate(queries, 1) * HD**-0.5, attended)
-        out_ref[...] = out.T
+                head["grads"][t] = head["grads"][t] + d_query[:, t * 128 : t * 128 + 128]
+    for head in heads:
+        out = jnp.where(sub, jnp.concatenate(head["grads"], 1) * HD**-0.5, head["att"])
+        head["out"][...] = out.T
 
 
 def call(body, outs, *args, scalar=True, scratch=(), flops=0):
@@ -251,7 +267,7 @@
 
 def per_device(query, keys, values, grad_out):
     device = lax.axis_index("seq")
-    place = jnp.stack([device & 1, (device >> 1) & 1]).astype(jnp.int32)
+    place = jnp.stack([device & 1, ((device >> 1) ^ (device >> 2) ^ (device >> 3)) & 1]).astype(jnp.int32)
     chip_rows = gather_pair(jnp.stack([query, keys, values, grad_out]), CORE)
     send, own = call(sort_rows, [((256, 384), BF16), ((256, 512), BF16)], place, chip_rows)
     other = swap_with(send, Y_ONE)
@@ -265,7 +281,7 @@
     ring = [(0, 0), (1, 0), (2, 0), (2, 128)]
     b4 = [(n, at, 32) for n, at in ring]
     b3 = [(n, at, 64) for n, at in ring] + [(4, 0, 128)]
-    steps = ((1, b1, Y_TWO), (2, b2, Y_SIX), (4, b4, Z_TWO), (3, b3, Z_ONE))
+    steps = ((1, b1, Y_THREE), (2, b2, Y_SIX), (4, b4, Z_TWO), (3, b3, Z_ONE))
     kv = {0: kv0}
     for part, blocks, flip in steps:
         rows = jnp.concatenate([kv[n][at : at + size] for n, at, size in blocks], 0)
@@ -276,7 +292,11 @@
         + [((n, 256), F32) for n in (256, 256, 384, 128)],
         qg_a, qg_b, *(kv[n] for n in range(5)),
         scalar=False,
-        scratch=[pltpu.VMEM((7 * 256, 512), F32)],
+        scratch=[
+            pltpu.VMEM((1536, 512), F32), pltpu.VMEM((1536, 256), F32),
+            pltpu.VMEM((1536, 512), F32), pltpu.VMEM((1536, 256), F32),
+            pltpu.VMEM((128, 1536), BF16), pltpu.VMEM((128, 1536), BF16),
+        ],
         flops=int(6e8),
     )
     for part, blocks, flip in reversed(steps):

time: 95.6 us -> 92.6 us (0.969)
  blocking collectives: 84.6 us -> 82.3 us
    all_gather x12, blocking collectives: 84.6 us -> 82.3 us  [gather_pair(): lax.all_gather(block, 'seq', axis_index_groups=pairs, axis=0, tiled=False)]
where the time goes in v3:
time: 92.6 us; the launch traced here: 92.4 us
  blocking collectives  82.3 us (89%)
  Pallas kernels  6.67 us (7%)
  other arithmetic  1.78 us (2%)
  between operations  1.2 us (1%)
    all_gather x12, blocking collectives, gather_pair(): lax.all_gather(block, 'seq', axis_index_groups=pairs, axis=0, tiled=False)  82.3 us
    pallas_call x4, Pallas kernels, call(): pl.pallas_call(body, out_shape=[jax.ShapeDtypeStruct(s, d) for s, d in ou...  6.67 us

profile of v3, /device:TPU:1, one launch (start us, length us, event | category | flops | bytes accessed | tf_op | source)
XLA Modules:
  0.0 92.4 jit_solution(17549302287569699307)
XLA Ops:
  0.7 0.1 pad_add_fusion.where_ref
  0.7 1.1 %pad_maximum_fusion.1 = bf16[4,128,384]{2,1,0:T(8,128)(2,1)S(1)} fusion(bf16[1,128,384]{2,1,0:T(8,128)(2,1)} %bitcast.124, bf16[1,128,384]{2,1,0:T(8,128)(2,1)} %bitcast.125, bf16[1,128,384]{2,1,0:T(8,128)(2,1)} %bitcast.126, bf16[1,128,384]{2,1,0:T(8,128)(2,1)} %bitcast.127), kind=kLoop, calls=%fused_computation.1 | loop fusion | flops 589824 | bytes 786432 | tf_op jit(solution)/shard_map/stack | solution.py:271
  1.8 8.9 %all-gather = bf16[8,128,384]{2,1,0:T(8,128)(2,1)S(1)} all-gather(bf16[4,128,384]{2,1,0:T(8,128)(2,1)S(1)} %pad_maximum_fusion.1), channel_id=2, replica_groups={{0,1},{2,3},{4,5},{6,7},{8,9},{10,11},{12,13},{14,15},{16,17},{18,19},{..., dimensions={0}, use_global_device_ids=true | all-gather | bytes 1179648 | tf_op jit(solution)/shard_map/all_gather | solution.py:19
  10.7 1.1 %shard_map.75 = (bf16[256,384]{1,0:T(8,128)(2,1)S(1)}, bf16[256,512]{1,0:T(8,128)(2,1)S(1)}) custom-call(s32[2]{0:T(128)S(1)} %pad_add_fusion.where_ref, bf16[2,4,128,384]{3,2,1,0:T(8,128)(2,1)S(1)} %bitcast.121), custom_call_target="tpu_custom_call" | custom-call | bytes 786440 | tf_op jit(solution)/shard_map/pallas_call | solution.py:231
  11.8 6.8 %all-gather.1 = bf16[512,384]{1,0:T(8,128)(2,1)S(1)} all-gather(bf16[256,384]{1,0:T(8,128)(2,1)S(1)} %get-tuple-element.16), channel_id=3, replica_groups={{0,2},{1,3},{4,6},{5,7},{8,10},{9,11},{12,14},{13,15},{16,18},{17,19},{..., dimensions={0}, use_global_device_ids=true | all-gather | bytes 589824 | tf_op jit(solution)/shard_map/all_gather | solution.py:19
  19.0 6.4 %all-gather.2 = bf16[512,256]{1,0:T(8,128)(2,1)S(1)} all-gather(bf16[256,256]{1,0:T(8,128)(2,1)S(1)} %get-tuple-element.55), channel_id=4, replica_groups={{0,6},{1,7},{2,4},{3,5},{8,14},{9,15},{10,12},{11,13},{16,22},{17,23},{..., dimensions={0}, use_global_device_ids=true | all-gather | bytes 393216 | tf_op jit(solution)/shard_map/all_gather | solution.py:19
  25.5 6.6 %all-gather.3 = bf16[512,256]{1,0:T(8,128)(2,1)S(1)} all-gather(bf16[256,256]{1,0:T(8,128)(2,1)S(1)} %constant_dynamic-update-slice_fusion.28), channel_id=5, replica_groups={{0,12},{1,13},{2,14},{3,15},{4,8},{5,9},{6,10},{7,11},{16,28},{17,29},{..., dimensions={0}, use_global_device_ids=true | all-gather | bytes 393216 | tf_op jit(solution)/shard_map/all_gather | solution.py:19
  32.2 5.3 %all-gather.4 = bf16[256,256]{1,0:T(8,128)(2,1)S(1)} all-gather(bf16[128,256]{1,0:T(8,128)(2,1)S(1)} %constant_dynamic-update-slice_fusion.35), channel_id=6, replica_groups={{0,32},{1,33},{2,34},{3,35},{4,36},{5,37},{6,38},{7,39},{8,40},{9,41},{..., dimensions={0}, use_global_device_ids=true | all-gather | bytes 196608 | tf_op jit(solution)/shard_map/all_gather | solution.py:19
  37.5 5.5 %all-gather.5 = bf16[768,256]{1,0:T(8,128)(2,1)S(1)} all-gather(bf16[384,256]{1,0:T(8,128)(2,1)S(1)} %get-tuple-element.28), channel_id=7, replica_groups={{0,16},{1,17},{2,18},{3,19},{4,20},{5,21},{6,22},{7,23},{8,24},{9,25},{..., dimensions={0}, use_global_device_ids=true | all-gather | bytes 589824 | tf_op jit(solution)/shard_map/all_gather | solution.py:19
  43.0 3.3 %shard_map.76 = (f32[512,128]{1,0:T(8,128)S(1)}, f32[256,128]{1,0:T(8,128)S(1)}, f32[512,256]{1,0:T(8,128)S(1)}, f32[256,256]{1,0:T(8,128)S(1)}, f32[256,256]{1,...) custom-call(bf16[512,128]{1,0:T(8,128)(2,1)S(1)} %constant_dynamic-update-slice_fusion.qga_ref, ...), custom_call_target="tpu_custom_call" | custom-call | flops 600000000 | bytes 983040 | tf_op jit(solution)/shard_map/pallas_call | solution.py:231
  46.5 5.2 %all-gather.6 = bf16[768,256]{1,0:T(8,128)(2,1)S(1)} all-gather(bf16[384,256]{1,0:T(8,128)(2,1)S(1)} %convert_element_type.38), channel_id=8, replica_groups={{0,16},{1,17},{2,18},{3,19},{4,20},{5,21},{6,22},{7,23},{8,24},{9,25},{..., dimensions={0}, use_global_device_ids=true | all-gather | bytes 589824 | tf_op jit(solution)/shard_map/all_gather | solution.py:19
  51.9 5.3 %all-gather.7 = bf16[256,256]{1,0:T(8,128)(2,1)S(1)} all-gather(bf16[128,256]{1,0:T(8,128)(2,1)S(1)} %fusion.10), channel_id=9, replica_groups={{0,32},{1,33},{2,34},{3,35},{4,36},{5,37},{6,38},{7,39},{8,40},{9,41},{..., dimensions={0}, use_global_device_ids=true | all-gather | bytes 196608 | tf_op jit(solution)/shard_map/all_gather | solution.py:19
  57.3 6.6 %all-gather.8 = bf16[512,256]{1,0:T(8,128)(2,1)S(1)} all-gather(bf16[256,256]{1,0:T(8,128)(2,1)S(1)} %convert_element_type.42), channel_id=10, replica_groups={{0,12},{1,13},{2,14},{3,15},{4,8},{5,9},{6,10},{7,11},{16,28},{17,29},{..., dimensions={0}, use_global_device_ids=true | all-gather | bytes 393216 | tf_op jit(solution)/shard_map/all_gather | solution.py:19
  63.9 0.1 fusion.6
  64.0 6.4 %all-gather.9 = bf16[512,256]{1,0:T(8,128)(2,1)S(1)} all-gather(bf16[256,256]{1,0:T(8,128)(2,1)S(1)} %convert_element_type.44), channel_id=11, replica_groups={{0,6},{1,7},{2,4},{3,5},{8,14},{9,15},{10,12},{11,13},{16,22},{17,23},{..., dimensions={0}, use_global_device_ids=true | all-gather | bytes 393216 | tf_op jit(solution)/shard_map/all_gather | solution.py:19
  70.5 5.8 %all_gather.90 = bf16[2,256,384]{2,1,0:T(8,128)(2,1)S(1)} all-gather(bf16[1,256,384]{2,1,0:T(8,128)(2,1)S(1)} %pad_maximum_fusion.2), channel_id=1, replica_groups={{0,2},{1,3},{4,6},{5,7},{8,10},{9,11},{12,14},{13,15},{16,18},{17,19},{..., dimensions={0}, use_global_device_ids=true | all-gather | bytes 589824 | tf_op jit(solution)/shard_map/all_gather | solution.py:19
  76.5 0.9 shard_map.77
  77.3 13.6 %all-gather.10 = bf16[256,768]{1,0:T(8,128)(2,1)S(1)} all-gather(bf16[128,768]{1,0:T(8,128)(2,1)S(1)} %get-tuple-element.25), channel_id=12, replica_groups={{0,1},{2,3},{4,5},{6,7},{8,9},{10,11},{12,13},{14,15},{16,17},{18,19},{..., dimensions={0}, use_global_device_ids=true | all-gather | bytes 589824 | tf_op jit(solution)/shard_map/all_gather | solution.py:19
  90.9 1.4 %shard_map.78 = (bf16[128,384]{1,0:T(8,128)(2,1)}, bf16[128,384]{1,0:T(8,128)(2,1)}, bf16[128,384]{1,0:T(8,128)(2,1)}, bf16[128,384]{1,0:T(8,128)(2,1)}) custom-call(s32[2]{0:T(128)S(1)} %pad_add_fusion.where_ref, bf16[128,768]{1,0:T(8,128)(2,1)S(1)} %get-tuple-element.24.keep_ref, bf16[2,128,768]{2,1,0:T(8,128)(2,1)S(1)} %bitcast.122), custom_call_target="tpu_custom_call" | custom-call | bytes 589832 | tf_op jit(solution)/shard_map/pallas_call | solution.py:231
  (78 shorter events, 0.9 us)

commit v4 on v3

--- a/solution.py
+++ b/solution.py
@@ -10,7 +10,7 @@
 F32 = jnp.float32
 BF16 = jnp.bfloat16
 
-CORE, Y_ONE, Y_THREE, Y_SIX, Z_ONE, Z_TWO = 1, 2, 6, 12, 16, 32
+CORE, Y_ONE, Y_THREE, Y_SEVEN, Z_ONE, Z_TWO = 1, 2, 6, 14, 16, 32
 
 
 def gather_pair(block, flip):
@@ -41,11 +41,10 @@
     return jnp.where(low, first, pltpu.roll(second, HD, 1))
 
 
-def source_rows(shape, axis, head):
+def source_rows(shape, axis):
     i = lax.broadcasted_iota(jnp.int32, shape, axis)
     row = jnp.where(i < 64, 4 + 8 * (i - 32), jnp.where(i < 128, 2 + 4 * (i - 64), 1 + 2 * (i - 128)))
-    row = jnp.where(i < 16, 16 * i, jnp.where(i < 32, 8 + 16 * (i - 16), row))
-    return (row + head) & 255
+    return jnp.where(i < 16, 16 * i, jnp.where(i < 32, 8 + 16 * (i - 16), row))
 
 
 def sort_rows(where_ref, x_ref, send_ref, own_ref):
@@ -59,11 +58,13 @@
         q, k, v, g = (tile(array, h) for array in range(4))
         return jnp.concatenate([pair_up(q, g, h % 2), pair_up(k, v, h % 2)], 1)
 
-    lane = lax.broadcasted_iota(jnp.int32, (256, 256), 1)
+    lane = lax.broadcasted_iota(jnp.int32, (256, 128), 1)
+    source = source_rows((256, 128), 0)
     slots = []
     for s in range(3):
         rows = jnp.where(core == 0, head(s), head(s + 3)).astype(BF16)
-        order = (lane == source_rows((256, 256), 0, 3 * core + s)).astype(BF16)
+        row = (source + (3 * core + s)) & 255
+        order = jnp.concatenate([lane == row, lane + 128 == row], 1).astype(BF16)
         slots.append(dot(order, rows))
     send_ref[:, :256] = jnp.where(odd == 0, slots[2], slots[0]).astype(BF16)
     send_ref[:, 256:] = slots[1][:, 128:].astype(BF16)
@@ -79,8 +80,9 @@
         [own_ref[:, 256:384], own_ref[:, 384:] + recv_ref[:, 256:].astype(F32)], 1
     ).astype(BF16)
     sub = lax.broadcasted_iota(jnp.int32, (256, 256), 0)
+    source = source_rows((1, 256), 1)
     for s, slot in enumerate((first, middle, third)):
-        order = (sub == source_rows((256, 256), 1, 3 * core + s)).astype(BF16)
+        order = (sub == ((source + (3 * core + s)) & 255)).astype(BF16)
         rows = dot(order, slot)
         cols = slice(s * 256, s * 256 + 256)
         keep_ref[:, cols] = jnp.where(core == 0, rows[:128], rows[128:]).astype(BF16)
@@ -107,8 +109,11 @@
             right_ref[:, tile] = jnp.where(mask, pltpu.roll(even, HD, 1), odd).astype(BF16)
 
 
-PIECES = ((0, 0, 256, 0), (0, 256, 256, None), (1, 0, 256, 1), (2, 0, 256, 2), (3, 0, 256, 3), (3, 256, 128, 4), (4, 0, 128, 4))
-STARTS = (0, 512, 768, 1024, 1408)
+PIECES = (
+    (0, 0, 256, 0), (0, 256, 256, None), (1, 0, 256, 1), (1, 256, 128, 2), (2, 0, 128, 2),
+    (3, 0, 256, 3), (3, 256, 128, 4), (4, 0, 128, 4),
+)
+STARTS = (0, 512, 896, 1024, 1408)
 
 
 def rank(shape, axis, step):
@@ -151,7 +156,7 @@
             width = max(128, total >> (level or 0))
             counts = [None] * (width // 128)
             if level is not None and level < 4:
-                counts[0] = shared[max(level, 1) - 1] + (1.0 - level)
+                counts[0] = shared[max(level, 1) - 1][:rows] + (1.0 - level)
             if level == 0 and total == 512:
                 counts[1] = 2.0
             valid = None
@@ -267,7 +272,7 @@
 
 def per_device(query, keys, values, grad_out):
     device = lax.axis_index("seq")
-    place = jnp.stack([device & 1, ((device >> 1) ^ (device >> 2) ^ (device >> 3)) & 1]).astype(jnp.int32)
+    place = jnp.stack([device & 1, ((device >> 1) ^ (device >> 2)) & 1]).astype(jnp.int32)
     chip_rows = gather_pair(jnp.stack([query, keys, values, grad_out]), CORE)
     send, own = call(sort_rows, [((256, 384), BF16), ((256, 512), BF16)], place, chip_rows)
     other = swap_with(send, Y_ONE)
@@ -276,12 +281,13 @@
     kv0 = interleave(
         jnp.concatenate([own[:, 128:256], own[:, 384:]], 1), other[:, 128:]
     )
-    b1 = [(0, 0, 256)]
-    b2 = [(0, 0, 128), (1, 0, 128)]
-    ring = [(0, 0), (1, 0), (2, 0), (2, 128)]
-    b4 = [(n, at, 32) for n, at in ring]
-    b3 = [(n, at, 64) for n, at in ring] + [(4, 0, 128)]
-    steps = ((1, b1, Y_THREE), (2, b2, Y_SIX), (4, b4, Z_TWO), (3, b3, Z_ONE))
+    ring = [(0, 0), (1, 0), (1, 256), (2, 0)]
+    steps = (
+        (2, [(0, 0, 128)], Y_SEVEN),
+        (1, [(0, 0, 256), (2, 0, 128)], Y_THREE),
+        (4, [(n, at, 32) for n, at in ring], Z_TWO),
+        (3, [(n, at, 64) for n, at in ring] + [(4, 0, 128)], Z_ONE),
+    )
     kv = {0: kv0}
     for part, blocks, flip in steps:
         rows = jnp.concatenate([kv[n][at : at + size] for n, at, size in blocks], 0)
@@ -289,7 +295,7 @@
     out_a, out_b, *grads = call(
         attend,
         [((512, 128), F32), ((256, 128), F32), ((512, 256), F32)]
-        + [((n, 256), F32) for n in (256, 256, 384, 128)],
+        + [((n, 256), F32) for n in (384, 128, 384, 128)],
         qg_a, qg_b, *(kv[n] for n in range(5)),
         scalar=False,
         scratch=[

time: 92.6 us -> 92.1 us (level)
  no operation moved by 1% of the time
where the time goes in v4:
time: 92.1 us; the launch traced here: 91.8 us
  blocking collectives  81.8 us (89%)
  Pallas kernels  6.71 us (7%)
  other arithmetic  1.75 us (2%)
  between operations  1.18 us (1%)
    all_gather x12, blocking collectives, gather_pair(): lax.all_gather(block, 'seq', axis_index_groups=pairs, axis=0, tiled=False)  81.8 us
    pallas_call x4, Pallas kernels, call(): pl.pallas_call(body, out_shape=[jax.ShapeDtypeStruct(s, d) for s, d in ou...  6.71 us

profile of v4, /device:TPU:1, one launch (start us, length us, event | category | flops | bytes accessed | tf_op | source)
XLA Modules:
  0.0 91.8 jit_solution(18071110734549403529)
XLA Ops:
  0.6 0.1 pad_add_fusion.where_ref
  0.7 1.1 %pad_maximum_fusion.1 = bf16[4,128,384]{2,1,0:T(8,128)(2,1)S(1)} fusion(bf16[1,128,384]{2,1,0:T(8,128)(2,1)} %bitcast.119, bf16[1,128,384]{2,1,0:T(8,128)(2,1)} %bitcast.120, bf16[1,128,384]{2,1,0:T(8,128)(2,1)} %bitcast.121, bf16[1,128,384]{2,1,0:T(8,128)(2,1)} %bitcast.122), kind=kLoop, calls=%fused_computation.1 | loop fusion | flops 589824 | bytes 786432 | tf_op jit(solution)/shard_map/stack | solution.py:276
  1.8 8.9 %all-gather = bf16[8,128,384]{2,1,0:T(8,128)(2,1)S(1)} all-gather(bf16[4,128,384]{2,1,0:T(8,128)(2,1)S(1)} %pad_maximum_fusion.1), channel_id=2, replica_groups={{0,1},{2,3},{4,5},{6,7},{8,9},{10,11},{12,13},{14,15},{16,17},{18,19},{..., dimensions={0}, use_global_device_ids=true | all-gather | bytes 1179648 | tf_op jit(solution)/shard_map/all_gather | solution.py:19
  10.7 1.1 %shard_map.75 = (bf16[256,384]{1,0:T(8,128)(2,1)S(1)}, bf16[256,512]{1,0:T(8,128)(2,1)S(1)}) custom-call(s32[2]{0:T(128)S(1)} %pad_add_fusion.where_ref, bf16[2,4,128,384]{3,2,1,0:T(8,128)(2,1)S(1)} %bitcast.114), custom_call_target="tpu_custom_call" | custom-call | bytes 786440 | tf_op jit(solution)/shard_map/pallas_call | solution.py:236
  11.8 6.8 %all-gather.1 = bf16[512,384]{1,0:T(8,128)(2,1)S(1)} all-gather(bf16[256,384]{1,0:T(8,128)(2,1)S(1)} %get-tuple-element.16), channel_id=3, replica_groups={{0,2},{1,3},{4,6},{5,7},{8,10},{9,11},{12,14},{13,15},{16,18},{17,19},{..., dimensions={0}, use_global_device_ids=true | all-gather | bytes 589824 | tf_op jit(solution)/shard_map/all_gather | solution.py:19
  18.9 5.0 %all-gather.2 = bf16[256,256]{1,0:T(8,128)(2,1)S(1)} all-gather(bf16[128,256]{1,0:T(8,128)(2,1)S(1)} %get-tuple-element.48), channel_id=4, replica_groups={{0,14},{1,15},{2,12},{3,13},{4,10},{5,11},{6,8},{7,9},{16,30},{17,31},{..., dimensions={0}, use_global_device_ids=true | all-gather | bytes 196608 | tf_op jit(solution)/shard_map/all_gather | solution.py:19
  24.0 7.1 %all-gather.3 = bf16[768,256]{1,0:T(8,128)(2,1)S(1)} all-gather(bf16[384,256]{1,0:T(8,128)(2,1)S(1)} %get-tuple-element.30), channel_id=5, replica_groups={{0,6},{1,7},{2,4},{3,5},{8,14},{9,15},{10,12},{11,13},{16,22},{17,23},{..., dimensions={0}, use_global_device_ids=true | all-gather | bytes 589824 | tf_op jit(solution)/shard_map/all_gather | solution.py:19
  31.3 4.7 %all-gather.4 = bf16[256,256]{1,0:T(8,128)(2,1)S(1)} all-gather(bf16[128,256]{1,0:T(8,128)(2,1)S(1)} %constant_dynamic-update-slice_fusion.35), channel_id=6, replica_groups={{0,32},{1,33},{2,34},{3,35},{4,36},{5,37},{6,38},{7,39},{8,40},{9,41},{..., dimensions={0}, use_global_device_ids=true | all-gather | bytes 196608 | tf_op jit(solution)/shard_map/all_gather | solution.py:19
  36.0 5.9 %all-gather.5 = bf16[768,256]{1,0:T(8,128)(2,1)S(1)} all-gather(bf16[384,256]{1,0:T(8,128)(2,1)S(1)} %get-tuple-element.28), channel_id=7, replica_groups={{0,16},{1,17},{2,18},{3,19},{4,20},{5,21},{6,22},{7,23},{8,24},{9,25},{..., dimensions={0}, use_global_device_ids=true | all-gather | bytes 589824 | tf_op jit(solution)/shard_map/all_gather | solution.py:19
  41.9 3.4 %shard_map.76 = (f32[512,128]{1,0:T(8,128)S(1)}, f32[256,128]{1,0:T(8,128)S(1)}, f32[512,256]{1,0:T(8,128)S(1)}, f32[384,256]{1,0:T(8,128)S(1)}, f32[128,256]{1,...) custom-call(bf16[512,128]{1,0:T(8,128)(2,1)S(1)} %constant_dynamic-update-slice_fusion.qga_ref, ...), custom_call_target="tpu_custom_call" | custom-call | flops 600000000 | bytes 983040 | tf_op jit(solution)/shard_map/pallas_call | solution.py:236
  45.5 5.2 %all-gather.6 = bf16[768,256]{1,0:T(8,128)(2,1)S(1)} all-gather(bf16[384,256]{1,0:T(8,128)(2,1)S(1)} %convert_element_type.38), channel_id=8, replica_groups={{0,16},{1,17},{2,18},{3,19},{4,20},{5,21},{6,22},{7,23},{8,24},{9,25},{..., dimensions={0}, use_global_device_ids=true | all-gather | bytes 589824 | tf_op jit(solution)/shard_map/all_gather | solution.py:19
  50.8 5.3 %all-gather.7 = bf16[256,256]{1,0:T(8,128)(2,1)S(1)} all-gather(bf16[128,256]{1,0:T(8,128)(2,1)S(1)} %fusion.9), channel_id=9, replica_groups={{0,32},{1,33},{2,34},{3,35},{4,36},{5,37},{6,38},{7,39},{8,40},{9,41},{..., dimensions={0}, use_global_device_ids=true | all-gather | bytes 196608 | tf_op jit(solution)/shard_map/all_gather | solution.py:19
  56.2 7.0 %all-gather.8 = bf16[768,256]{1,0:T(8,128)(2,1)S(1)} all-gather(bf16[384,256]{1,0:T(8,128)(2,1)S(1)} %convert_element_type.42), channel_id=10, replica_groups={{0,6},{1,7},{2,4},{3,5},{8,14},{9,15},{10,12},{11,13},{16,22},{17,23},{..., dimensions={0}, use_global_device_ids=true | all-gather | bytes 589824 | tf_op jit(solution)/shard_map/all_gather | solution.py:19
  63.3 5.0 %all-gather.9 = bf16[256,256]{1,0:T(8,128)(2,1)S(1)} all-gather(bf16[128,256]{1,0:T(8,128)(2,1)S(1)} %fusion.7), channel_id=11, replica_groups={{0,14},{1,15},{2,12},{3,13},{4,10},{5,11},{6,8},{7,9},{16,30},{17,31},{..., dimensions={0}, use_global_device_ids=true | all-gather | bytes 196608 | tf_op jit(solution)/shard_map/all_gather | solution.py:19
  68.5 13.3 %all_gather.90 = bf16[2,256,384]{2,1,0:T(8,128)(2,1)S(1)} all-gather(bf16[1,256,384]{2,1,0:T(8,128)(2,1)S(1)} %pad_maximum_fusion.2), channel_id=1, replica_groups={{0,2},{1,3},{4,6},{5,7},{8,10},{9,11},{12,14},{13,15},{16,18},{17,19},{..., dimensions={0}, use_global_device_ids=true | all-gather | bytes 589824 | tf_op jit(solution)/shard_map/all_gather | solution.py:19
  81.9 0.9 shard_map.77
  82.8 7.6 %all-gather.10 = bf16[256,768]{1,0:T(8,128)(2,1)S(1)} all-gather(bf16[128,768]{1,0:T(8,128)(2,1)S(1)} %get-tuple-element.25), channel_id=12, replica_groups={{0,1},{2,3},{4,5},{6,7},{8,9},{10,11},{12,13},{14,15},{16,17},{18,19},{..., dimensions={0}, use_global_device_ids=true | all-gather | bytes 589824 | tf_op jit(solution)/shard_map/all_gather | solution.py:19
  90.4 1.4 %shard_map.78 = (bf16[128,384]{1,0:T(8,128)(2,1)}, bf16[128,384]{1,0:T(8,128)(2,1)}, bf16[128,384]{1,0:T(8,128)(2,1)}, bf16[128,384]{1,0:T(8,128)(2,1)}) custom-call(s32[2]{0:T(128)S(1)} %pad_add_fusion.where_ref, bf16[128,768]{1,0:T(8,128)(2,1)S(1)} %get-tuple-element.24.keep_ref, bf16[2,128,768]{2,1,0:T(8,128)(2,1)S(1)} %bitcast.115), custom_call_target="tpu_custom_call" | custom-call | bytes 589832 | tf_op jit(solution)/shard_map/pallas_call | solution.py:236
  (78 shorter events, 1.0 us)

commit v5 on v4

--- a/solution.py
+++ b/solution.py
@@ -47,8 +47,13 @@
     return jnp.where(i < 16, 16 * i, jnp.where(i < 32, 8 + 16 * (i - 16), row))
 
 
-def sort_rows(where_ref, x_ref, send_ref, own_ref):
-    core, odd = where_ref[0], where_ref[1]
+def own_place():
+    device = lax.axis_index("seq")
+    return device & 1, ((device >> 1) ^ (device >> 2)) & 1
+
+
+def sort_rows(x_ref, send_ref, own_ref):
+    core, odd = own_place()
 
     def tile(array, h):
         cols = slice((h // 2) * 128, (h // 2) * 128 + 128)
@@ -72,8 +77,8 @@
     own_ref[:, 256:] = slots[1].astype(BF16)
 
 
-def unsort_rows(where_ref, own_ref, recv_ref, send_ref, keep_ref):
-    core, odd = where_ref[0], where_ref[1]
+def unsort_rows(own_ref, recv_ref, send_ref, keep_ref):
+    core, odd = own_place()
     first = jnp.where(odd == 0, own_ref[:, :256], recv_ref[:, :256].astype(F32)).astype(BF16)
     third = jnp.where(odd == 0, recv_ref[:, :256].astype(F32), own_ref[:, :256]).astype(BF16)
     middle = jnp.concatenate(
@@ -89,8 +94,8 @@
         send_ref[:, cols] = jnp.where(core == 0, rows[128:], rows[:128]).astype(BF16)
 
 
-def join_heads(where_ref, keep_ref, recv_ref, att_ref, dq_ref, dk_ref, dv_ref):
-    core = where_ref[0]
+def join_heads(keep_ref, recv_ref, att_ref, dq_ref, dk_ref, dv_ref):
+    core, _ = own_place()
     keep, recv = keep_ref[...].astype(F32), recv_ref[1 - core].astype(F32)
     low = jnp.where(core == 0, keep, recv)
     high = jnp.where(core == 0, recv, keep)
@@ -166,11 +171,9 @@
             place += rows
         heads.append(head)
 
-    for head in heads:
+    def score(head):
         head["top"] = [jnp.full((1, 128), NEG, F32) for _ in range(head["total"] // 128)]
-    for n in range(len(PIECES)):
-        for head in heads:
-            part, row, rows, width, place, counts, valid = head["pieces"][n]
+        for part, row, rows, width, place, counts, valid in head["pieces"]:
             keys = kv_refs[part][row : row + rows, head["cols"]]
             start = STARTS[part] + row
             head["t"][:, start : start + rows] = keys.T
@@ -183,55 +186,56 @@
             for t in range(width // 128):
                 head["top"][t] = jnp.maximum(head["top"][t], top[:, t * 128 : t * 128 + 128])
 
-    for head in heads:
+    def weigh(head):
         tiles = head["total"] // 128
-        head["peak"] = jnp.concatenate(head["top"], 1)
-        head["sums"] = [jnp.zeros((1, 128), F32) for _ in range(tiles)]
-        head["accs"] = [jnp.zeros((128, 128), F32) for _ in range(tiles)]
-    for n in range(len(PIECES)):
-        for head in heads:
-            part, row, rows, width, place, counts, valid = head["pieces"][n]
-            weights = jnp.exp(head["e"][place : place + rows, :width] - head["peak"][:, :width])
+        peak = jnp.concatenate(head["top"], 1)
+        sums = [jnp.zeros((1, 128), F32) for _ in range(tiles)]
+        accs = [jnp.zeros((HD, 128), F32) for _ in range(tiles)]
+        for part, row, rows, width, place, counts, valid in head["pieces"]:
+            weights = jnp.exp(head["e"][place : place + rows, :width] - peak[:, :width])
             if any(count is not None for count in counts):
                 cut = [weights[:, t * 128 : t * 128 + 128] for t in range(width // 128)]
                 cut = [w if c is None else w * c for w, c in zip(cut, counts)]
                 weights = jnp.concatenate(cut, 1)
             head["e"][place : place + rows, :width] = weights
             start = STARTS[part] + row
-            acc = dot(head["t"][:, start : start + rows], weights.astype(BF16))
+            acc = dot(head["t"][HD:, start : start + rows], weights.astype(BF16))
             added = jnp.sum(weights, axis=0, keepdims=True)
             for t in range(width // 128):
                 tile = slice(t * 128, t * 128 + 128)
-                head["sums"][t] = head["sums"][t] + added[:, tile]
-                head["accs"][t] = head["accs"][t] + acc[:, tile]
-
-    for head in heads:
-        head["inverse"] = 1.0 / jnp.concatenate(head["sums"], 1)
-        head["att"] = (jnp.concatenate(head["accs"], 1) * head["inverse"]).astype(BF16).astype(F32)
-        head["delta"] = jnp.sum(head["g_t"] * head["att"], axis=0, keepdims=True)
-        head["grads"] = [jnp.zeros((128, 128), F32) for _ in range(head["total"] // 128)]
-    for n in range(len(PIECES)):
-        for head in heads:
-            part, row, rows, width, place, counts, valid = head["pieces"][n]
+                sums[t] = sums[t] + added[:, tile]
+                accs[t] = accs[t] + acc[:, tile]
+        head["inverse"] = 1.0 / jnp.concatenate(sums, 1)
+        head["att"] = (jnp.concatenate(accs, 1) * head["inverse"]).astype(BF16).astype(F32)
+        head["delta"] = jnp.sum(head["g_t"][HD:] * head["att"], axis=0, keepdims=True)
+
+    def differentiate(head):
+        grads_q = [jnp.zeros((HD, 128), F32) for _ in range(head["total"] // 128)]
+        for part, row, rows, width, place, counts, valid in head["pieces"]:
             probs = head["e"][place : place + rows, :width] * head["inverse"][:, :width]
             grads = probs * (head["p"][place : place + rows, :width] - head["delta"][:, :width])
             grads = grads.astype(BF16)
             both = dot(grads, head["q_b"][:width]) + dot(probs.astype(BF16), head["g_b"][:width])
             d_refs[part][row : row + rows, head["cols"]] = both
             start = STARTS[part] + row
-            d_query = dot(head["t"][:, start : start + rows], grads)
+            d_query = dot(head["t"][:HD, start : start + rows], grads)
             for t in range(width // 128):
-                head["grads"][t] = head["grads"][t] + d_query[:, t * 128 : t * 128 + 128]
-    for head in heads:
-        out = jnp.where(sub, jnp.concatenate(head["grads"], 1) * HD**-0.5, head["att"])
+                grads_q[t] = grads_q[t] + d_query[:, t * 128 : t * 128 + 128]
+        out = jnp.concatenate([jnp.concatenate(grads_q, 1) * HD**-0.5, head["att"]], 0)
         head["out"][...] = out.T
 
-
-def call(body, outs, *args, scalar=True, scratch=(), flops=0):
+    longer, shorter = heads
+    score(shorter)
+    score(longer)
+    weigh(shorter)
+    weigh(longer)
+    differentiate(shorter)
+    differentiate(longer)
+
+
+def call(body, outs, *args, scratch=(), flops=0):
     vmem = pl.BlockSpec(memory_space=pltpu.VMEM)
     specs = [vmem] * len(args)
-    if scalar:
-        specs[0] = pl.BlockSpec(memory_space=pltpu.SMEM)
     moved = sum(a.size * a.dtype.itemsize for a in args)
     return pl.pallas_call(
         body,
@@ -271,10 +275,8 @@
 
 
 def per_device(query, keys, values, grad_out):
-    device = lax.axis_index("seq")
-    place = jnp.stack([device & 1, ((device >> 1) ^ (device >> 2)) & 1]).astype(jnp.int32)
     chip_rows = gather_pair(jnp.stack([query, keys, values, grad_out]), CORE)
-    send, own = call(sort_rows, [((256, 384), BF16), ((256, 512), BF16)], place, chip_rows)
+    send, own = call(sort_rows, [((256, 384), BF16), ((256, 512), BF16)], chip_rows)
     other = swap_with(send, Y_ONE)
     qg_a = interleave(own[:, :128], other[:, :128])
     qg_b = own[:, 256:384]
@@ -297,7 +299,6 @@
         [((512, 128), F32), ((256, 128), F32), ((512, 256), F32)]
         + [((n, 256), F32) for n in (384, 128, 384, 128)],
         qg_a, qg_b, *(kv[n] for n in range(5)),
-        scalar=False,
         scratch=[
             pltpu.VMEM((1536, 512), F32), pltpu.VMEM((1536, 256), F32),
             pltpu.VMEM((1536, 512), F32), pltpu.VMEM((1536, 256), F32),
@@ -311,9 +312,9 @@
     own_kv, other_kv = separate(grads[0])
     send = jnp.concatenate([other_a, other_kv], 1).astype(BF16)
     own = jnp.concatenate([own_a, own_kv[:, :128], out_b, own_kv[:, 128:]], 1)
-    send, keep = call(unsort_rows, [((128, 768), BF16)] * 2, place, own, swap_with(send, Y_ONE))
+    send, keep = call(unsort_rows, [((128, 768), BF16)] * 2, own, swap_with(send, Y_ONE))
     return tuple(
-        call(join_heads, [((128, 384), BF16)] * 4, place, keep, gather_pair(send, CORE))
+        call(join_heads, [((128, 384), BF16)] * 4, keep, gather_pair(send, CORE))
     )
 
 

time: 92.1 us -> 89.9 us (0.976)
  Pallas kernels: 6.71 us -> 4.66 us
    pallas_call x4, Pallas kernels: 6.71 us -> 4.66 us  [call(): pl.pallas_call(body, out_shape=[jax.ShapeDtypeStruct(s, d) for s, d in ou...]
where the time goes in v5:
time: 89.9 us; the launch traced here: 89.7 us
  blocking collectives  81.8 us (91%)
  Pallas kernels  4.66 us (5%)
  other arithmetic  1.68 us (2%)
  between operations  1.17 us (1%)
    all_gather x12, blocking collectives, gather_pair(): lax.all_gather(block, 'seq', axis_index_groups=pairs, axis=0, tiled=False)  81.8 us
    pallas_call x4, Pallas kernels, call(): pl.pallas_call(body, out_shape=[jax.ShapeDtypeStruct(s, d) for s, d in ou...  4.66 us

profile of v5, /device:TPU:1, one launch (start us, length us, event | category | flops | bytes accessed | tf_op | source)
XLA Modules:
  0.0 89.7 jit_solution(14430670830754352807)
XLA Ops:
  0.6 1.1 %pad_maximum_fusion.1 = bf16[4,128,384]{2,1,0:T(8,128)(2,1)S(1)} fusion(bf16[1,128,384]{2,1,0:T(8,128)(2,1)} %bitcast.117, bf16[1,128,384]{2,1,0:T(8,128)(2,1)} %bitcast.118, bf16[1,128,384]{2,1,0:T(8,128)(2,1)} %bitcast.119, bf16[1,128,384]{2,1,0:T(8,128)(2,1)} %bitcast.120), kind=kLoop, calls=%fused_computation.1 | loop fusion | flops 589824 | bytes 786432 | tf_op jit(solution)/shard_map/stack | solution.py:278
  1.8 8.9 %all-gather = bf16[8,128,384]{2,1,0:T(8,128)(2,1)S(1)} all-gather(bf16[4,128,384]{2,1,0:T(8,128)(2,1)S(1)} %pad_maximum_fusion.1), channel_id=2, replica_groups={{0,1},{2,3},{4,5},{6,7},{8,9},{10,11},{12,13},{14,15},{16,17},{18,19},{..., dimensions={0}, use_global_device_ids=true | all-gather | bytes 1179648 | tf_op jit(solution)/shard_map/all_gather | solution.py:19
  10.6 0.5 shard_map.75
  11.2 6.8 %all-gather.1 = bf16[512,384]{1,0:T(8,128)(2,1)S(1)} all-gather(bf16[256,384]{1,0:T(8,128)(2,1)S(1)} %get-tuple-element.16), channel_id=3, replica_groups={{0,2},{1,3},{4,6},{5,7},{8,10},{9,11},{12,14},{13,15},{16,18},{17,19},{..., dimensions={0}, use_global_device_ids=true | all-gather | bytes 589824 | tf_op jit(solution)/shard_map/all_gather | solution.py:19
  18.3 5.0 %all-gather.2 = bf16[256,256]{1,0:T(8,128)(2,1)S(1)} all-gather(bf16[128,256]{1,0:T(8,128)(2,1)S(1)} %get-tuple-element.48), channel_id=4, replica_groups={{0,14},{1,15},{2,12},{3,13},{4,10},{5,11},{6,8},{7,9},{16,30},{17,31},{..., dimensions={0}, use_global_device_ids=true | all-gather | bytes 196608 | tf_op jit(solution)/shard_map/all_gather | solution.py:19
  23.4 7.1 %all-gather.3 = bf16[768,256]{1,0:T(8,128)(2,1)S(1)} all-gather(bf16[384,256]{1,0:T(8,128)(2,1)S(1)} %get-tuple-element.30), channel_id=5, replica_groups={{0,6},{1,7},{2,4},{3,5},{8,14},{9,15},{10,12},{11,13},{16,22},{17,23},{..., dimensions={0}, use_global_device_ids=true | all-gather | bytes 589824 | tf_op jit(solution)/shard_map/all_gather | solution.py:19
  30.7 4.7 %all-gather.4 = bf16[256,256]{1,0:T(8,128)(2,1)S(1)} all-gather(bf16[128,256]{1,0:T(8,128)(2,1)S(1)} %constant_dynamic-update-slice_fusion.35), channel_id=6, replica_groups={{0,32},{1,33},{2,34},{3,35},{4,36},{5,37},{6,38},{7,39},{8,40},{9,41},{..., dimensions={0}, use_global_device_ids=true | all-gather | bytes 196608 | tf_op jit(solution)/shard_map/all_gather | solution.py:19
  35.4 5.9 %all-gather.5 = bf16[768,256]{1,0:T(8,128)(2,1)S(1)} all-gather(bf16[384,256]{1,0:T(8,128)(2,1)S(1)} %get-tuple-element.28), channel_id=7, replica_groups={{0,16},{1,17},{2,18},{3,19},{4,20},{5,21},{6,22},{7,23},{8,24},{9,25},{..., dimensions={0}, use_global_device_ids=true | all-gather | bytes 589824 | tf_op jit(solution)/shard_map/all_gather | solution.py:19
  41.3 2.9 %shard_map.76 = (f32[512,128]{1,0:T(8,128)S(1)}, f32[256,128]{1,0:T(8,128)S(1)}, f32[512,256]{1,0:T(8,128)S(1)}, f32[384,256]{1,0:T(8,128)S(1)}, f32[128,256]{1,...) custom-call(bf16[512,128]{1,0:T(8,128)(2,1)S(1)} %constant_dynamic-update-slice_fusion.qga_ref, ...), custom_call_target="tpu_custom_call" | custom-call | flops 600000000 | bytes 983040 | tf_op jit(solution)/shard_map/pallas_call | solution.py:240
  44.4 5.2 %all-gather.6 = bf16[768,256]{1,0:T(8,128)(2,1)S(1)} all-gather(bf16[384,256]{1,0:T(8,128)(2,1)S(1)} %convert_element_type.38), channel_id=8, replica_groups={{0,16},{1,17},{2,18},{3,19},{4,20},{5,21},{6,22},{7,23},{8,24},{9,25},{..., dimensions={0}, use_global_device_ids=true | all-gather | bytes 589824 | tf_op jit(solution)/shard_map/all_gather | solution.py:19
  49.7 5.3 %all-gather.7 = bf16[256,256]{1,0:T(8,128)(2,1)S(1)} all-gather(bf16[128,256]{1,0:T(8,128)(2,1)S(1)} %fusion.9), channel_id=9, replica_groups={{0,32},{1,33},{2,34},{3,35},{4,36},{5,37},{6,38},{7,39},{8,40},{9,41},{..., dimensions={0}, use_global_device_ids=true | all-gather | bytes 196608 | tf_op jit(solution)/shard_map/all_gather | solution.py:19
  55.2 7.0 %all-gather.8 = bf16[768,256]{1,0:T(8,128)(2,1)S(1)} all-gather(bf16[384,256]{1,0:T(8,128)(2,1)S(1)} %convert_element_type.42), channel_id=10, replica_groups={{0,6},{1,7},{2,4},{3,5},{8,14},{9,15},{10,12},{11,13},{16,22},{17,23},{..., dimensions={0}, use_global_device_ids=true | all-gather | bytes 589824 | tf_op jit(solution)/shard_map/all_gather | solution.py:19
  62.3 5.0 %all-gather.9 = bf16[256,256]{1,0:T(8,128)(2,1)S(1)} all-gather(bf16[128,256]{1,0:T(8,128)(2,1)S(1)} %fusion.7), channel_id=11, replica_groups={{0,14},{1,15},{2,12},{3,13},{4,10},{5,11},{6,8},{7,9},{16,30},{17,31},{..., dimensions={0}, use_global_device_ids=true | all-gather | bytes 196608 | tf_op jit(solution)/shard_map/all_gather | solution.py:19
  67.4 13.2 %all_gather.90 = bf16[2,256,384]{2,1,0:T(8,128)(2,1)S(1)} all-gather(bf16[1,256,384]{2,1,0:T(8,128)(2,1)S(1)} %pad_maximum_fusion.2), channel_id=1, replica_groups={{0,2},{1,3},{4,6},{5,7},{8,10},{9,11},{12,14},{13,15},{16,18},{17,19},{..., dimensions={0}, use_global_device_ids=true | all-gather | bytes 589824 | tf_op jit(solution)/shard_map/all_gather | solution.py:19
  80.8 0.3 shard_map.77
  81.1 7.6 %all-gather.10 = bf16[256,768]{1,0:T(8,128)(2,1)S(1)} all-gather(bf16[128,768]{1,0:T(8,128)(2,1)S(1)} %get-tuple-element.25), channel_id=12, replica_groups={{0,1},{2,3},{4,5},{6,7},{8,9},{10,11},{12,13},{14,15},{16,17},{18,19},{..., dimensions={0}, use_global_device_ids=true | all-gather | bytes 589824 | tf_op jit(solution)/shard_map/all_gather | solution.py:19
  88.8 0.9 shard_map.78
  (78 shorter events, 1.0 us)

commit v6 on v5

--- a/solution.py
+++ b/solution.py
@@ -74,16 +74,17 @@
     send_ref[:, :256] = jnp.where(odd == 0, slots[2], slots[0]).astype(BF16)
     send_ref[:, 256:] = slots[1][:, 128:].astype(BF16)
     own_ref[:, :256] = jnp.where(odd == 0, slots[0], slots[2]).astype(BF16)
-    own_ref[:, 256:] = slots[1].astype(BF16)
-
-
-def unsort_rows(own_ref, recv_ref, send_ref, keep_ref):
+    own_ref[:, 256:384] = slots[1][:, 128:].astype(BF16)
+    own_ref[:, 384:] = slots[1][:, :128].astype(BF16)
+
+
+def unsort_rows(a_ref, b_ref, d_ref, recv_ref, send_ref, keep_ref):
     core, odd = own_place()
-    first = jnp.where(odd == 0, own_ref[:, :256], recv_ref[:, :256].astype(F32)).astype(BF16)
-    third = jnp.where(odd == 0, recv_ref[:, :256].astype(F32), own_ref[:, :256]).astype(BF16)
-    middle = jnp.concatenate(
-        [own_ref[:, 256:384], own_ref[:, 384:] + recv_ref[:, 256:].astype(F32)], 1
-    ).astype(BF16)
+    mine = jnp.concatenate([a_ref[...], d_ref[:, :128].astype(BF16)], 1)
+    first = jnp.where(odd == 0, mine, recv_ref[:, :256])
+    third = jnp.where(odd == 0, recv_ref[:, :256], mine)
+    shared = d_ref[:, 128:] + recv_ref[:, 256:].astype(F32)
+    middle = jnp.concatenate([b_ref[...], shared.astype(BF16)], 1)
     sub = lax.broadcasted_iota(jnp.int32, (256, 256), 0)
     source = source_rows((1, 256), 1)
     for s, slot in enumerate((first, middle, third)):
@@ -127,30 +128,56 @@
 
 
 def key_ranks(level):
-    i = lax.broadcasted_iota(jnp.int32, (256, 128), 0) & (511 >> max(level, 1))
-    return sum((i < (32 << k)).astype(F32) for k in range(4))
-
-
-def attend(qga_ref, qgb_ref, kv0_ref, r1_ref, r2_ref, r3_ref, r4_ref,
-           outa_ref, outb_ref, d0_ref, d1_ref, d2_ref, d3_ref, d4_ref,
+    i = lax.broadcasted_iota(jnp.int32, (256, 128), 0) & (127 >> max(level - 1, 0))
+    return sum((i < (16 << k)).astype(F32) for k in range(4))
+
+
+CLASSES = (0, 16, 32, 64, 128, 256)
+
+
+def interleave(own, partner):
+    parts = []
+    for a, b in zip(CLASSES, CLASSES[1:]):
+        parts += [own[a:b], partner[a:b]]
+    return jnp.concatenate(parts, 0)
+
+
+def attend(own_ref, other_ref, qgb_ref, kv0_ref, r1_ref, r2_ref, r3_ref, r4_ref, kv5_ref,
+           outa_ref, outo_ref, outb_ref, d0_ref, d1_ref, d2_ref, d3_ref, d4_ref, d5_ref,
            ea_ref, eb_ref, pa_ref, pb_ref, ta_ref, tb_ref):
-    kv_refs = (kv0_ref, r1_ref, r2_ref, r3_ref, r4_ref)
-    d_refs = (d0_ref, d1_ref, d2_ref, d3_ref, d4_ref)
+    kv_refs = (None, r1_ref, r2_ref, r3_ref, r4_ref)
+    d_refs = (None, d1_ref, d2_ref, d3_ref, d4_ref)
+
+    def keys_of(part, row, rows, cols):
+        if part:
+            return kv_refs[part][row : row + rows, cols]
+        half = slice(row // 2, row // 2 + 128)
+        return jnp.concatenate([kv0_ref[half, cols], kv5_ref[half, cols]], 0)
+
+    def put(part, row, rows, cols, both):
+        if part:
+            d_refs[part][row : row + rows, cols] = both
+        else:
+            half = slice(row // 2, row // 2 + 128)
+            d0_ref[half, cols] = both[:128]
+            d5_ref[half, cols] = both[128:]
+
     sub = lax.broadcasted_iota(jnp.int32, (128, 1), 0) < HD
     ranks = [key_ranks(level) for level in (1, 2, 3)]
     heads = []
-    for which, (qg_ref, out_ref, e_ref, p_ref, t_ref) in enumerate(
-        ((qga_ref, outa_ref, ea_ref, pa_ref, ta_ref), (qgb_ref, outb_ref, eb_ref, pb_ref, tb_ref))
+    pair = interleave(own_ref[...], other_ref[...])
+    for which, (qg, e_ref, p_ref, t_ref) in enumerate(
+        ((pair, ea_ref, pa_ref, ta_ref), (qgb_ref[...], eb_ref, pb_ref, tb_ref))
     ):
-        total = qg_ref.shape[0]
-        qg = qg_ref[...].astype(F32)
+        total = qg.shape[0]
+        qg = qg.astype(F32)
         low = left_half(qg.shape)
         turned = qg.T
         g_t = jnp.where(sub, 0.0, turned)
         query_rank = rank((1, 128), 1, total // 16)
         shared = [jnp.minimum(r, query_rank) for r in ranks]
         head = dict(
-            total=total, out=out_ref, e=e_ref, p=p_ref, t=t_ref, g_t=g_t, g_tb=g_t.astype(BF16),
+            total=total, e=e_ref, p=p_ref, t=t_ref, g_t=g_t, g_tb=g_t.astype(BF16),
             q_t=jnp.where(sub, turned * HD**-0.5, 0.0).astype(BF16),
             q_b=jnp.where(low, qg * HD**-0.5, 0.0).astype(BF16),
             g_b=jnp.where(low, 0.0, qg).astype(BF16),
@@ -174,7 +201,7 @@
     def score(head):
         head["top"] = [jnp.full((1, 128), NEG, F32) for _ in range(head["total"] // 128)]
         for part, row, rows, width, place, counts, valid in head["pieces"]:
-            keys = kv_refs[part][row : row + rows, head["cols"]]
+            keys = keys_of(part, row, rows, head["cols"])
             start = STARTS[part] + row
             head["t"][:, start : start + rows] = keys.T
             scores = dot(keys, head["q_t"][:, :width])
@@ -216,21 +243,24 @@
             grads = probs * (head["p"][place : place + rows, :width] - head["delta"][:, :width])
             grads = grads.astype(BF16)
             both = dot(grads, head["q_b"][:width]) + dot(probs.astype(BF16), head["g_b"][:width])
-            d_refs[part][row : row + rows, head["cols"]] = both
+            put(part, row, rows, head["cols"], both)
             start = STARTS[part] + row
             d_query = dot(head["t"][:HD, start : start + rows], grads)
             for t in range(width // 128):
                 grads_q[t] = grads_q[t] + d_query[:, t * 128 : t * 128 + 128]
         out = jnp.concatenate([jnp.concatenate(grads_q, 1) * HD**-0.5, head["att"]], 0)
-        head["out"][...] = out.T
+        return out.T.astype(BF16)
 
     longer, shorter = heads
     score(shorter)
     score(longer)
     weigh(shorter)
     weigh(longer)
-    differentiate(shorter)
-    differentiate(longer)
+    outb_ref[...] = differentiate(shorter)
+    out = differentiate(longer)
+    for a, b in zip(CLASSES, CLASSES[1:]):
+        outa_ref[a:b] = out[2 * a : a + b]
+        outo_ref[a:b] = out[a + b : 2 * b]
 
 
 def call(body, outs, *args, scratch=(), flops=0):
@@ -248,24 +278,6 @@
     )(*args)
 
 
-CLASSES = (0, 16, 32, 64, 128, 256)
-
-
-def interleave(own, partner):
-    parts = []
-    for a, b in zip(CLASSES, CLASSES[1:]):
-        parts += [own[a:b], partner[a:b]]
-    return jnp.concatenate(parts, 0)
-
-
-def separate(rows):
-    own, partner = [], []
-    for a, b in zip(CLASSES, CLASSES[1:]):
-        own.append(rows[2 * a : a + b])
-        partner.append(rows[a + b : 2 * b])
-    return jnp.concatenate(own, 0), jnp.concatenate(partner, 0)
-
-
 def add_rows(arrays, blocks, extra):
     extra, start = extra.astype(F32), 0
     for n, at, size in blocks:
@@ -278,27 +290,21 @@
     chip_rows = gather_pair(jnp.stack([query, keys, values, grad_out]), CORE)
     send, own = call(sort_rows, [((256, 384), BF16), ((256, 512), BF16)], chip_rows)
     other = swap_with(send, Y_ONE)
-    qg_a = interleave(own[:, :128], other[:, :128])
-    qg_b = own[:, 256:384]
-    kv0 = interleave(
-        jnp.concatenate([own[:, 128:256], own[:, 384:]], 1), other[:, 128:]
+    kv = {0: own[:, 128:384], 5: other[:, 128:]}
+    ring = [(0, 0), (5, 0), (1, 0), (1, 128), (1, 256), (1, 320), (2, 0), (2, 64)]
+    steps = (
+        (2, [(0, 0, 64), (5, 0, 64)], Y_SEVEN),
+        (1, [(0, 0, 128), (5, 0, 128), (2, 0, 128)], Y_THREE),
+        (4, [(n, at, 16) for n, at in ring], Z_TWO),
+        (3, [(n, at, 32) for n, at in ring] + [(4, 0, 128)], Z_ONE),
     )
-    ring = [(0, 0), (1, 0), (1, 256), (2, 0)]
-    steps = (
-        (2, [(0, 0, 128)], Y_SEVEN),
-        (1, [(0, 0, 256), (2, 0, 128)], Y_THREE),
-        (4, [(n, at, 32) for n, at in ring], Z_TWO),
-        (3, [(n, at, 64) for n, at in ring] + [(4, 0, 128)], Z_ONE),
-    )
-    kv = {0: kv0}
     for part, blocks, flip in steps:
         rows = jnp.concatenate([kv[n][at : at + size] for n, at, size in blocks], 0)
         kv[part] = swap_with(rows, flip)
-    out_a, out_b, *grads = call(
+    *outs, d0, d1, d2, d3, d4, d5 = call(
         attend,
-        [((512, 128), F32), ((256, 128), F32), ((512, 256), F32)]
-        + [((n, 256), F32) for n in (384, 128, 384, 128)],
-        qg_a, qg_b, *(kv[n] for n in range(5)),
+        [((256, 128), BF16)] * 3 + [((n, 256), F32) for n in (256, 384, 128, 384, 128, 256)],
+        own[:, :128], other[:, :128], own[:, 384:], *(kv[n] for n in range(6)),
         scratch=[
             pltpu.VMEM((1536, 512), F32), pltpu.VMEM((1536, 256), F32),
             pltpu.VMEM((1536, 512), F32), pltpu.VMEM((1536, 256), F32),
@@ -306,13 +312,11 @@
         ],
         flops=int(6e8),
     )
+    grads = [d0, d1, d2, d3, d4, d5]
     for part, blocks, flip in reversed(steps):
         add_rows(grads, blocks, swap_with(grads[part].astype(BF16), flip))
-    own_a, other_a = separate(out_a)
-    own_kv, other_kv = separate(grads[0])
-    send = jnp.concatenate([other_a, other_kv], 1).astype(BF16)
-    own = jnp.concatenate([own_a, own_kv[:, :128], out_b, own_kv[:, 128:]], 1)
-    send, keep = call(unsort_rows, [((128, 768), BF16)] * 2, own, swap_with(send, Y_ONE))
+    send = jnp.concatenate([outs[1], grads[5].astype(BF16)], 1)
+    send, keep = call(unsort_rows, [((128, 768), BF16)] * 2, outs[0], outs[2], grads[0], swap_with(send, Y_ONE))
     return tuple(
         call(join_heads, [((128, 384), BF16)] * 4, keep, gather_pair(send, CORE))
     )

time: 89.9 us -> 89.5 us (level)
  no operation moved by 1% of the time
where the time goes in v6:
time: 89.5 us; the launch traced here: 89.3 us
  blocking collectives  81.8 us (91%)
  Pallas kernels  4.67 us (5%)
  other arithmetic  1.65 us (2%)
  between operations  1.07 us (1%)
    all_gather x12, blocking collectives, gather_pair(): lax.all_gather(block, 'seq', axis_index_groups=pairs, axis=0, tiled=False)  81.8 us
    pallas_call x4, Pallas kernels, call(): pl.pallas_call(body, out_shape=[jax.ShapeDtypeStruct(s, d) for s, d in ou...  4.67 us

profile of v6, /device:TPU:1, one launch (start us, length us, event | category | flops | bytes accessed | tf_op | source)
XLA Modules:
  0.0 89.3 jit_solution(8788130248214301423)
XLA Ops:
  0.6 1.1 %pad_maximum_fusion = bf16[4,128,384]{2,1,0:T(8,128)(2,1)S(1)} fusion(bf16[1,128,384]{2,1,0:T(8,128)(2,1)} %bitcast.204, bf16[1,128,384]{2,1,0:T(8,128)(2,1)} %bitcast.205, bf16[1,128,384]{2,1,0:T(8,128)(2,1)} %bitcast.206, bf16[1,128,384]{2,1,0:T(8,128)(2,1)} %bitcast.207), kind=kLoop, calls=%fused_computation | loop fusion | flops 589824 | bytes 786432 | tf_op jit(solution)/shard_map/stack | solution.py:290
  1.8 8.9 %all-gather = bf16[8,128,384]{2,1,0:T(8,128)(2,1)S(1)} all-gather(bf16[4,128,384]{2,1,0:T(8,128)(2,1)S(1)} %pad_maximum_fusion), channel_id=2, replica_groups={{0,1},{2,3},{4,5},{6,7},{8,9},{10,11},{12,13},{14,15},{16,17},{18,19},{..., dimensions={0}, use_global_device_ids=true | all-gather | bytes 1179648 | tf_op jit(solution)/shard_map/all_gather | solution.py:19
  10.6 0.5 shard_map.75
  11.3 6.8 %all-gather.1 = bf16[512,384]{1,0:T(8,128)(2,1)S(1)} all-gather(bf16[256,384]{1,0:T(8,128)(2,1)S(1)} %get-tuple-element.18), channel_id=3, replica_groups={{0,2},{1,3},{4,6},{5,7},{8,10},{9,11},{12,14},{13,15},{16,18},{17,19},{..., dimensions={0}, use_global_device_ids=true | all-gather | bytes 589824 | tf_op jit(solution)/shard_map/all_gather | solution.py:19
  18.1 5.0 %all-gather.2 = bf16[256,256]{1,0:T(8,128)(2,1)S(1)} all-gather(bf16[128,256]{1,0:T(8,128)(2,1)S(1)} %pad_maximum_fusion.3), channel_id=4, replica_groups={{0,14},{1,15},{2,12},{3,13},{4,10},{5,11},{6,8},{7,9},{16,30},{17,31},{..., dimensions={0}, use_global_device_ids=true | all-gather | bytes 196608 | tf_op jit(solution)/shard_map/all_gather | solution.py:19
  23.2 7.1 %all-gather.3 = bf16[768,256]{1,0:T(8,128)(2,1)S(1)} all-gather(bf16[384,256]{1,0:T(8,128)(2,1)S(1)} %pad_maximum_fusion.1), channel_id=5, replica_groups={{0,6},{1,7},{2,4},{3,5},{8,14},{9,15},{10,12},{11,13},{16,22},{17,23},{..., dimensions={0}, use_global_device_ids=true | all-gather | bytes 589824 | tf_op jit(solution)/shard_map/all_gather | solution.py:19
  30.5 4.7 %all-gather.4 = bf16[256,256]{1,0:T(8,128)(2,1)S(1)} all-gather(bf16[128,256]{1,0:T(8,128)(2,1)S(1)} %constant_dynamic-update-slice_fusion), channel_id=6, replica_groups={{0,32},{1,33},{2,34},{3,35},{4,36},{5,37},{6,38},{7,39},{8,40},{9,41},{..., dimensions={0}, use_global_device_ids=true | all-gather | bytes 196608 | tf_op jit(solution)/shard_map/all_gather | solution.py:19
  35.3 5.9 %all-gather.5 = bf16[768,256]{1,0:T(8,128)(2,1)S(1)} all-gather(bf16[384,256]{1,0:T(8,128)(2,1)S(1)} %get-tuple-element.30), channel_id=7, replica_groups={{0,16},{1,17},{2,18},{3,19},{4,20},{5,21},{6,22},{7,23},{8,24},{9,25},{..., dimensions={0}, use_global_device_ids=true | all-gather | bytes 589824 | tf_op jit(solution)/shard_map/all_gather | solution.py:19
  41.2 2.9 %shard_map.76 = (bf16[256,128]{1,0:T(8,128)(2,1)S(1)}, bf16[256,128]{1,0:T(8,128)(2,1)S(1)}, bf16[256,128]{1,0:T(8,128)(2,1)S(1)}, f32[256,256]{1,0:T(8,128)S(1)...) custom-call(bf16[256,128]{1,0:T(8,128)(2,1)S(1)} %get-tuple-element., ...), custom_call_target="tpu_custom_call" | custom-call | flops 600000000 | bytes 983040 | tf_op jit(solution)/shard_map/pallas_call | solution.py:270
  44.1 5.2 %all-gather.6 = bf16[768,256]{1,0:T(8,128)(2,1)S(1)} all-gather(bf16[384,256]{1,0:T(8,128)(2,1)S(1)} %convert_element_type.31), channel_id=8, replica_groups={{0,16},{1,17},{2,18},{3,19},{4,20},{5,21},{6,22},{7,23},{8,24},{9,25},{..., dimensions={0}, use_global_device_ids=true | all-gather | bytes 589824 | tf_op jit(solution)/shard_map/all_gather | solution.py:19
  49.5 5.3 %all-gather.7 = bf16[256,256]{1,0:T(8,128)(2,1)S(1)} all-gather(bf16[128,256]{1,0:T(8,128)(2,1)S(1)} %fusion.9), channel_id=9, replica_groups={{0,32},{1,33},{2,34},{3,35},{4,36},{5,37},{6,38},{7,39},{8,40},{9,41},{..., dimensions={0}, use_global_device_ids=true | all-gather | bytes 196608 | tf_op jit(solution)/shard_map/all_gather | solution.py:19
  54.9 7.0 %all-gather.8 = bf16[768,256]{1,0:T(8,128)(2,1)S(1)} all-gather(bf16[384,256]{1,0:T(8,128)(2,1)S(1)} %convert_element_type.35), channel_id=10, replica_groups={{0,6},{1,7},{2,4},{3,5},{8,14},{9,15},{10,12},{11,13},{16,22},{17,23},{..., dimensions={0}, use_global_device_ids=true | all-gather | bytes 589824 | tf_op jit(solution)/shard_map/all_gather | solution.py:19
  62.0 0.1 fusion.4
  62.1 5.0 %all-gather.9 = bf16[256,256]{1,0:T(8,128)(2,1)S(1)} all-gather(bf16[128,256]{1,0:T(8,128)(2,1)S(1)} %get-tuple-element.33), channel_id=11, replica_groups={{0,14},{1,15},{2,12},{3,13},{4,10},{5,11},{6,8},{7,9},{16,30},{17,31},{..., dimensions={0}, use_global_device_ids=true | all-gather | bytes 196608 | tf_op jit(solution)/shard_map/all_gather | solution.py:19
  67.2 13.3 %all-gather.10 = bf16[512,384]{1,0:T(8,128)(2,1)S(1)} all-gather(bf16[256,384]{1,0:T(8,128)(2,1)S(1)} %pad_maximum_fusion.2), channel_id=12, replica_groups={{0,2},{1,3},{4,6},{5,7},{8,10},{9,11},{12,14},{13,15},{16,18},{17,19},{..., dimensions={0}, use_global_device_ids=true | all-gather | bytes 589824 | tf_op jit(solution)/shard_map/all_gather | solution.py:19
  80.5 0.3 shard_map.77
  80.8 7.6 %all-gather.11 = bf16[256,768]{1,0:T(8,128)(2,1)S(1)} all-gather(bf16[128,768]{1,0:T(8,128)(2,1)S(1)} %get-tuple-element.29), channel_id=13, replica_groups={{0,1},{2,3},{4,5},{6,7},{8,9},{10,11},{12,13},{14,15},{16,17},{18,19},{..., dimensions={0}, use_global_device_ids=true | all-gather | bytes 589824 | tf_op jit(solution)/shard_map/all_gather | solution.py:19
  88.4 0.9 shard_map.78
  (55 shorter events, 0.6 us)

commit v7 on v6

--- a/solution.py
+++ b/solution.py
@@ -156,7 +156,7 @@
 
     def put(part, row, rows, cols, both):
         if part:
-            d_refs[part][row : row + rows, cols] = both
+            d_refs[part][row : row + rows, cols] = both.astype(d_refs[part].dtype)
         else:
             half = slice(row // 2, row // 2 + 128)
             d0_ref[half, cols] = both[:128]
@@ -303,7 +303,8 @@
         kv[part] = swap_with(rows, flip)
     *outs, d0, d1, d2, d3, d4, d5 = call(
         attend,
-        [((256, 128), BF16)] * 3 + [((n, 256), F32) for n in (256, 384, 128, 384, 128, 256)],
+        [((256, 128), BF16)] * 3
+        + [((n, 256), BF16 if part == 3 else F32) for part, n in enumerate((256, 384, 128, 384, 128, 256))],
         own[:, :128], other[:, :128], own[:, 384:], *(kv[n] for n in range(6)),
         scratch=[
             pltpu.VMEM((1536, 512), F32), pltpu.VMEM((1536, 256), F32),

time: 89.5 us -> 89.5 us (level)
  no operation moved by 1% of the time
where the time goes in v7:
time: 89.5 us; the launch traced here: 89.3 us
  blocking collectives  81.8 us (91%)
  Pallas kernels  4.67 us (5%)
  other arithmetic  1.63 us (2%)
  between operations  1.06 us (1%)
    all_gather x12, blocking collectives, gather_pair(): lax.all_gather(block, 'seq', axis_index_groups=pairs, axis=0, tiled=False)  81.8 us
    pallas_call x4, Pallas kernels, call(): pl.pallas_call(body, out_shape=[jax.ShapeDtypeStruct(s, d) for s, d in ou...  4.67 us

profile of v7, /device:TPU:1, one launch (start us, length us, event | category | flops | bytes accessed | tf_op | source)
XLA Modules:
  0.0 89.3 jit_solution(5613730894616873863)
XLA Ops:
  0.6 1.1 %pad_maximum_fusion = bf16[4,128,384]{2,1,0:T(8,128)(2,1)S(1)} fusion(bf16[1,128,384]{2,1,0:T(8,128)(2,1)} %bitcast.204, bf16[1,128,384]{2,1,0:T(8,128)(2,1)} %bitcast.205, bf16[1,128,384]{2,1,0:T(8,128)(2,1)} %bitcast.206, bf16[1,128,384]{2,1,0:T(8,128)(2,1)} %bitcast.207), kind=kLoop, calls=%fused_computation | loop fusion | flops 589824 | bytes 786432 | tf_op jit(solution)/shard_map/stack | solution.py:290
  1.8 8.9 %all-gather = bf16[8,128,384]{2,1,0:T(8,128)(2,1)S(1)} all-gather(bf16[4,128,384]{2,1,0:T(8,128)(2,1)S(1)} %pad_maximum_fusion), channel_id=2, replica_groups={{0,1},{2,3},{4,5},{6,7},{8,9},{10,11},{12,13},{14,15},{16,17},{18,19},{..., dimensions={0}, use_global_device_ids=true | all-gather | bytes 1179648 | tf_op jit(solution)/shard_map/all_gather | solution.py:19
  10.6 0.5 shard_map.75
  11.3 6.8 %all-gather.1 = bf16[512,384]{1,0:T(8,128)(2,1)S(1)} all-gather(bf16[256,384]{1,0:T(8,128)(2,1)S(1)} %get-tuple-element.18), channel_id=3, replica_groups={{0,2},{1,3},{4,6},{5,7},{8,10},{9,11},{12,14},{13,15},{16,18},{17,19},{..., dimensions={0}, use_global_device_ids=true | all-gather | bytes 589824 | tf_op jit(solution)/shard_map/all_gather | solution.py:19
  18.1 5.0 %all-gather.2 = bf16[256,256]{1,0:T(8,128)(2,1)S(1)} all-gather(bf16[128,256]{1,0:T(8,128)(2,1)S(1)} %pad_maximum_fusion.3), channel_id=4, replica_groups={{0,14},{1,15},{2,12},{3,13},{4,10},{5,11},{6,8},{7,9},{16,30},{17,31},{..., dimensions={0}, use_global_device_ids=true | all-gather | bytes 196608 | tf_op jit(solution)/shard_map/all_gather | solution.py:19
  23.2 7.1 %all-gather.3 = bf16[768,256]{1,0:T(8,128)(2,1)S(1)} all-gather(bf16[384,256]{1,0:T(8,128)(2,1)S(1)} %pad_maximum_fusion.1), channel_id=5, replica_groups={{0,6},{1,7},{2,4},{3,5},{8,14},{9,15},{10,12},{11,13},{16,22},{17,23},{..., dimensions={0}, use_global_device_ids=true | all-gather | bytes 589824 | tf_op jit(solution)/shard_map/all_gather | solution.py:19
  30.5 4.7 %all-gather.4 = bf16[256,256]{1,0:T(8,128)(2,1)S(1)} all-gather(bf16[128,256]{1,0:T(8,128)(2,1)S(1)} %constant_dynamic-update-slice_fusion), channel_id=6, replica_groups={{0,32},{1,33},{2,34},{3,35},{4,36},{5,37},{6,38},{7,39},{8,40},{9,41},{..., dimensions={0}, use_global_device_ids=true | all-gather | bytes 196608 | tf_op jit(solution)/shard_map/all_gather | solution.py:19
  35.3 5.9 %all-gather.5 = bf16[768,256]{1,0:T(8,128)(2,1)S(1)} all-gather(bf16[384,256]{1,0:T(8,128)(2,1)S(1)} %get-tuple-element.30), channel_id=7, replica_groups={{0,16},{1,17},{2,18},{3,19},{4,20},{5,21},{6,22},{7,23},{8,24},{9,25},{..., dimensions={0}, use_global_device_ids=true | all-gather | bytes 589824 | tf_op jit(solution)/shard_map/all_gather | solution.py:19
  41.2 2.9 %shard_map.76 = (bf16[256,128]{1,0:T(8,128)(2,1)S(1)}, bf16[256,128]{1,0:T(8,128)(2,1)S(1)}, bf16[256,128]{1,0:T(8,128)(2,1)S(1)}, f32[256,256]{1,0:T(8,128)S(1)...) custom-call(bf16[256,128]{1,0:T(8,128)(2,1)S(1)} %get-tuple-element., ...), custom_call_target="tpu_custom_call" | custom-call | flops 600000000 | bytes 983040 | tf_op jit(solution)/shard_map/pallas_call | solution.py:270
  44.1 5.2 %all-gather.6 = bf16[768,256]{1,0:T(8,128)(2,1)S(1)} all-gather(bf16[384,256]{1,0:T(8,128)(2,1)S(1)} %get-tuple-element.22), channel_id=8, replica_groups={{0,16},{1,17},{2,18},{3,19},{4,20},{5,21},{6,22},{7,23},{8,24},{9,25},{..., dimensions={0}, use_global_device_ids=true | all-gather | bytes 589824 | tf_op jit(solution)/shard_map/all_gather | solution.py:19
  49.5 5.3 %all-gather.7 = bf16[256,256]{1,0:T(8,128)(2,1)S(1)} all-gather(bf16[128,256]{1,0:T(8,128)(2,1)S(1)} %fusion.9), channel_id=9, replica_groups={{0,32},{1,33},{2,34},{3,35},{4,36},{5,37},{6,38},{7,39},{8,40},{9,41},{..., dimensions={0}, use_global_device_ids=true | all-gather | bytes 196608 | tf_op jit(solution)/shard_map/all_gather | solution.py:19
  54.9 7.0 %all-gather.8 = bf16[768,256]{1,0:T(8,128)(2,1)S(1)} all-gather(bf16[384,256]{1,0:T(8,128)(2,1)S(1)} %convert_element_type.31), channel_id=10, replica_groups={{0,6},{1,7},{2,4},{3,5},{8,14},{9,15},{10,12},{11,13},{16,22},{17,23},{..., dimensions={0}, use_global_device_ids=true | all-gather | bytes 589824 | tf_op jit(solution)/shard_map/all_gather | solution.py:19
  61.9 0.1 fusion.4
  62.0 5.0 %all-gather.9 = bf16[256,256]{1,0:T(8,128)(2,1)S(1)} all-gather(bf16[128,256]{1,0:T(8,128)(2,1)S(1)} %get-tuple-element.33), channel_id=11, replica_groups={{0,14},{1,15},{2,12},{3,13},{4,10},{5,11},{6,8},{7,9},{16,30},{17,31},{..., dimensions={0}, use_global_device_ids=true | all-gather | bytes 196608 | tf_op jit(solution)/shard_map/all_gather | solution.py:19
  67.2 13.3 %all-gather.10 = bf16[512,384]{1,0:T(8,128)(2,1)S(1)} all-gather(bf16[256,384]{1,0:T(8,128)(2,1)S(1)} %pad_maximum_fusion.2), channel_id=12, replica_groups={{0,2},{1,3},{4,6},{5,7},{8,10},{9,11},{12,14},{13,15},{16,18},{17,19},{..., dimensions={0}, use_global_device_ids=true | all-gather | bytes 589824 | tf_op jit(solution)/shard_map/all_gather | solution.py:19
  80.4 0.3 shard_map.77
  80.8 7.6 %all-gather.11 = bf16[256,768]{1,0:T(8,128)(2,1)S(1)} all-gather(bf16[128,768]{1,0:T(8,128)(2,1)S(1)} %get-tuple-element.29), channel_id=13, replica_groups={{0,1},{2,3},{4,5},{6,7},{8,9},{10,11},{12,13},{14,15},{16,17},{18,19},{..., dimensions={0}, use_global_device_ids=true | all-gather | bytes 589824 | tf_op jit(solution)/shard_map/all_gather | solution.py:19
  88.4 0.9 shard_map.78
  (54 shorter events, 0.6 us)
